TPU v7x, 32 devices: a whole 2x2x4 slice. The times are simulated.
32 devices in a mesh: dp: 16 (over z, x, core), tensor: 2 (over y).
Axes of the slice: x: 2, y: 2, z: 4, core: 2. Of those that a mesh axis runs over, the one named last changes fastest.
Arguments:
- tokens: bfloat16 [2048, 1152], P('dp'), may hold values from -40 to 40
- conditions: bfloat16 [16, 1152], P('dp'), may hold values from -6 to 6
- mod_weight: bfloat16 [1152, 6912], P(None, 'dp'), may hold values from -0.1875 to 0.1875
- mod_bias: bfloat16 [6912], P('dp'), may hold values from -3 to 3
- qkv_weight: bfloat16 [1152, 3, 1152], P('dp', None, 'tensor'), may hold values from -0.1875 to 0.1875
- qv_bias: bfloat16 [2, 1152], P('tensor', 'dp'), may hold values from -3 to 3
- proj_weight: bfloat16 [1152, 1152], P('tensor', 'dp'), may hold values from -0.75 to 0.75
- proj_bias: bfloat16 [1152], P('dp'), may hold values from -3 to 3
- fc1_weight: bfloat16 [1152, 4608], P('dp', 'tensor'), may hold values from -0.1875 to 0.1875
- fc1_bias: bfloat16 [2, 2304], P('tensor', 'dp'), may hold values from -3 to 3
- fc2_weight: bfloat16 [4608, 1152], P('tensor', 'dp'), may hold values from -0.1875 to 0.1875
- fc2_bias: bfloat16 [1152], P('dp'), may hold values from -3 to 3
- cotangent: bfloat16 [2048, 1152], P('dp'), may hold values from -6 to 6
Outputs:
- block_out: bfloat16 [2048, 1152], P('dp')
- tokens_grad: float32 [2048, 1152], P('dp')
- conditions_grad: float32 [16, 1152], P('dp')
- mod_weight_grad: float32 [1152, 6912], P(None, 'dp')
- mod_bias_grad: float32 [6912], P('dp')
- qkv_weight_grad: float32 [1152, 3, 1152], P('dp', None, 'tensor')
- qv_bias_grad: float32 [2, 1152], P('tensor', 'dp')
- proj_weight_grad: float32 [1152, 1152], P('tensor', 'dp')
- proj_bias_grad: float32 [1152], P('dp')
- fc1_weight_grad: float32 [1152, 4608], P('dp', 'tensor')
- fc1_bias_grad: float32 [2, 2304], P('tensor', 'dp')
- fc2_weight_grad: float32 [4608, 1152], P('tensor', 'dp')
- fc2_bias_grad: float32 [1152], P('dp')
All inputs are finite; a program needn't handle non-finite values.
Results may differ from a plain program's by a relative error of at most 0.015.
Values may be sent and summed in bfloat16 or wider, within the bound.
No kernel may reach another device: no remote copies, remote signals or barrier semaphores. Data moves between devices by JAX's collectives and lax.ppermute only.
A program may use at most 192 MiB of HBM per device.

v0:
```python
import jax
import jax.numpy as jnp
from jax import lax
from jax.sharding import PartitionSpec as P

HEAD = 72


epsilon = 1e-06


def layer_norm(values):
    row_mean = jnp.mean(values, axis=-1, keepdims=True)
    centered = values - row_mean
    variance = jnp.mean(centered * centered, axis=-1, keepdims=True)
    return centered * lax.rsqrt(variance + epsilon)


def modulate(values, shift_by, scale_by):
    return layer_norm(values) * (1.0 + scale_by) + shift_by


def tanh_gelu(values):
    return jax.nn.gelu(values, approximate=True)


def product(left, right, einsum_form):
    return jnp.einsum(einsum_form, left, right, preferred_element_type=jnp.float32)


def local(
    tokens,
    conditions,
    mod_weight,
    mod_bias,
    qkv_weight,
    qv_bias,
    proj_weight,
    proj_bias,
    fc1_weight,
    fc1_bias,
    fc2_weight,
    fc2_bias,
    cotangent,
):
    seq_len, width = tokens.shape
    tensor_width = qkv_weight.shape[2]
    heads_here = tensor_width // HEAD
    factor = HEAD ** (-0.5)
    bf16 = jnp.bfloat16
    f32 = jnp.float32
    half_rows = seq_len // lax.axis_size("tensor")
    row_start = lax.axis_index("tensor") * half_rows
    cond_values = conditions.astype(f32)
    silu_conds = jax.nn.silu(cond_values).astype(bf16)
    all_silu = lax.all_gather(silu_conds, "dp", axis=0, tiled=True)
    mod_columns = product(all_silu, mod_weight, "ld,dc->lc") + mod_bias.astype(f32)
    mod_row = lax.all_to_all(mod_columns, "dp", split_axis=0, concat_axis=1, tiled=True)
    modulation = mod_row.reshape(6, width)
    shift_attn = modulation[0]
    scale_attn = modulation[1]
    gate_attn = modulation[2]
    shift_mlp = modulation[3]
    scale_mlp = modulation[4]
    gate_mlp = modulation[5]
    gathered = (
        lax.all_gather(qkv_weight, "dp", axis=0, tiled=True),
        lax.all_gather(qv_bias, "dp", axis=1, tiled=True),
        lax.all_gather(proj_weight, "dp", axis=1, tiled=True),
        lax.all_gather(proj_bias, "dp", axis=0, tiled=True),
        lax.all_gather(fc1_weight, "dp", axis=0, tiled=True),
        lax.all_gather(fc1_bias, "dp", axis=1, tiled=True),
        lax.all_gather(fc2_weight, "dp", axis=1, tiled=True),
        lax.all_gather(fc2_bias, "dp", axis=0, tiled=True),
    )
    (
        qkv_full,
        qv_full,
        proj_full,
        proj_bias_full,
        fc1_full,
        fc1_bias_full,
        fc2_full,
        fc2_bias_full,
    ) = gathered
    qkv_matrix = qkv_full.reshape(width, 3 * tensor_width)
    qv_values = qv_full.astype(f32)[0]
    inputs = tokens.astype(f32)
    inputs_half = lax.dynamic_slice_in_dim(inputs, row_start, half_rows, 0)
    normed_one = modulate(inputs, shift_attn, scale_attn).astype(bf16)
    projected = product(normed_one, qkv_matrix, "sd,df->sf")
    head_shape = (seq_len, heads_here, HEAD)
    queries = (
        (projected[:, :tensor_width] + qv_values[:tensor_width]).astype(bf16).reshape(head_shape)
    )
    keys_heads = projected[:, tensor_width : 2 * tensor_width].astype(bf16).reshape(head_shape)
    values_heads = (
        (projected[:, 2 * tensor_width :] + qv_values[tensor_width:])
        .astype(bf16)
        .reshape(head_shape)
    )
    scores = product(queries, keys_heads, "qhd,khd->hqk") * factor
    row_max = jnp.max(scores, axis=-1, keepdims=True)
    exponent = jnp.exp(scores - row_max)
    row_total = jnp.sum(exponent, axis=-1, keepdims=True)
    probs = exponent / row_total
    log_total = row_max + jnp.log(row_total)
    attended = (
        product(probs.astype(bf16), values_heads, "hqk,khd->qhd")
        .reshape(seq_len, tensor_width)
        .astype(bf16)
    )
    branch_half = lax.psum_scatter(
        product(attended, proj_full, "sf,fd->sd").astype(jnp.bfloat16),
        "tensor",
        scatter_dimension=0,
        tiled=True,
    ).astype(jnp.float32) + proj_bias_full.astype(f32)
    hidden_half = inputs_half + gate_attn * branch_half
    normed_two_half = modulate(hidden_half, shift_mlp, scale_mlp).astype(bf16)
    normed_two = lax.all_gather(normed_two_half, "tensor", axis=0, tiled=True)
    pre_act = product(normed_two, fc1_full, "sd,df->sf") + fc1_bias_full.astype(f32)[0]
    activated = tanh_gelu(pre_act).astype(bf16)
    mlp_half = lax.psum_scatter(
        product(activated, fc2_full, "sf,fd->sd").astype(jnp.bfloat16),
        "tensor",
        scatter_dimension=0,
        tiled=True,
    ).astype(jnp.float32) + fc2_bias_full.astype(f32)
    block_half = hidden_half + gate_mlp * mlp_half
    qkv_again, proj_back, fc1_back, fc2_back = (
        lax.all_gather(qkv_weight, "dp", axis=0, tiled=True),
        lax.all_gather(proj_weight, "dp", axis=1, tiled=True),
        lax.all_gather(fc1_weight, "dp", axis=0, tiled=True),
        lax.all_gather(fc2_weight, "dp", axis=1, tiled=True),
    )
    qkv_back = qkv_again.reshape(width, 3 * tensor_width)
    grad_out = cotangent.astype(f32)
    grad_out_half = lax.dynamic_slice_in_dim(grad_out, row_start, half_rows, 0)
    grad_gate_mlp = jnp.sum(grad_out_half * mlp_half, axis=0)
    grad_branch_mlp = gate_mlp * grad_out
    fc2_bias_grad = jnp.sum(grad_branch_mlp, axis=0)
    grad_branch_low = grad_branch_mlp.astype(bf16)
    fc2_weight_grad = product(activated, grad_branch_low, "sf,sd->fd")
    grad_activated = product(grad_branch_low, fc2_back, "sd,fd->sf")
    gelu_value, gelu_pull = jax.vjp(tanh_gelu, pre_act)
    grad_pre = gelu_pull(grad_activated)[0]
    fc1_bias_grad = jnp.sum(grad_pre, axis=0)[None, :]
    grad_pre_low = grad_pre.astype(bf16)
    fc1_weight_grad = product(normed_two, grad_pre_low, "sd,sf->df")
    grad_normed_two_half = lax.psum_scatter(
        product(grad_pre_low, fc1_back, "sf,df->sd").astype(jnp.bfloat16),
        "tensor",
        scatter_dimension=0,
        tiled=True,
    ).astype(jnp.float32)
    norm_value, norm_pull = jax.vjp(modulate, hidden_half, shift_mlp, scale_mlp)
    grad_hidden_norm, grad_shift_mlp, grad_scale_mlp = norm_pull(grad_normed_two_half)
    grad_hidden_half = grad_out_half + grad_hidden_norm
    grad_gate_attn = jnp.sum(grad_hidden_half * branch_half, axis=0)
    grad_branch_half = gate_attn * grad_hidden_half
    proj_bias_part = jnp.sum(grad_branch_half, axis=0)
    grad_attn_low = lax.all_gather(grad_branch_half.astype(bf16), "tensor", axis=0, tiled=True)
    proj_weight_grad = product(attended, grad_attn_low, "sf,sd->fd")
    grad_attended = product(grad_attn_low, proj_back, "sd,fd->sf").astype(bf16).reshape(head_shape)
    scores_again = product(queries, keys_heads, "qhd,khd->hqk") * factor
    probs_again = jnp.exp(scores_again - log_total)
    grad_values = product(probs_again.astype(bf16), grad_attended, "hqk,qhd->khd")
    grad_probs = product(grad_attended, values_heads, "qhd,khd->hqk")
    grad_scores = (
        probs_again * (grad_probs - jnp.sum(probs_again * grad_probs, axis=-1, keepdims=True))
    ).astype(bf16)
    grad_queries = product(grad_scores, keys_heads, "hqk,khd->qhd") * factor
    grad_keys = product(grad_scores, queries, "hqk,qhd->khd") * factor
    grad_queries = grad_queries.reshape(seq_len, tensor_width)
    grad_keys = grad_keys.reshape(seq_len, tensor_width)
    grad_values = grad_values.reshape(seq_len, tensor_width)
    qv_bias_grad = jnp.concatenate([jnp.sum(grad_queries, axis=0), jnp.sum(grad_values, axis=0)])[
        None, :
    ]
    grad_qkv_low = jnp.concatenate([grad_queries, grad_keys, grad_values], axis=1).astype(bf16)
    qkv_weight_grad = product(normed_one, grad_qkv_low, "sd,sf->df").reshape(width, 3, tensor_width)
    grad_normed_one_half = lax.psum_scatter(
        product(grad_qkv_low, qkv_back, "sf,df->sd").astype(jnp.bfloat16),
        "tensor",
        scatter_dimension=0,
        tiled=True,
    ).astype(jnp.float32)
    first_value, first_pull = jax.vjp(modulate, inputs_half, shift_attn, scale_attn)
    grad_inputs_norm, grad_shift_attn, grad_scale_attn = first_pull(grad_normed_one_half)
    tokens_grad_half = grad_hidden_half + grad_inputs_norm
    grad_mod_part = jnp.stack(
        [
            grad_shift_attn,
            grad_scale_attn,
            grad_gate_attn,
            grad_shift_mlp,
            grad_scale_mlp,
            grad_gate_mlp,
        ]
    ).reshape(1, 6 * width)
    block_rows, tokens_grad, grad_mod_parts, proj_bias_parts = (
        lax.all_gather(block_half.astype(jnp.bfloat16), "tensor", axis=0, tiled=True).astype(
            block_half.dtype
        ),
        lax.all_gather(tokens_grad_half.astype(jnp.bfloat16), "tensor", axis=0, tiled=True).astype(
            tokens_grad_half.dtype
        ),
        lax.all_gather(grad_mod_part.astype(jnp.bfloat16), "tensor", axis=0, tiled=True).astype(
            grad_mod_part.dtype
        ),
        lax.all_gather(
            proj_bias_part[None, :].astype(jnp.bfloat16), "tensor", axis=0, tiled=True
        ).astype(jnp.float32),
    )
    block_out = block_rows.astype(bf16)
    proj_bias_grad = jnp.sum(proj_bias_parts, axis=0)
    grad_mod = jnp.sum(grad_mod_parts, axis=0, keepdims=True).astype(bf16)
    grad_mod_columns = lax.all_to_all(grad_mod, "dp", split_axis=1, concat_axis=0, tiled=True)
    mod_bias_grad = jnp.sum(grad_mod_columns.astype(f32), axis=0)
    mod_weight_grad = product(all_silu, grad_mod_columns, "ld,lc->dc")
    grad_silu = lax.psum_scatter(
        product(grad_mod_columns, mod_weight, "lc,dc->ld"), "dp", scatter_dimension=0, tiled=True
    )
    silu_value, silu_pull = jax.vjp(jax.nn.silu, cond_values)
    conditions_grad = silu_pull(grad_silu)[0]
    reduced = (
        lax.psum_scatter(qkv_weight_grad, "dp", scatter_dimension=0, tiled=True),
        lax.psum_scatter(qv_bias_grad, "dp", scatter_dimension=1, tiled=True),
        lax.psum_scatter(proj_weight_grad, "dp", scatter_dimension=1, tiled=True),
        lax.psum_scatter(proj_bias_grad, "dp", scatter_dimension=0, tiled=True),
        lax.psum_scatter(fc1_weight_grad, "dp", scatter_dimension=0, tiled=True),
        lax.psum_scatter(fc1_bias_grad, "dp", scatter_dimension=1, tiled=True),
        lax.psum_scatter(fc2_weight_grad, "dp", scatter_dimension=1, tiled=True),
        lax.psum_scatter(fc2_bias_grad, "dp", scatter_dimension=0, tiled=True),
    )
    return (
        block_out,
        tokens_grad,
        conditions_grad,
        mod_weight_grad,
        mod_bias_grad,
        reduced[0],
        reduced[1],
        reduced[2],
        reduced[3],
        reduced[4],
        reduced[5],
        reduced[6],
        reduced[7],
    )


def solution(mesh):
    return jax.shard_map(
        local,
        mesh=mesh,
        in_specs=(
            P("dp", None),
            P("dp", None),
            P(None, "dp"),
            P("dp"),
            P("dp", None, "tensor"),
            P("tensor", "dp"),
            P("tensor", "dp"),
            P("dp"),
            P("dp", "tensor"),
            P("tensor", "dp"),
            P("tensor", "dp"),
            P("dp"),
            P("dp", None),
        ),
        out_specs=(
            P("dp", None),
            P("dp", None),
            P("dp", None),
            P(None, "dp"),
            P("dp"),
            P("dp", None, "tensor"),
            P("tensor", "dp"),
            P("tensor", "dp"),
            P("dp"),
            P("dp", "tensor"),
            P("tensor", "dp"),
            P("tensor", "dp"),
            P("dp"),
        ),
        check_vma=False,
    )
```

profile of v0, /device:TPU:0, one launch (start us, length us, event | category | flops | bytes accessed | tf_op | source)
XLA Modules:
  0.0 910.8 jit_solution(15523124739500727486)
XLA Ops:
  10.7 23.5 %all-gather.1 = bf16[16,1,1152]{2,1,0:T(2,128)(2,1)S(1)} all-gather(bf16[1,1,1152]{2,1,0:T(2,128)(2,1)S(1)} %get-tuple-element.39), channel_id=1, replica_groups=mesh['dp'=16,'tensor'=2] {'dp'}, dimensions={0}, use_global_device_ids=true | all-gather | bytes 39168 | tf_op jit(solution)/shard_map/all_gather | solution.py:56
  35.9 3.5 all-to-all-start
  42.4 62.4 %all-reduce.10 = (bf16[1152]{0:T(1024)(128)(2,1)S(1)}, bf16[1152]{0:T(1024)(128)(2,1)S(1)}, bf16[2304]{0:T(1024)(128)(2,1)S(1)}, bf16[1152]{0:T(1024)(128)(2,1)S(1)}) all-reduce(bf16[1152]{0:T(1024)(128)(2,1)S(1)} %dynamic-update-slice, bf16[1152]{0:T(1024)(128)(2,1)S(1)} %dynamic-update-slice.1, ...), channel_id=1, replica_groups=mesh['dp'=16,'tensor'=2] {'dp'}, use_global_device_ids=true, to_apply=%add | all-reduce | flops 5760 | bytes 23040
  105.6 6.6 copy.45
  123.1 6.0 reduce-scatter.15.cloned.1.call-done
  131.6 6.3 all_gather.54
  137.9 49.7 %all-gather.13.cloned.1.call-done = bf16[1152,2304]{1,0:T(8,128)(2,1)} async-done(((bf16[72,2304]{1,0:T(8,128)(2,1)}), bf16[1152,2304]{1,0:T(8,128)(2,1)}) %all-gather.13.cloned.1.call-update) | async-done | bytes 5308432 | tf_op jit(solution)/shard_map/all_gather | solution.py:71
  187.5 4.6 convolution_add_fusion
  192.1 52.4 %all-gather.15.cloned.1.call-done = bf16[2304,1152]{0,1:T(8,128)(2,1)} async-done(((bf16[2304,72]{0,1:T(8,128)(2,1)}), bf16[2304,1152]{0,1:T(8,128)(2,1)}) %all-gather.15.cloned.1.call-update) | async-done | bytes 5308432 | tf_op jit(solution)/shard_map/all_gather | solution.py:73
  244.5 5.2 fusion.55
  253.8 5.3 convolution_convert_fusion.2
  259.2 4.6 reduce-scatter.19.cloned.1.call-done
  266.6 12.0 %reduce-scatter.17.cloned.1.call-done = bf16[64,1152]{1,0:T(8,128)(2,1)} async-done(((bf16[128,1152]{1,0:T(8,128)(2,1)}), bf16[64,1152]{1,0:T(8,128)(2,1)}) %reduce-scatter.17.cloned.1.call-update) | async-done | bytes 147472 | tf_op jit(solution)/shard_map/reduce_scatter | solution.py:124
  282.0 6.4 all_gather.60
  293.1 12.0 %reduce-scatter.21.cloned.1.call-done = bf16[64,1152]{1,0:T(8,128)(2,1)} async-done(((bf16[128,1152]{1,0:T(8,128)(2,1)}), bf16[64,1152]{1,0:T(8,128)(2,1)}) %reduce-scatter.21.cloned.1.call-update) | async-done | bytes 147472 | tf_op jit(solution)/shard_map/reduce_scatter | solution.py:183
  309.2 4.5 all-gather.2
  315.9 5.6 all-to-all-start.1
  323.1 4.9 all-to-all-done.1
  332.2 4.4 fusion.28
  336.6 9.5 %copy.51 = f32[1152,3,576]{2,0,1:T(8,128)} copy(f32[1152,3,576]{0,2,1:T(8,128)} %bitcast.72) | data formatting | bytes 15925248 | tf_op jit(solution)/shard_map/reshape | solution.py:182
  347.4 5.5 fusion.26
  354.0 5.6 fusion.21
  360.5 23.9 %reduce-scatter.29.cloned.1.call-done = f32[144,1]{1,0:T(8,128)} async-done(((f32[2304,1]{1,0:T(8,128)}), f32[144,1]{1,0:T(8,128)}) %reduce-scatter.29.cloned.1.call-update) | async-done | bytes 592
  386.2 4.3 all-gather.3
  390.6 57.7 %all-reduce.9 = (f32[1,1152]{1,0:T(1,128)S(1)}, f32[1152]{0:T(1024)S(1)}, f32[1152]{0:T(1024)S(1)}) all-reduce(f32[1,1152]{1,0:T(1,128)S(1)} %broadcast_in_dim.16, f32[1152]{0:T(1024)S(1)} %convert_reduce_fusion.2, f32[1152]{0:T(1024)S(1)} %multiply_reduce_fusion.1), channel_id=9, replica_groups=mesh['dp'=16,'tensor'=2] {'dp'}, use_global_device_ids=true, to_apply=%region_29.30.clone | all-reduce | flops 3456 | bytes 27648
  449.5 7.4 all_gather.59
  457.6 5.8 all_gather.61
  466.7 5.4 all-reduce.13.cloned.1.call-done
  474.1 69.1 %reduce-scatter.31.cloned.1.call-done = f32[576,72]{0,1:T(8,128)} async-done(((f32[576,1152]{0,1:T(8,128)}), f32[576,72]{0,1:T(8,128)}) %reduce-scatter.31.cloned.1.call-update) | async-done | bytes 165904
  543.2 111.0 %reduce-scatter.23.cloned.1.call-done = f32[72,3,576]{2,0,1:T(8,128)} async-done(((f32[1152,3,576]{2,0,1:T(8,128)}), f32[72,3,576]{2,0,1:T(8,128)}) %reduce-scatter.23.cloned.1.call-update) | async-done | bytes 497680 | tf_op jit(solution)/shard_map/reduce_scatter | solution.py:228
  654.3 124.8 %reduce-scatter.27.cloned.1.call-done = f32[2304,72]{0,1:T(8,128)} async-done(((f32[2304,1152]{0,1:T(8,128)}), f32[2304,72]{0,1:T(8,128)}) %reduce-scatter.27.cloned.1.call-update) | async-done | bytes 663568 | tf_op jit(solution)/shard_map/reduce_scatter | solution.py:234
  779.1 124.5 %reduce-scatter.25.cloned.1.call-done = f32[72,2304]{1,0:T(8,128)} async-done(((f32[1152,2304]{1,0:T(8,128)}), f32[72,2304]{1,0:T(8,128)}) %reduce-scatter.25.cloned.1.call-update) | async-done | bytes 663568 | tf_op jit(solution)/shard_map/reduce_scatter | solution.py:232
  (278 shorter events, 59.4 us)
Async XLA Ops:
  7.2 34.1 %copy-start.65 = (bf16[1,144]{1,0:T(2,128)(2,1)S(1)}, bf16[1,144]{1,0:T(2,128)(2,1)}, u32[]{:S(2)}) copy-start(bf16[1,144]{1,0:T(2,128)(2,1)} %param.22) | copy-start | bytes 868
  7.2 34.2 %copy-start.70 = (bf16[72]{0:T(256)(128)(2,1)S(1)}, bf16[72]{0:T(256)(128)(2,1)}, u32[]{:S(2)}) copy-start(bf16[72]{0:T(256)(128)(2,1)} %param.20) | copy-start | bytes 436
  7.2 34.4 %copy-start.71 = (bf16[1,72]{1,0:T(2,128)(2,1)S(1)}, bf16[1,72]{1,0:T(2,128)(2,1)}, u32[]{:S(2)}) copy-start(bf16[1,72]{1,0:T(2,128)(2,1)} %param.18) | copy-start | bytes 436
  7.2 34.7 %copy-start.72 = (bf16[72]{0:T(256)(128)(2,1)S(1)}, bf16[72]{0:T(256)(128)(2,1)}, u32[]{:S(2)}) copy-start(bf16[72]{0:T(256)(128)(2,1)} %param.24) | copy-start | bytes 436
  7.2 97.6 %copy-start.3 = (bf16[128,1152]{1,0:T(8,128)(2,1)S(1)}, bf16[128,1152]{1,0:T(8,128)(2,1)}, u32[]{:S(2)}) copy-start(bf16[128,1152]{1,0:T(8,128)(2,1)} %param.13) | copy-start | bytes 884740
  7.3 98.4 %all-gather.9.cloned.1.call-start = ((), (), s32[]{:S(2)}) async-start(), calls=%async_computation.11 | async-start | bytes 4700160 | tf_op jit(solution)/shard_map/all_gather | solution.py:67
  8.0 108.9 %all-gather.11.cloned.1.call-start = ((), (), s32[]{:S(2)}) async-start(), calls=%async_computation.12 | async-start | bytes 1566720 | tf_op jit(solution)/shard_map/all_gather | solution.py:69
  35.9 69.4 %all-to-all-start = ((f32[16,1,432]{2,1,0:T(1,128)}), f32[16,1,432]{2,1,0:T(1,128)S(1)}, u32[]{:S(2)}, u32[]{:S(2)}) async-start(f32[16,1,432]{2,1,0:T(1,128)} %copy.44), calls=%async_computation | async-start | bytes 65536 | tf_op jit(solution)/shard_map/all_to_all | solution.py:58
  39.4 89.7 %reduce-scatter.15.cloned.1.call-start = ((), (), s32[]{:S(2)}) async-start(), calls=%async_computation.13 | async-start | bytes 442368 | tf_op jit(solution)/shard_map/reduce_scatter | solution.py:113
  105.6 173.1 %copy-start.33 = (f32[1152]{0:T(1024)}, f32[1152]{0:T(1024)S(1)}, u32[]{:S(2)}) copy-start(f32[1152]{0:T(1024)S(1)} %get-tuple-element.21) | copy-start | bytes 13828
  105.6 201.7 %copy-start.31 = (f32[1152]{0:T(1024)}, f32[1152]{0:T(1024)S(1)}, u32[]{:S(2)}) copy-start(f32[1152]{0:T(1024)S(1)} %get-tuple-element.25) | copy-start | bytes 13828
  119.7 67.9 %all-gather.13.cloned.1.call-start = ((), (), s32[]{:S(2)}) async-start(), calls=%async_computation.14 | async-start | bytes 5640192 | tf_op jit(solution)/shard_map/all_gather | solution.py:71
  120.2 124.3 %all-gather.15.cloned.1.call-start = ((), (), s32[]{:S(2)}) async-start(), calls=%async_computation.15 | async-start | bytes 5640192 | tf_op jit(solution)/shard_map/all_gather | solution.py:73
  120.8 143.0 %reduce-scatter.19.cloned.1.call-start = ((), (), s32[]{:S(2)}) async-start(), calls=%async_computation.17 | async-start | bytes 442368 | tf_op jit(solution)/shard_map/reduce_scatter | solution.py:151
  187.5 63.0 %slice-start = ((s8[5308416]{0:T(1024)(128)(4,1)}), s8[1114112]{0:T(1024)(128)(4,1)S(1)}, s32[]{:S(2)}) async-start(s8[5308416]{0:T(1024)(128)(4,1)} %bitcast.75), calls=%async_computation.25 | async-start | bytes 2228224
  253.0 25.6 %reduce-scatter.17.cloned.1.call-start = ((), (), s32[]{:S(2)}) async-start(), calls=%async_computation.16 | async-start | bytes 442368 | tf_op jit(solution)/shard_map/reduce_scatter | solution.py:124
  259.1 46.0 %reduce-scatter.21.cloned.1.call-start = ((), (), s32[]{:S(2)}) async-start(), calls=%async_computation.18 | async-start | bytes 442368 | tf_op jit(solution)/shard_map/reduce_scatter | solution.py:183
  315.9 12.1 %all-to-all-start.1 = ((bf16[16,2,216]{2,1,0:T(2,128)(2,1)}), bf16[16,2,216]{2,1,0:T(2,128)(2,1)S(1)}, u32[]{:S(2)}, u32[]{:S(2)}) async-start(bf16[16,2,216]{2,1,0:T(2,128)(2,1)} %reshape.279), calls=%async_computation.5 | async-start | bytes 32768 | tf_op jit(solution)/shard_map/all_to_all | solution.py:219
  321.5 62.9 %reduce-scatter.29.cloned.1.call-start = ((), (), s32[]{:S(2)}) async-start(), calls=%async_computation.22 | async-start | bytes 1253376
  323.0 149.0 %all-reduce.13.cloned.1.call-start = ((), (), s32[]{:S(2)}) async-start(), calls=%async_computation.23 | async-start | bytes 147456
  329.0 214.2 %reduce-scatter.31.cloned.1.call-start = ((), (), s32[]{:S(2)}) async-start(), calls=%async_computation.24 | async-start | bytes 3133440
  331.3 323.0 %reduce-scatter.23.cloned.1.call-start = ((), (), s32[]{:S(2)}) async-start(), calls=%async_computation.19 | async-start | bytes 9400320 | tf_op jit(solution)/shard_map/reduce_scatter | solution.py:228
  346.1 432.9 %reduce-scatter.27.cloned.1.call-start = ((), (), s32[]{:S(2)}) async-start(), calls=%async_computation.21 | async-start | bytes 11280384 | tf_op jit(solution)/shard_map/reduce_scatter | solution.py:234
  352.9 550.7 %reduce-scatter.25.cloned.1.call-start = ((), (), s32[]{:S(2)}) async-start(), calls=%async_computation.20 | async-start | bytes 11280384 | tf_op jit(solution)/shard_map/reduce_scatter | solution.py:232
  359.6 89.9 %copy-start.23 = (bf16[64,1152]{1,0:T(8,128)(2,1)S(1)}, bf16[64,1152]{1,0:T(8,128)(2,1)}, u32[]{:S(2)}) copy-start(bf16[64,1152]{1,0:T(8,128)(2,1)} %get-tuple-element.45) | copy-start | bytes 442372
  359.6 97.8 %copy-start.69 = (f32[64]{0:T(128)S(1)}, f32[64]{0:T(128)}, u32[]{:S(2)}) copy-start(f32[64]{0:T(128)} %get-tuple-element.14) | copy-start | bytes 772
  359.6 97.8 %copy-start.9 = (f32[64,1152]{1,0:T(8,128)S(1)}, f32[64,1152]{1,0:T(8,128)}, u32[]{:S(2)}) copy-start(f32[64,1152]{1,0:T(8,128)} %copy-done.8) | copy-start | bytes 884740
  359.6 97.8 %copy-start.13 = (bf16[64,1152]{1,0:T(8,128)(2,1)S(1)}, bf16[64,1152]{1,0:T(8,128)(2,1)}, u32[]{:S(2)}) copy-start(bf16[64,1152]{1,0:T(8,128)(2,1)} %reduce-scatter.21.cloned.1.call-done) | copy-start | bytes 442372
  359.6 97.8 %copy-start.57 = (f32[64]{0:T(128)S(1)}, f32[64]{0:T(128)}, u32[]{:S(2)}) copy-start(f32[64]{0:T(128)} %copy-done.56) | copy-start | bytes 772
  359.6 97.8 %copy-start.59 = (f32[64]{0:T(128)S(1)}, f32[64]{0:T(128)}, u32[]{:S(2)}) copy-start(f32[64]{0:T(128)} %copy-done.58) | copy-start | bytes 772
  359.6 97.8 %copy-start.61 = (f32[64]{0:T(128)S(1)}, f32[64]{0:T(128)}, u32[]{:S(2)}) copy-start(f32[64]{0:T(128)} %copy-done.60) | copy-start | bytes 772
  464.3 440.0 %copy-start.1 = (bf16[1152,432]{0,1:T(8,128)(2,1)S(1)}, bf16[1152,432]{0,1:T(8,128)(2,1)}, u32[]{:S(2)}) copy-start(bf16[1152,432]{0,1:T(8,128)(2,1)} %param.15) | copy-start | bytes 2985988
  (59 other events, 458.2 us)
Sparse Core Ops, SparseCore 0:
  10.3 55.4 all-gather.8
  68.0 38.0 all-gather.10
  119.8 9.2 reduce-scatter.14
  131.1 56.3 all-gather.12
  189.6 54.9 all-gather.14
  253.1 10.6 reduce-scatter.18
  266.6 12.0 reduce-scatter.16
  293.1 12.0 reduce-scatter.20
  326.0 58.4 reduce-scatter.28
  387.7 84.2 all-reduce.12
  477.1 66.1 reduce-scatter.30
  548.4 105.8 reduce-scatter.22
  658.9 120.1 reduce-scatter.26
  783.5 119.9 reduce-scatter.24
where the time goes:
time: 912 us; the launch traced here: 911 us
  waiting for transfers between devices  603 us (66%)
  blocking collectives  178 us (20%)
  matrix products  49 us (5%)
  local copies, waits for them, and re-layouts  32.1 us (4%)
  other arithmetic  21.7 us (2%)
  between operations  16.9 us (2%)
  starting transfers between devices  9.69 us (1%)
    reduce_scatter x1, waiting for transfers between devices, local(): lax.psum_scatter(fc2_weight_grad, 'dp', scatter_dimension=1, tiled=True)  125 us
    reduce_scatter x1, waiting for transfers between devices, local(): lax.psum_scatter(fc1_weight_grad, 'dp', scatter_dimension=0, tiled=True)  125 us
    unnamed x2, blocking collectives  120 us
    reduce_scatter x1, waiting for transfers between devices, local(): lax.psum_scatter(qkv_weight_grad, 'dp', scatter_dimension=0, tiled=True)  111 us
    unnamed x17, waiting for transfers between devices  101 us
    all_gather x1, waiting for transfers between devices, local(): lax.all_gather(fc2_weight, 'dp', axis=1, tiled=True)  52.4 us
    all_gather x1, waiting for transfers between devices, local(): lax.all_gather(fc1_weight, 'dp', axis=0, tiled=True)  49.7 us
    dot_general x21, matrix products, product(): jnp.einsum(einsum_form, left, right, preferred_element_type=jnp.float32)  49 us
  transfers between devices with their start and end apart: 16, of which 13 were waited for; matrix products, arithmetic and copies ran while one was open for 8% of the time, Pallas kernels for 0%

commit v1 on v0

v1 whole, which is shorter than its diff:
```python
import jax
import jax.numpy as jnp
from jax import lax
from jax.sharding import Mesh, PartitionSpec as P

HEAD = 72
EPSILON = 1e-06
GROUP = 4

bf16 = jnp.bfloat16
f32 = jnp.float32


def product(left, right, form):
    return jnp.einsum(form, left, right, preferred_element_type=f32)


def exchange(value, axis, mask=1):
    size = lax.axis_size(axis)
    return lax.ppermute(value, axis, [(i, i ^ mask) for i in range(size)])


def reorder(value, position):
    count = value.shape[0]
    bit = 1
    while bit < count:
        parts = value.reshape((count // (2 * bit), 2, bit) + value.shape[1:])
        flip = (position // bit) % 2 == 1
        first = jnp.where(flip, parts[:, 1], parts[:, 0])
        second = jnp.where(flip, parts[:, 0], parts[:, 1])
        value = jnp.stack([first, second], axis=1).reshape(value.shape)
        bit *= 2
    return value


def gather_dp(value):
    for axis in ("core", "xx"):
        value = jnp.concatenate([value, exchange(value, axis)], axis=0)
    mask = 1
    while mask < lax.axis_size("zz"):
        value = jnp.concatenate([value, exchange(value, "zz", mask)], axis=0)
        mask *= 2
    return value


def gather_four(value):
    value = jnp.concatenate([value, exchange(value, "xx")], axis=0)
    return jnp.concatenate([value, exchange(value, "core")], axis=0)


def gather_eight(value):
    over_y = exchange(value, "tensor")
    over_x = exchange(value, "xx")
    over_xy = exchange(value, ("xx", "tensor"), 3)
    near = jnp.concatenate([value, over_y, over_x, over_xy], axis=0)
    return jnp.concatenate([near, exchange(near, "core")], axis=0)


def scatter_eight(partial):
    half = partial.shape[0] // 2
    rows = half // 4
    near = partial[:half] + exchange(partial[half:].astype(bf16), "core").astype(f32)
    sent = near.astype(bf16)
    over_y = exchange(sent[rows : 2 * rows], "tensor")
    over_x = exchange(sent[2 * rows : 3 * rows], "xx")
    over_xy = exchange(sent[3 * rows :], ("xx", "tensor"), 3)
    return (near[:rows] + over_y.astype(f32)) + (over_x.astype(f32) + over_xy.astype(f32))


def swap_four(chunks, place):
    parts = [lax.dynamic_index_in_dim(chunks, place ^ d, 0, keepdims=False) for d in range(4)]
    got = [
        parts[0],
        exchange(parts[1], "core"),
        exchange(parts[2], "xx"),
        exchange(parts[3], ("xx", "core"), 3),
    ]
    return reorder(jnp.stack(got), place)


def norm(values):
    mean = jnp.mean(values, axis=-1, keepdims=True)
    centered = values - mean
    variance = jnp.mean(centered * centered, axis=-1, keepdims=True)
    inverse = lax.rsqrt(variance + EPSILON)
    return centered * inverse, inverse


def norm_back(grad, normed, inverse, scale):
    scaled = grad * (1.0 + scale)
    mean_scaled = jnp.mean(scaled, axis=-1, keepdims=True)
    mean_product = jnp.mean(scaled * normed, axis=-1, keepdims=True)
    return inverse * (scaled - mean_scaled - normed * mean_product)


def tanh_gelu(values):
    return jax.nn.gelu(values, approximate=True)


def local(
    tokens,
    conditions,
    mod_weight,
    mod_bias,
    qkv_weight,
    qv_bias,
    proj_weight,
    proj_bias,
    fc1_weight,
    fc1_bias,
    fc2_weight,
    fc2_bias,
    cotangent,
):
    seq, width = tokens.shape
    rows = seq // 2
    d_rows = qkv_weight.shape[0]
    t_width = qkv_weight.shape[2]
    hidden = fc1_weight.shape[1]
    feats = t_width // GROUP
    units = hidden // GROUP
    heads = feats // HEAD
    n_dp = width // d_rows
    factor = HEAD ** (-0.5)
    t = lax.axis_index("tensor")
    place = lax.axis_index("xx") * 2 + lax.axis_index("core")
    dp = lax.axis_index("zz") * GROUP + place

    qkv_chunks = qkv_weight.reshape(d_rows, 3, GROUP, feats).transpose(2, 0, 1, 3)
    qkv_chunks = qkv_chunks.reshape(GROUP, d_rows, 3 * feats)
    proj_chunks = proj_weight.T.reshape(d_rows, GROUP, feats).transpose(1, 0, 2)
    fc1_chunks = fc1_weight.reshape(d_rows, GROUP, units).transpose(1, 0, 2)
    fc2_chunks = fc2_weight.T.reshape(d_rows, GROUP, units).transpose(1, 0, 2)
    attn_part = swap_four(jnp.concatenate([qkv_chunks, proj_chunks], axis=2), place)
    mlp_part = swap_four(jnp.concatenate([fc1_chunks, fc2_chunks], axis=2), place)
    attn_part = attn_part.reshape(GROUP * d_rows, 4 * feats)
    mlp_part = mlp_part.reshape(GROUP * d_rows, 2 * units)
    attn_full = lax.all_gather(attn_part, "zz", axis=0, tiled=True)
    mlp_full = lax.all_gather(mlp_part, "zz", axis=0, tiled=True)
    qkv_full = attn_full[:, : 3 * feats]
    proj_full = attn_full[:, 3 * feats :]
    fc1_full = mlp_full[:, :units]
    fc2_full = mlp_full[:, units:]

    cond_values = conditions.astype(f32)
    silu_conds = jax.nn.silu(cond_values).astype(bf16)
    small = jnp.concatenate(
        [silu_conds, qv_bias, proj_bias[None], fc1_bias, fc2_bias[None]], axis=1
    )
    small = reorder(gather_dp(small), dp)
    n_qv, n_b, n_f = qv_bias.shape[1], proj_bias.shape[0], fc1_bias.shape[1]
    cuts = [width, width + n_qv, width + n_qv + n_b, width + n_qv + n_b + n_f]
    all_silu = small[:, : cuts[0]]
    qv_full = small[:, cuts[0] : cuts[1]].reshape(2, GROUP, feats).astype(f32)
    proj_bias_full = small[:, cuts[1] : cuts[2]].reshape(width).astype(f32)
    fc1_bias_full = small[:, cuts[2] : cuts[3]].reshape(GROUP, units).astype(f32)
    fc2_bias_full = small[:, cuts[3] :].reshape(width).astype(f32)
    qv_here = lax.dynamic_index_in_dim(qv_full, place, 1, keepdims=False)
    fc1_bias_here = lax.dynamic_index_in_dim(fc1_bias_full, place, 0, keepdims=False)
    mod_columns = product(all_silu, mod_weight, "ld,dc->lc") + mod_bias.astype(f32)
    mod_row = lax.all_to_all(
        mod_columns, ("zz", "xx", "core"), split_axis=0, concat_axis=1, tiled=True
    )
    mod_rows = gather_four(mod_row).reshape(GROUP, 6, width)
    shift_attn, scale_attn, gate_attn, shift_mlp, scale_mlp, gate_mlp = [
        mod_rows[:, i] for i in range(6)
    ]

    def own_order(value):
        first = lax.dynamic_slice_in_dim(value, t * rows, rows, 0)
        second = lax.dynamic_slice_in_dim(value, (1 - t) * rows, rows, 0)
        return jnp.concatenate([first, second], axis=0)

    def true_order(own, other):
        return jnp.where(
            t == 0,
            jnp.concatenate([own, other], axis=0),
            jnp.concatenate([other, own], axis=0),
        )

    tokens_own = own_order(tokens)
    cot_own = own_order(cotangent)
    tokens_all = gather_four(tokens_own).astype(f32).reshape(GROUP, seq, width)
    cot_all = gather_four(cot_own).astype(f32).reshape(GROUP, seq, width)
    inputs_half = tokens_own[:rows].astype(f32)
    grad_out_half = cot_own[:rows].astype(f32)

    total = GROUP * seq
    normed_one = norm(tokens_all)[0] * (1.0 + scale_attn[:, None]) + shift_attn[:, None]
    normed_one = normed_one.astype(bf16).reshape(total, width)
    projected = product(normed_one, qkv_full, "sd,df->sf")
    head_shape = (GROUP, seq, heads, HEAD)
    queries = (projected[:, :feats] + qv_here[0]).astype(bf16).reshape(head_shape)
    keys = projected[:, feats : 2 * feats].astype(bf16).reshape(head_shape)
    values = (projected[:, 2 * feats :] + qv_here[1]).astype(bf16).reshape(head_shape)
    scores = product(queries, keys, "lqhd,lkhd->lhqk") * factor
    exponent = jnp.exp(scores - jnp.max(scores, axis=-1, keepdims=True))
    probs = exponent / jnp.sum(exponent, axis=-1, keepdims=True)
    probs_low = probs.astype(bf16)
    attended = product(probs_low, values, "lhqk,lkhd->lqhd").astype(bf16).reshape(total, feats)
    branch_half = scatter_eight(product(attended, proj_full, "sf,df->sd")) + proj_bias_full
    hidden_half = inputs_half + gate_attn[0] * branch_half

    norm_two, inverse_two = norm(hidden_half)
    normed_two_half = (norm_two * (1.0 + scale_mlp[0]) + shift_mlp[0]).astype(bf16)
    normed_two = gather_eight(normed_two_half)
    pre_act = product(normed_two, fc1_full, "sd,df->sf") + fc1_bias_here
    activated = tanh_gelu(pre_act).astype(bf16)
    mlp_half = scatter_eight(product(activated, fc2_full, "sf,df->sd")) + fc2_bias_full
    block_half = (hidden_half + gate_mlp[0] * mlp_half).astype(bf16)

    def token_sum(value):
        parts = jnp.sum(value.reshape(2 * GROUP, rows, width), axis=1)
        pairs = parts[0::2] + parts[1::2]
        return (pairs[0] + pairs[1]) + (pairs[2] + pairs[3])

    grad_branch_mlp = (gate_mlp[:, None] * cot_all).reshape(total, width)
    fc2_bias_part = token_sum(grad_branch_mlp)
    grad_branch_low = grad_branch_mlp.astype(bf16)
    fc2_grad = product(grad_branch_low, activated, "sd,sf->df").astype(bf16)
    grad_activated = product(grad_branch_low, fc2_full, "sd,df->sf")
    grad_pre = jax.vjp(tanh_gelu, pre_act)[1](grad_activated)[0]
    fc1_bias_part = jnp.sum(grad_pre, axis=0)
    grad_pre_low = grad_pre.astype(bf16)
    fc1_grad = product(normed_two, grad_pre_low, "sd,sf->df").astype(bf16)
    mlp_grad = lax.psum_scatter(
        jnp.concatenate([fc1_grad, fc2_grad], axis=1), "zz", scatter_dimension=0, tiled=True
    )
    grad_normed_two = scatter_eight(product(grad_pre_low, fc1_full, "sf,df->sd"))
    grad_hidden_half = grad_out_half + norm_back(
        grad_normed_two, norm_two, inverse_two, scale_mlp[0]
    )
    grad_branch_half = (gate_attn[0] * grad_hidden_half).astype(bf16)

    grad_branch_all = gather_eight(grad_branch_half)
    proj_bias_part = token_sum(grad_branch_all.astype(f32))
    proj_grad = product(grad_branch_all, attended, "sd,sf->df").astype(bf16)
    grad_attended = product(grad_branch_all, proj_full, "sd,df->sf").astype(bf16)
    grad_attended = grad_attended.reshape(head_shape)
    grad_values = product(probs_low, grad_attended, "lhqk,lqhd->lkhd")
    grad_probs = product(grad_attended, values, "lqhd,lkhd->lhqk")
    grad_scores = probs * (grad_probs - jnp.sum(probs * grad_probs, axis=-1, keepdims=True))
    grad_scores = grad_scores.astype(bf16)
    grad_queries = product(grad_scores, keys, "lhqk,lkhd->lqhd") * factor
    grad_keys = product(grad_scores, queries, "lhqk,lqhd->lkhd") * factor
    grad_queries = grad_queries.reshape(total, feats)
    grad_keys = grad_keys.reshape(total, feats)
    grad_values = grad_values.reshape(total, feats)
    grad_qkv_low = jnp.concatenate([grad_queries, grad_keys, grad_values], axis=1).astype(bf16)
    qkv_grad = product(normed_one, grad_qkv_low, "sd,sf->df").astype(bf16)
    attn_grad = lax.psum_scatter(
        jnp.concatenate([qkv_grad, proj_grad], axis=1), "zz", scatter_dimension=0, tiled=True
    )
    grad_normed_one = scatter_eight(product(grad_qkv_low, qkv_full, "sf,df->sd"))
    norm_one, inverse_one = norm(inputs_half)
    tokens_grad_half = grad_hidden_half + norm_back(
        grad_normed_one, norm_one, inverse_one, scale_attn[0]
    )

    block_out = true_order(block_half, exchange(block_half, "tensor"))
    tokens_grad_half = tokens_grad_half.astype(bf16)
    tokens_grad = true_order(tokens_grad_half, exchange(tokens_grad_half, "tensor")).astype(f32)
    grad_mod = jnp.stack(
        [
            jnp.sum(grad_normed_one, axis=0),
            jnp.sum(grad_normed_one * norm_one, axis=0),
            jnp.sum(grad_hidden_half * branch_half, axis=0),
            jnp.sum(grad_normed_two, axis=0),
            jnp.sum(grad_normed_two * norm_two, axis=0),
            jnp.sum(grad_out_half * mlp_half, axis=0),
        ]
    ).reshape(1, 6 * width)
    grad_mod = (grad_mod + exchange(grad_mod, "tensor")).astype(bf16)
    grad_mod_columns = lax.all_to_all(
        grad_mod, ("zz", "xx", "core"), split_axis=1, concat_axis=0, tiled=True
    )
    mod_bias_grad = jnp.sum(grad_mod_columns.astype(f32), axis=0)
    mod_weight_grad = product(all_silu, grad_mod_columns, "ld,lc->dc")
    grad_silu = lax.psum_scatter(
        product(grad_mod_columns, mod_weight, "lc,dc->ld"),
        ("zz", "xx", "core"),
        scatter_dimension=0,
        tiled=True,
    )
    conditions_grad = jax.vjp(jax.nn.silu, cond_values)[1](grad_silu)[0]

    biases = jnp.concatenate(
        [
            jnp.sum(grad_queries, axis=0),
            jnp.sum(grad_values, axis=0),
            fc1_bias_part,
            proj_bias_part,
            fc2_bias_part,
        ]
    )
    biases = lax.psum(biases, "zz")
    own = 2 * feats + units
    group_biases = biases[None, :own]
    for axis in ("core", "xx"):
        group_biases = jnp.concatenate([group_biases, exchange(group_biases, axis)], axis=0)
    group_biases = reorder(group_biases, place)
    qv_all = jnp.concatenate(
        [group_biases[:, :feats].reshape(-1), group_biases[:, feats : 2 * feats].reshape(-1)]
    )
    fc1_all = group_biases[:, 2 * feats :].reshape(-1)
    proj_all = biases[own : own + width]
    fc2_all = biases[own + width :]

    def piece(vector):
        size = vector.shape[0] // n_dp
        return lax.dynamic_slice_in_dim(vector, dp * size, size, 0)

    mlp_grad = swap_four(mlp_grad.reshape(GROUP, d_rows, 2 * units), place).astype(f32)
    attn_grad = swap_four(attn_grad.reshape(GROUP, d_rows, 4 * feats), place).astype(f32)
    fc1_weight_grad = mlp_grad[:, :, :units].transpose(1, 0, 2).reshape(d_rows, hidden)
    fc2_weight_grad = mlp_grad[:, :, units:].transpose(1, 0, 2).reshape(d_rows, hidden).T
    qkv_weight_grad = attn_grad[:, :, : 3 * feats].reshape(GROUP, d_rows, 3, feats)
    qkv_weight_grad = qkv_weight_grad.transpose(1, 2, 0, 3).reshape(d_rows, 3, t_width)
    proj_weight_grad = attn_grad[:, :, 3 * feats :].transpose(1, 0, 2).reshape(d_rows, t_width).T
    return (
        block_out,
        tokens_grad,
        conditions_grad,
        mod_weight_grad,
        mod_bias_grad,
        qkv_weight_grad,
        piece(qv_all)[None],
        proj_weight_grad,
        piece(proj_all),
        fc1_weight_grad,
        piece(fc1_all)[None],
        fc2_weight_grad,
        piece(fc2_all),
    )


def solution(mesh):
    n_dp, n_tensor = mesh.shape["dp"], mesh.shape["tensor"]
    cut = Mesh(
        mesh.devices.reshape(n_dp // GROUP, 2, 2, n_tensor), ("zz", "xx", "core", "tensor")
    )
    dp = ("zz", "xx", "core")
    return jax.shard_map(
        local,
        mesh=cut,
        in_specs=(
            P(dp, None),
            P(dp, None),
            P(None, dp),
            P(dp),
            P(dp, None, "tensor"),
            P("tensor", dp),
            P("tensor", dp),
            P(dp),
            P(dp, "tensor"),
            P("tensor", dp),
            P("tensor", dp),
            P(dp),
            P(dp, None),
        ),
        out_specs=(
            P(dp, None),
            P(dp, None),
            P(dp, None),
            P(None, dp),
            P(dp),
            P(dp, None, "tensor"),
            P("tensor", dp),
            P("tensor", dp),
            P(dp),
            P(dp, "tensor"),
            P("tensor", dp),
            P("tensor", dp),
            P(dp),
        ),
        check_vma=False,
    )
```

time: 912 us -> 454 us (0.50)
  waiting for transfers between devices: 603 us -> 235 us
  blocking collectives: 178 us -> 15.9 us
  starting transfers between devices: 9.69 us -> 53.7 us
  other arithmetic: 21.7 us -> 41.5 us
  local copies, waits for them, and re-layouts: 32.1 us -> 51.2 us
  matrix products: 49 us -> 34.4 us
    reduce_scatter x7 -> x2, waiting for transfers between devices: 395 us -> 76.2 us  [the longest x1 41.3 us: local(): lax.psum_scatter(jnp.concatenate([fc1_grad, fc2_grad], axis=1), 'zz', sca...]
    unnamed x2 -> x0, blocking collectives: 120 us -> none
    ppermute x0 -> x51, waiting for transfers between devices: none -> 69.6 us  [exchange(): return lax.ppermute(value, axis, [(i, i ^ mask) for i in range(size)])]
    unnamed x17 -> x6, waiting for transfers between devices: 101 us -> 34.9 us
    all_gather x7 -> x0, blocking collectives: 58.2 us -> none  [the longest x1 23.5 us: local(): all_silu = lax.all_gather(silu_conds, 'dp', axis=0, tiled=True)]
    all_gather x4 -> x2, waiting for transfers between devices: 102 us -> 48.5 us  [the longest x1 25.3 us: local(): mlp_full = lax.all_gather(mlp_part, 'zz', axis=0, tiled=True)]
    ppermute x0 -> x51, starting transfers between devices: none -> 45.5 us  [exchange(): return lax.ppermute(value, axis, [(i, i ^ mask) for i in range(size)])]
    psum x0 -> x1, blocking collectives: none -> 15.9 us  [local(): biases = lax.psum(biases, 'zz')]
  transfers between devices with their start and end apart: 16 -> 58, of which waited for: 13 -> 37; matrix products, arithmetic and copies ran while one was open for 8% -> 17% of each run, Pallas kernels for 0% -> 0%
where the time goes in v1:
time: 454 us; the launch traced here: 447 us
  waiting for transfers between devices  235 us (52%)
  starting transfers between devices  53.7 us (12%)
  local copies, waits for them, and re-layouts  51.2 us (11%)
  other arithmetic  41.5 us (9%)
  matrix products  34.4 us (8%)
  between operations  16 us (4%)
  blocking collectives  15.9 us (4%)
    ppermute x51, waiting for transfers between devices, exchange(): return lax.ppermute(value, axis, [(i, i ^ mask) for i in range(size)])  69.6 us
    ppermute x51, starting transfers between devices, exchange(): return lax.ppermute(value, axis, [(i, i ^ mask) for i in range(size)])  45.5 us
    reduce_scatter x1, waiting for transfers between devices, local(): lax.psum_scatter(jnp.concatenate([fc1_grad, fc2_grad], axis=1), 'zz', sca...  41.3 us
    unnamed x6, waiting for transfers between devices  34.9 us
    reduce_scatter x1, waiting for transfers between devices, local(): lax.psum_scatter(jnp.concatenate([qkv_grad, proj_grad], axis=1), 'zz', sc...  34.9 us
    dot_general x20, matrix products, product(): return jnp.einsum(form, left, right, preferred_element_type=f32)  33.3 us
    all_gather x1, waiting for transfers between devices, local(): mlp_full = lax.all_gather(mlp_part, 'zz', axis=0, tiled=True)  25.3 us
    all_gather x1, waiting for transfers between devices, local(): attn_full = lax.all_gather(attn_part, 'zz', axis=0, tiled=True)  23.3 us
  transfers between devices with their start and end apart: 58, of which 37 were waited for; matrix products, arithmetic and copies ran while one was open for 17% of the time, Pallas kernels for 0%

profile of v1, /device:TPU:0, one launch (start us, length us, event | category | flops | bytes accessed | tf_op | source)
XLA Modules:
  0.0 447.4 jit_solution(3270463783850013230)
XLA Ops:
  12.4 2.6 collective-permute-start.1
  24.1 2.7 collective-permute-start.3
  26.8 3.6 fusion.43
  33.8 3.5 all-to-all-start
  46.2 2.4 collective-permute-done.6
  57.7 23.3 %all-gather.3.cloned.1.call-done = bf16[1152,576]{1,0:T(8,128)(2,1)} async-done(((bf16[288,576]{1,0:T(8,128)(2,1)}), bf16[1152,576]{1,0:T(8,128)(2,1)}) %all-gather.3.cloned.1.call-update) | async-done | bytes 1327120 | tf_op jit(solution)/shard_map/all_gather | solution.py:138
  111.5 2.5 collective-permute-done.16
  119.1 25.3 %all-gather.5.cloned.1.call-done = bf16[1152,1152]{1,0:T(8,128)(2,1)} async-done(((bf16[288,1152]{1,0:T(8,128)(2,1)}), bf16[1152,1152]{1,0:T(8,128)(2,1)}) %all-gather.5.cloned.1.call-update) | async-done | bytes 2654224 | tf_op jit(solution)/shard_map/all_gather | solution.py:139
  144.4 2.9 convolution_add_fusion
  157.0 2.4 collective-permute-done.23
  159.4 2.6 collective-permute-done.24
  167.4 6.4 %collective-permute-done.27 = bf16[128,1152]{1,0:T(8,128)(2,1)S(1)} collective-permute-done((bf16[128,1152]{1,0:T(8,128)(2,1)S(1)}, bf16[128,1152]{1,0:T(8,128)(2,1)S(1)}, u32[]{:S(2)}, u32[]{:S(2)}) %collective-permute-start.27) | collective-permute-done | bytes 294944 | tf_op jit(solution)/shard_map/ppermute | solution.py:20
  176.8 3.0 fusion.156
  186.9 2.4 collective-permute-done.30
  207.1 2.6 convolution_convert_fusion.5
  211.3 2.7 fusion.141
  228.4 2.5 collective-permute-done.40
  233.6 3.1 convolution_convert_fusion.2
  238.9 4.1 all-to-all-start.1
  244.2 5.3 %all-to-all-done.1 = bf16[16,2,216]{2,1,0:T(2,128)(2,1)} async-done(((bf16[16,2,216]{2,1,0:T(2,128)(2,1)}), bf16[16,2,216]{2,1,0:T(2,128)(2,1)}, u32[]{:S(2)}, u32[]{:S(2)}) %all-to-all-start.1) | async-done | bytes 13856 | tf_op jit(solution)/shard_map/all_to_all | solution.py:274
  252.7 2.4 pad_maximum_fusion.1
  255.0 2.6 copy.209
  261.5 2.5 convolution_convert_fusion.1
  266.9 5.2 %copy.211 = bf16[1152,1152]{1,0:T(8,128)(2,1)} copy(bf16[1152,1152]{0,1:T(8,128)(2,1)} %pad_maximum_fusion) | data formatting | bytes 5308416
  273.1 15.9 %psum.7 = f32[3168]{0:T(1024)S(1)} all-reduce(f32[3168]{0:T(1024)S(1)} %concatenate.138), channel_id=1, replica_groups=mesh['zz'=4,'xx'=2,'core'=2,'tensor'=2] {'zz'}, use_global_device_ids=true, to_apply=%region_27.28 | all-reduce | flops 3168 | bytes 25344 | tf_op jit(solution)/shard_map/psum | solution.py:296
  300.1 34.8 %all-reduce.3.cloned.1.call-done = f32[16,1152]{1,0:T(8,128)} async-done(((f32[16,1152]{1,0:T(8,128)}), f32[16,1152]{1,0:T(8,128)}) %all-reduce.3.cloned.1.call-update) | async-done | bytes 73744
  336.9 34.9 %reduce-scatter.7.cloned.1.call-done = bf16[288,576]{1,0:T(8,128)(2,1)} async-done(((bf16[1152,576]{1,0:T(8,128)(2,1)}), bf16[288,576]{1,0:T(8,128)(2,1)}) %reduce-scatter.7.cloned.1.call-update) | async-done | bytes 331792 | tf_op jit(solution)/shard_map/reduce_scatter | solution.py:251
  375.7 2.8 collective-permute-done.44
  381.7 2.5 reshape.434
  384.2 41.3 %reduce-scatter.9.cloned.1.call-done = bf16[288,1152]{1,0:T(8,128)(2,1)} async-done(((bf16[1152,1152]{1,0:T(8,128)(2,1)}), bf16[288,1152]{1,0:T(8,128)(2,1)}) %reduce-scatter.9.cloned.1.call-update) | async-done | bytes 663568 | tf_op jit(solution)/shard_map/reduce_scatter | solution.py:226
  429.8 4.1 collective-permute-done.49
  433.9 2.6 collective-permute-done.50
  (476 shorter events, 174.0 us)
Async XLA Ops:
  15.7 38.4 %collective-permute-start.4 = (bf16[128,1152]{1,0:T(8,128)(2,1)}, bf16[128,1152]{1,0:T(8,128)(2,1)S(1)}, u32[]{:S(2)}, u32[]{:S(2)}) collective-permute-start(bf16[128,1152]{1,0:T(8,128)(2,1)} %pad_maximum_fusion.15), channel_id=1, source_target_pairs={{0,4},{4,0},{1,5},{5,1},{2,6},{6,2},{3,7},{7,3},{8,12},{12,8},{9,1... | collective-permute-start | bytes 884744 | tf_op jit(solution)/shard_map/ppermute | solution.py:20
  16.7 7.4 %collective-permute-start.2 = (bf16[4,1512]{1,0:T(4,128)(2,1)S(1)}, bf16[4,1512]{1,0:T(4,128)(2,1)S(1)}, u32[]{:S(2)}, u32[]{:S(2)}) collective-permute-start(bf16[4,1512]{1,0:T(4,128)(2,1)S(1)} %pad_maximum_fusion.23), channel_id=1, source_target_pairs={{0,8},{8,0},{16,24},{24,16},{1,9},{9,1},{17,25},{25,17},{2,10},{10... | collective-permute-start | bytes 36296 | tf_op jit(solution)/shard_map/ppermute | solution.py:20
  19.8 17.6 %collective-permute-start.8 = (bf16[72,576]{1,0:T(8,128)(2,1)}, bf16[72,576]{1,0:T(8,128)(2,1)}, u32[]{:S(2)}, u32[]{:S(2)}) collective-permute-start(bf16[72,576]{1,0:T(8,128)(2,1)} %bitcast.11), channel_id=1, source_target_pairs={{0,2},{2,0},{1,3},{3,1},{4,6},{6,4},{5,7},{7,5},{8,10},{10,8},{9,1... | collective-permute-start | bytes 248840 | tf_op jit(solution)/shard_map/ppermute | solution.py:20
  20.5 19.8 %collective-permute-start.9 = (bf16[72,576]{1,0:T(8,128)(2,1)}, bf16[72,576]{1,0:T(8,128)(2,1)}, u32[]{:S(2)}, u32[]{:S(2)}) collective-permute-start(bf16[72,576]{1,0:T(8,128)(2,1)} %bitcast.13), channel_id=1, source_target_pairs={{0,4},{4,0},{1,5},{5,1},{2,6},{6,2},{3,7},{7,3},{8,12},{12,8},{9,1... | collective-permute-start | bytes 248840 | tf_op jit(solution)/shard_map/ppermute | solution.py:20
  22.8 18.7 %collective-permute-start.10 = (bf16[72,576]{1,0:T(8,128)(2,1)}, bf16[72,576]{1,0:T(8,128)(2,1)}, u32[]{:S(2)}, u32[]{:S(2)}) collective-permute-start(bf16[72,576]{1,0:T(8,128)(2,1)} %bitcast.15), channel_id=1, source_target_pairs={{0,6},{2,4},{4,2},{6,0},{1,7},{3,5},{5,3},{7,1},{8,14},{10,12},{12... | collective-permute-start | bytes 248840 | tf_op jit(solution)/shard_map/ppermute | solution.py:20
  24.1 7.1 %collective-permute-start.3 = (bf16[8,1512]{1,0:T(8,128)(2,1)S(1)}, bf16[8,1512]{1,0:T(8,128)(2,1)S(1)}, u32[]{:S(2)}, u32[]{:S(2)}) collective-permute-start(bf16[8,1512]{1,0:T(8,128)(2,1)S(1)} %pad_maximum_fusion.20), channel_id=1, source_target_pairs={{0,16},{8,24},{16,0},{24,8},{1,17},{9,25},{17,1},{25,9},{2,18},{10... | collective-permute-start | bytes 72584 | tf_op jit(solution)/shard_map/ppermute | solution.py:20
  31.2 17.6 %collective-permute-start.19 = (bf16[72,1152]{1,0:T(8,128)(2,1)}, bf16[72,1152]{1,0:T(8,128)(2,1)S(1)}, u32[]{:S(2)}, u32[]{:S(2)}) collective-permute-start(bf16[72,1152]{1,0:T(8,128)(2,1)} %bitcast.195), channel_id=1, source_target_pairs={{0,2},{2,0},{1,3},{3,1},{4,6},{6,4},{5,7},{7,5},{8,10},{10,8},{9,1... | collective-permute-start | bytes 497672 | tf_op jit(solution)/shard_map/ppermute | solution.py:20
  33.8 10.5 %all-to-all-start = ((f32[16,1,432]{2,1,0:T(1,128)}), f32[16,1,432]{2,1,0:T(1,128)S(1)}, u32[]{:S(2)}, u32[]{:S(2)}) async-start(f32[16,1,432]{2,1,0:T(1,128)} %copy.165), calls=%async_computation | async-start | bytes 65536 | tf_op jit(solution)/shard_map/all_to_all | solution.py:161
  37.3 43.7 %all-gather.3.cloned.1.call-start = ((), (), s32[]{:S(2)}) async-start(), calls=%async_computation.4 | async-start | bytes 1843200 | tf_op jit(solution)/shard_map/all_gather | solution.py:138
  37.4 11.6 %collective-permute-start.20 = (bf16[72,1152]{1,0:T(8,128)(2,1)S(1)}, bf16[72,1152]{1,0:T(8,128)(2,1)}, u32[]{:S(2)}, u32[]{:S(2)}) collective-permute-start(bf16[72,1152]{1,0:T(8,128)(2,1)S(1)} %bitcast.222), channel_id=1, source_target_pairs={{0,4},{4,0},{1,5},{5,1},{2,6},{6,2},{3,7},{7,3},{8,12},{12,8},{9,1... | collective-permute-start | bytes 497672 | tf_op jit(solution)/shard_map/ppermute | solution.py:20
  40.3 9.9 %collective-permute-start.21 = (bf16[72,1152]{1,0:T(8,128)(2,1)S(1)}, bf16[72,1152]{1,0:T(8,128)(2,1)}, u32[]{:S(2)}, u32[]{:S(2)}) collective-permute-start(bf16[72,1152]{1,0:T(8,128)(2,1)S(1)} %bitcast.221), channel_id=1, source_target_pairs={{0,6},{2,4},{4,2},{6,0},{1,7},{3,5},{5,3},{7,1},{8,14},{10,12},{12... | collective-permute-start | bytes 497672 | tf_op jit(solution)/shard_map/ppermute | solution.py:20
  44.1 100.3 %all-gather.5.cloned.1.call-start = ((), (), s32[]{:S(2)}) async-start(), calls=%async_computation.5 | async-start | bytes 3317760 | tf_op jit(solution)/shard_map/all_gather | solution.py:139
  94.7 6.7 %collective-permute-start.13 = (bf16[64,1152]{1,0:T(8,128)(2,1)S(1)}, bf16[64,1152]{1,0:T(8,128)(2,1)S(1)}, u32[]{:S(2)}, u32[]{:S(2)}) collective-permute-start(bf16[64,1152]{1,0:T(8,128)(2,1)S(1)} %get-tuple-element.82), channel_id=1, source_target_pairs={{0,4},{4,0},{1,5},{5,1},{2,6},{6,2},{3,7},{7,3},{8,12},{12,8},{9,1... | collective-permute-start | bytes 442376 | tf_op jit(solution)/shard_map/ppermute | solution.py:20
  96.2 7.3 %collective-permute-start.14 = (bf16[64,1152]{1,0:T(8,128)(2,1)S(1)}, bf16[64,1152]{1,0:T(8,128)(2,1)S(1)}, u32[]{:S(2)}, u32[]{:S(2)}) collective-permute-start(bf16[64,1152]{1,0:T(8,128)(2,1)S(1)} %get-tuple-element.81), channel_id=1, source_target_pairs={{0,5},{1,4},{4,1},{5,0},{2,7},{3,6},{6,3},{7,2},{8,13},{9,12},{12,... | collective-permute-start | bytes 442376 | tf_op jit(solution)/shard_map/ppermute | solution.py:20
  107.8 6.2 %collective-permute-start.16 = (bf16[64,1152]{1,0:T(8,128)(2,1)S(1)}, bf16[64,1152]{1,0:T(8,128)(2,1)S(1)}, u32[]{:S(2)}, u32[]{:S(2)}) collective-permute-start(bf16[64,1152]{1,0:T(8,128)(2,1)S(1)} %get-tuple-element.43), channel_id=1, source_target_pairs={{0,4},{4,0},{1,5},{5,1},{2,6},{6,2},{3,7},{7,3},{8,12},{12,8},{9,1... | collective-permute-start | bytes 442376 | tf_op jit(solution)/shard_map/ppermute | solution.py:20
  109.3 6.8 %collective-permute-start.17 = (bf16[64,1152]{1,0:T(8,128)(2,1)S(1)}, bf16[64,1152]{1,0:T(8,128)(2,1)S(1)}, u32[]{:S(2)}, u32[]{:S(2)}) collective-permute-start(bf16[64,1152]{1,0:T(8,128)(2,1)S(1)} %get-tuple-element.43), channel_id=1, source_target_pairs={{0,5},{1,4},{4,1},{5,0},{2,7},{3,6},{6,3},{7,2},{8,13},{9,12},{12,... | collective-permute-start | bytes 442376 | tf_op jit(solution)/shard_map/ppermute | solution.py:20
  154.7 7.3 %collective-permute-start.24 = (bf16[64,1152]{1,0:T(8,128)(2,1)}, bf16[64,1152]{1,0:T(8,128)(2,1)}, u32[]{:S(2)}, u32[]{:S(2)}) collective-permute-start(bf16[64,1152]{1,0:T(8,128)(2,1)} %get-tuple-element.79), channel_id=1, source_target_pairs={{0,4},{4,0},{1,5},{5,1},{2,6},{6,2},{3,7},{7,3},{8,12},{12,8},{9,1... | collective-permute-start | bytes 442376 | tf_op jit(solution)/shard_map/ppermute | solution.py:20
  156.4 7.6 %collective-permute-start.25 = (bf16[64,1152]{1,0:T(8,128)(2,1)S(1)}, bf16[64,1152]{1,0:T(8,128)(2,1)}, u32[]{:S(2)}, u32[]{:S(2)}) collective-permute-start(bf16[64,1152]{1,0:T(8,128)(2,1)S(1)} %get-tuple-element.78), channel_id=1, source_target_pairs={{0,5},{1,4},{4,1},{5,0},{2,7},{3,6},{6,3},{7,2},{8,13},{9,12},{12,... | collective-permute-start | bytes 442376 | tf_op jit(solution)/shard_map/ppermute | solution.py:20
  165.9 8.0 %collective-permute-start.27 = (bf16[128,1152]{1,0:T(8,128)(2,1)S(1)}, bf16[128,1152]{1,0:T(8,128)(2,1)S(1)}, u32[]{:S(2)}, u32[]{:S(2)}) collective-permute-start(bf16[128,1152]{1,0:T(8,128)(2,1)S(1)} %pad_maximum_fusion.16), channel_id=1, source_target_pairs={{0,4},{4,0},{1,5},{5,1},{2,6},{6,2},{3,7},{7,3},{8,12},{12,8},{9,1... | collective-permute-start | bytes 884744 | tf_op jit(solution)/shard_map/ppermute | solution.py:20
  184.9 6.7 %collective-permute-start.31 = (bf16[64,1152]{1,0:T(8,128)(2,1)S(1)}, bf16[64,1152]{1,0:T(8,128)(2,1)S(1)}, u32[]{:S(2)}, u32[]{:S(2)}) collective-permute-start(bf16[64,1152]{1,0:T(8,128)(2,1)S(1)} %get-tuple-element.76), channel_id=1, source_target_pairs={{0,4},{4,0},{1,5},{5,1},{2,6},{6,2},{3,7},{7,3},{8,12},{12,8},{9,1... | collective-permute-start | bytes 442376 | tf_op jit(solution)/shard_map/ppermute | solution.py:20
  186.3 7.3 %collective-permute-start.32 = (bf16[64,1152]{1,0:T(8,128)(2,1)S(1)}, bf16[64,1152]{1,0:T(8,128)(2,1)S(1)}, u32[]{:S(2)}, u32[]{:S(2)}) collective-permute-start(bf16[64,1152]{1,0:T(8,128)(2,1)S(1)} %get-tuple-element.75), channel_id=1, source_target_pairs={{0,5},{1,4},{4,1},{5,0},{2,7},{3,6},{6,3},{7,2},{8,13},{9,12},{12,... | collective-permute-start | bytes 442376 | tf_op jit(solution)/shard_map/ppermute | solution.py:20
  198.2 6.7 %collective-permute-start.35 = (bf16[64,1152]{1,0:T(8,128)(2,1)S(1)}, bf16[64,1152]{1,0:T(8,128)(2,1)S(1)}, u32[]{:S(2)}, u32[]{:S(2)}) collective-permute-start(bf16[64,1152]{1,0:T(8,128)(2,1)S(1)} %get-tuple-element.36), channel_id=1, source_target_pairs={{0,5},{1,4},{4,1},{5,0},{2,7},{3,6},{6,3},{7,2},{8,13},{9,12},{12,... | collective-permute-start | bytes 442376 | tf_op jit(solution)/shard_map/ppermute | solution.py:20
  221.7 6.7 %collective-permute-start.39 = (bf16[64,1152]{1,0:T(8,128)(2,1)S(1)}, bf16[64,1152]{1,0:T(8,128)(2,1)S(1)}, u32[]{:S(2)}, u32[]{:S(2)}) collective-permute-start(bf16[64,1152]{1,0:T(8,128)(2,1)S(1)} %get-tuple-element.73), channel_id=1, source_target_pairs={{0,4},{4,0},{1,5},{5,1},{2,6},{6,2},{3,7},{7,3},{8,12},{12,8},{9,1... | collective-permute-start | bytes 442376 | tf_op jit(solution)/shard_map/ppermute | solution.py:20
  223.2 7.8 %collective-permute-start.40 = (bf16[64,1152]{1,0:T(8,128)(2,1)S(1)}, bf16[64,1152]{1,0:T(8,128)(2,1)S(1)}, u32[]{:S(2)}, u32[]{:S(2)}) collective-permute-start(bf16[64,1152]{1,0:T(8,128)(2,1)S(1)} %get-tuple-element.72), channel_id=1, source_target_pairs={{0,5},{1,4},{4,1},{5,0},{2,7},{3,6},{6,3},{7,2},{8,13},{9,12},{12,... | collective-permute-start | bytes 442376 | tf_op jit(solution)/shard_map/ppermute | solution.py:20
  238.9 10.6 %all-to-all-start.1 = ((bf16[16,2,216]{2,1,0:T(2,128)(2,1)}), bf16[16,2,216]{2,1,0:T(2,128)(2,1)}, u32[]{:S(2)}, u32[]{:S(2)}) async-start(bf16[16,2,216]{2,1,0:T(2,128)(2,1)} %reshape.470), calls=%async_computation.1 | async-start | bytes 32768 | tf_op jit(solution)/shard_map/all_to_all | solution.py:274
  243.0 91.9 %all-reduce.3.cloned.1.call-start = ((), (), s32[]{:S(2)}) async-start(), calls=%async_computation.8 | async-start | bytes 147456
  252.6 119.3 %reduce-scatter.7.cloned.1.call-start = ((), (), s32[]{:S(2)}) async-start(), calls=%async_computation.6 | async-start | bytes 1843200 | tf_op jit(solution)/shard_map/reduce_scatter | solution.py:251
  257.6 167.9 %reduce-scatter.9.cloned.1.call-start = ((), (), s32[]{:S(2)}) async-start(), calls=%async_computation.7 | async-start | bytes 3317760 | tf_op jit(solution)/shard_map/reduce_scatter | solution.py:226
  258.9 30.2 %collective-permute-start.26 = (bf16[64,1152]{1,0:T(8,128)(2,1)S(1)}, bf16[64,1152]{1,0:T(8,128)(2,1)}, u32[]{:S(2)}, u32[]{:S(2)}) collective-permute-start(bf16[64,1152]{1,0:T(8,128)(2,1)S(1)} %copy-done.19), channel_id=1, source_target_pairs={{0,1},{1,0},{2,3},{3,2},{4,5},{5,4},{6,7},{7,6},{8,9},{9,8},{10,11... | collective-permute-start | bytes 442376 | tf_op jit(solution)/shard_map/ppermute | solution.py:20
  296.6 78.2 %collective-permute-start.41 = (bf16[64,1152]{1,0:T(8,128)(2,1)S(1)}, bf16[64,1152]{1,0:T(8,128)(2,1)S(1)}, u32[]{:S(2)}, u32[]{:S(2)}) collective-permute-start(bf16[64,1152]{1,0:T(8,128)(2,1)S(1)} %fusion.50), channel_id=1, source_target_pairs={{0,1},{1,0},{2,3},{3,2},{4,5},{5,4},{6,7},{7,6},{8,9},{9,8},{10,11... | collective-permute-start | bytes 442376 | tf_op jit(solution)/shard_map/ppermute | solution.py:20
  426.8 7.1 %collective-permute-start.49 = (bf16[72,1152]{1,0:T(8,128)(2,1)S(1)}, bf16[72,1152]{1,0:T(8,128)(2,1)S(1)}, u32[]{:S(2)}, u32[]{:S(2)}) collective-permute-start(bf16[72,1152]{1,0:T(8,128)(2,1)S(1)} %get-tuple-element.65), channel_id=1, source_target_pairs={{0,4},{4,0},{1,5},{5,1},{2,6},{6,2},{3,7},{7,3},{8,12},{12,8},{9,1... | collective-permute-start | bytes 497672 | tf_op jit(solution)/shard_map/ppermute | solution.py:20
  428.4 8.2 %collective-permute-start.50 = (bf16[72,1152]{1,0:T(8,128)(2,1)S(1)}, bf16[72,1152]{1,0:T(8,128)(2,1)S(1)}, u32[]{:S(2)}, u32[]{:S(2)}) collective-permute-start(bf16[72,1152]{1,0:T(8,128)(2,1)S(1)} %get-tuple-element.64), channel_id=1, source_target_pairs={{0,6},{2,4},{4,2},{6,0},{1,7},{3,5},{5,3},{7,1},{8,14},{10,12},{12... | collective-permute-start | bytes 497672 | tf_op jit(solution)/shard_map/ppermute | solution.py:20
  (94 other events, 752.6 us)
Sparse Core Ops, SparseCore 0:
  44.2 36.7 all-gather.2
  90.1 54.2 all-gather.4
  252.7 82.1 all-reduce.2
  337.2 34.6 reduce-scatter.6
  374.0 51.4 reduce-scatter.8

commit v2 on v1

--- a/solution.py
+++ b/solution.py
@@ -1,11 +1,15 @@
 import jax
 import jax.numpy as jnp
 from jax import lax
+from jax.experimental import pallas as pl
+from jax.experimental.pallas import tpu as pltpu
 from jax.sharding import Mesh, PartitionSpec as P
 
 HEAD = 72
 EPSILON = 1e-06
 GROUP = 4
+ROOT = 0.7978845608028654
+VMEM_LIMIT = 48 * 1024 * 1024
 
 bf16 = jnp.bfloat16
 f32 = jnp.float32
@@ -33,6 +37,39 @@
     return value
 
 
+def after(value, *others):
+    def nothing(*refs):
+        pass
+
+    return pl.pallas_call(
+        nothing,
+        out_shape=jax.ShapeDtypeStruct(value.shape, value.dtype),
+        in_specs=[pl.BlockSpec(memory_space=pl.ANY)] * (1 + len(others)),
+        out_specs=pl.BlockSpec(memory_space=pl.ANY),
+        input_output_aliases={0: 0},
+    )(value, *others)
+
+
+def scatter_dp(value):
+    masks = []
+    mask = 1
+    while mask < lax.axis_size("zz"):
+        masks.append(("zz", mask))
+        mask *= 2
+    for axis, mask in masks[::-1] + [("xx", 1), ("core", 1)]:
+        half = value.shape[0] // 2
+        value = value[:half] + exchange(value[half:], axis, mask)
+    return value
+
+
+def sum_zz(value):
+    mask = 1
+    while mask < lax.axis_size("zz"):
+        value = value + exchange(value, "zz", mask)
+        mask *= 2
+    return value
+
+
 def gather_dp(value):
     for axis in ("core", "xx"):
         value = jnp.concatenate([value, exchange(value, axis)], axis=0)
@@ -56,10 +93,9 @@
     return jnp.concatenate([near, exchange(near, "core")], axis=0)
 
 
-def scatter_eight(partial):
-    half = partial.shape[0] // 2
-    rows = half // 4
-    near = partial[:half] + exchange(partial[half:].astype(bf16), "core").astype(f32)
+def scatter_eight(keep, send):
+    rows = keep.shape[0] // 4
+    near = keep + exchange(send, "core").astype(f32)
     sent = near.astype(bf16)
     over_y = exchange(sent[rows : 2 * rows], "tensor")
     over_x = exchange(sent[2 * rows : 3 * rows], "xx")
@@ -93,8 +129,182 @@
     return inverse * (scaled - mean_scaled - normed * mean_product)
 
 
-def tanh_gelu(values):
-    return jax.nn.gelu(values, approximate=True)
+def transposed_dot(left, right):
+    return lax.dot_general(left, right, (((0,), (0,)), ((), ())), preferred_element_type=f32)
+
+
+def dot_rows(left, right):
+    return lax.dot_general(left, right, (((1,), (1,)), ((), ())), preferred_element_type=f32)
+
+
+def dot(left, right):
+    return lax.dot_general(left, right, (((1,), (0,)), ((), ())), preferred_element_type=f32)
+
+
+def call(kernel, outs, args, flops=0):
+    return pl.pallas_call(
+        kernel,
+        out_shape=[jax.ShapeDtypeStruct(shape, dtype) for shape, dtype in outs],
+        in_specs=[pl.BlockSpec(memory_space=pltpu.VMEM)] * len(args),
+        out_specs=[pl.BlockSpec(memory_space=pltpu.VMEM)] * len(outs),
+        compiler_params=pltpu.CompilerParams(vmem_limit_bytes=VMEM_LIMIT),
+        cost_estimate=pl.CostEstimate(flops=flops, bytes_accessed=0, transcendentals=0),
+    )(*args)
+
+
+def head_masks(feats):
+    lane = lax.broadcasted_iota(jnp.int32, (1, feats), 1)
+    return [(lane >= h * HEAD) & (lane < (h + 1) * HEAD) for h in range(feats // HEAD)]
+
+
+def only(mask, value):
+    return jnp.where(mask, value, jnp.zeros_like(value))
+
+
+def split_store(keep_ref, send_ref, value):
+    half = value.shape[0] // 2
+    keep_ref[...] = value[:half]
+    send_ref[...] = value[half:].astype(bf16)
+
+
+def attention_forward(tokens, shift, scale, weights, biases):
+    total, width = tokens.shape
+    feats = biases.shape[1]
+    seq = total // GROUP
+    factor = HEAD ** (-0.5)
+
+    def kernel(tok, sh, sc, w, b, normed, q_out, k_out, v_out, att, keep, send):
+        for i in range(GROUP):
+            rows = slice(i * seq, (i + 1) * seq)
+            value = norm(tok[rows, :].astype(f32))[0]
+            normed[rows, :] = (value * (1.0 + sc[i : i + 1, :]) + sh[i : i + 1, :]).astype(bf16)
+        projected = dot(normed[...], w[:, : 3 * feats])
+        q_out[...] = (projected[:, :feats] + b[0:1, :]).astype(bf16)
+        k_out[...] = projected[:, feats : 2 * feats].astype(bf16)
+        v_out[...] = (projected[:, 2 * feats :] + b[1:2, :]).astype(bf16)
+        masks = head_masks(feats)
+        for i in range(GROUP):
+            rows = slice(i * seq, (i + 1) * seq)
+            q, k, v = q_out[rows, :], k_out[rows, :], v_out[rows, :]
+            result = jnp.zeros((seq, feats), f32)
+            for mask in masks:
+                probs = softmax(dot_rows(only(mask, q), k) * factor)
+                result += dot(probs.astype(bf16), only(mask, v))
+            att[rows, :] = result.astype(bf16)
+        split_store(keep, send, dot_rows(att[...], w[:, 3 * feats :]))
+
+    return call(
+        kernel,
+        [
+            ((total, width), bf16),
+            ((total, feats), bf16),
+            ((total, feats), bf16),
+            ((total, feats), bf16),
+            ((total, feats), bf16),
+            ((total // 2, width), f32),
+            ((total // 2, width), bf16),
+        ],
+        (tokens, shift, scale, weights, biases),
+    )
+
+
+def softmax(scores):
+    exponent = jnp.exp(scores - jnp.max(scores, axis=-1, keepdims=True))
+    return exponent / jnp.sum(exponent, axis=-1, keepdims=True)
+
+
+def attention_backward(grad_branch, normed, q_all, k_all, v_all, att, weights):
+    total, width = normed.shape
+    feats = q_all.shape[1]
+    seq = total // GROUP
+    factor = HEAD ** (-0.5)
+
+    def kernel(g, n, q_in, k_in, v_in, a, w, grads, keep, send, bias, grad_in):
+        masks = head_masks(feats)
+        grad_att = dot(g[...], w[:, 3 * feats :]).astype(bf16)
+        q_sum = jnp.zeros((1, feats), f32)
+        v_sum = jnp.zeros((1, feats), f32)
+        for i in range(GROUP):
+            rows = slice(i * seq, (i + 1) * seq)
+            q, k, v = q_in[rows, :], k_in[rows, :], v_in[rows, :]
+            ga = grad_att[rows, :]
+            gq = jnp.zeros((seq, feats), f32)
+            gk = jnp.zeros((seq, feats), f32)
+            gv = jnp.zeros((seq, feats), f32)
+            for mask in masks:
+                probs = softmax(dot_rows(only(mask, q), k) * factor)
+                gv += only(mask, transposed_dot(probs.astype(bf16), ga))
+                gp = dot_rows(only(mask, ga), v)
+                gs = probs * (gp - jnp.sum(probs * gp, axis=-1, keepdims=True))
+                gs = gs.astype(bf16)
+                gq += only(mask, dot(gs, k))
+                gk += only(mask, transposed_dot(gs, q))
+            gq, gk = gq * factor, gk * factor
+            q_sum += jnp.sum(gq, axis=0, keepdims=True)
+            v_sum += jnp.sum(gv, axis=0, keepdims=True)
+            grad_in[rows, :] = jnp.concatenate([gq, gk, gv], axis=1).astype(bf16)
+        bias[0:1, :] = q_sum
+        bias[1:2, :] = v_sum
+        split_store(keep, send, dot_rows(grad_in[...], w[:, : 3 * feats]))
+        grads[:, : 3 * feats] = transposed_dot(n[...], grad_in[...]).astype(bf16)
+        grads[:, 3 * feats :] = transposed_dot(g[...], a[...]).astype(bf16)
+
+    return call(
+        kernel,
+        [
+            ((width, 4 * feats), bf16),
+            ((total // 2, width), f32),
+            ((total // 2, width), bf16),
+            ((2, feats), f32),
+            ((total, 3 * feats), bf16),
+        ],
+        (grad_branch, normed, q_all, k_all, v_all, att, weights),
+    )
+
+
+def feed_forward(normed, weights, bias, cot, gate):
+    total, width = normed.shape
+    units = weights.shape[1] // 2
+    seq = total // GROUP
+
+    def kernel(n, w, b, c, gt, grads, keep, send, out_keep, out_send, bias_out, fc2_out, grad_out):
+        sums = []
+        for i in range(2 * GROUP):
+            rows = slice(i * seq // 2, (i + 1) * seq // 2)
+            value = c[rows, :].astype(f32) * gt[i // 2 : i // 2 + 1, :]
+            sums.append(jnp.sum(value, axis=0, keepdims=True))
+            grad_out[rows, :] = value.astype(bf16)
+        pairs = [sums[2 * i] + sums[2 * i + 1] for i in range(GROUP)]
+        fc2_out[...] = (pairs[0] + pairs[1]) + (pairs[2] + pairs[3])
+        pre = dot(n[...], w[:, :units]) + b[...]
+        inner = ROOT * (pre + 0.044715 * (pre * pre * pre))
+        tanh = jnp.tanh(inner)
+        act = (0.5 * pre * (1.0 + tanh)).astype(bf16)
+        slope = 0.5 * (1.0 + tanh) + 0.5 * pre * (1.0 - tanh * tanh) * (
+            ROOT * (1.0 + 3 * 0.044715 * (pre * pre))
+        )
+        grad_pre = dot(grad_out[...], w[:, units:]) * slope
+        bias_out[...] = jnp.sum(grad_pre, axis=0, keepdims=True)
+        grad_pre = grad_pre.astype(bf16)
+        grads[:, units:] = transposed_dot(grad_out[...], act).astype(bf16)
+        grads[:, :units] = transposed_dot(n[...], grad_pre).astype(bf16)
+        split_store(keep, send, dot_rows(grad_pre, w[:, :units]))
+        split_store(out_keep, out_send, dot_rows(act, w[:, units:]))
+
+    return call(
+        kernel,
+        [
+            ((width, 2 * units), bf16),
+            ((total // 2, width), f32),
+            ((total // 2, width), bf16),
+            ((total // 2, width), f32),
+            ((total // 2, width), bf16),
+            ((1, units), f32),
+            ((1, width), f32),
+            ((total, width), bf16),
+        ],
+        (normed, weights, bias, cot, gate),
+    )
 
 
 def local(
@@ -119,9 +329,7 @@
     hidden = fc1_weight.shape[1]
     feats = t_width // GROUP
     units = hidden // GROUP
-    heads = feats // HEAD
     n_dp = width // d_rows
-    factor = HEAD ** (-0.5)
     t = lax.axis_index("tensor")
     place = lax.axis_index("xx") * 2 + lax.axis_index("core")
     dp = lax.axis_index("zz") * GROUP + place
@@ -131,18 +339,15 @@
     proj_chunks = proj_weight.T.reshape(d_rows, GROUP, feats).transpose(1, 0, 2)
     fc1_chunks = fc1_weight.reshape(d_rows, GROUP, units).transpose(1, 0, 2)
     fc2_chunks = fc2_weight.T.reshape(d_rows, GROUP, units).transpose(1, 0, 2)
-    attn_part = swap_four(jnp.concatenate([qkv_chunks, proj_chunks], axis=2), place)
+    attn_chunks = jnp.concatenate([qkv_chunks, proj_chunks], axis=2)
+    attn_part = swap_four(attn_chunks, place)
     mlp_part = swap_four(jnp.concatenate([fc1_chunks, fc2_chunks], axis=2), place)
     attn_part = attn_part.reshape(GROUP * d_rows, 4 * feats)
     mlp_part = mlp_part.reshape(GROUP * d_rows, 2 * units)
     attn_full = lax.all_gather(attn_part, "zz", axis=0, tiled=True)
     mlp_full = lax.all_gather(mlp_part, "zz", axis=0, tiled=True)
-    qkv_full = attn_full[:, : 3 * feats]
-    proj_full = attn_full[:, 3 * feats :]
-    fc1_full = mlp_full[:, :units]
-    fc2_full = mlp_full[:, units:]
-
-    cond_values = conditions.astype(f32)
+
+    cond_values = after(conditions, attn_chunks).astype(f32)
     silu_conds = jax.nn.silu(cond_values).astype(bf16)
     small = jnp.concatenate(
         [silu_conds, qv_bias, proj_bias[None], fc1_bias, fc2_bias[None]], axis=1
@@ -180,33 +385,34 @@
 
     tokens_own = own_order(tokens)
     cot_own = own_order(cotangent)
-    tokens_all = gather_four(tokens_own).astype(f32).reshape(GROUP, seq, width)
-    cot_all = gather_four(cot_own).astype(f32).reshape(GROUP, seq, width)
+    tokens_low = gather_four(tokens_own)
+    cot_low = gather_four(cot_own)
     inputs_half = tokens_own[:rows].astype(f32)
     grad_out_half = cot_own[:rows].astype(f32)
 
     total = GROUP * seq
-    normed_one = norm(tokens_all)[0] * (1.0 + scale_attn[:, None]) + shift_attn[:, None]
-    normed_one = normed_one.astype(bf16).reshape(total, width)
-    projected = product(normed_one, qkv_full, "sd,df->sf")
-    head_shape = (GROUP, seq, heads, HEAD)
-    queries = (projected[:, :feats] + qv_here[0]).astype(bf16).reshape(head_shape)
-    keys = projected[:, feats : 2 * feats].astype(bf16).reshape(head_shape)
-    values = (projected[:, 2 * feats :] + qv_here[1]).astype(bf16).reshape(head_shape)
-    scores = product(queries, keys, "lqhd,lkhd->lhqk") * factor
-    exponent = jnp.exp(scores - jnp.max(scores, axis=-1, keepdims=True))
-    probs = exponent / jnp.sum(exponent, axis=-1, keepdims=True)
-    probs_low = probs.astype(bf16)
-    attended = product(probs_low, values, "lhqk,lkhd->lqhd").astype(bf16).reshape(total, feats)
-    branch_half = scatter_eight(product(attended, proj_full, "sf,df->sd")) + proj_bias_full
+    normed_one, queries, keys, values, attended, keep, send = attention_forward(
+        tokens_low, shift_attn, scale_attn, attn_full, qv_here
+    )
+    branch_half = scatter_eight(keep, send) + proj_bias_full
     hidden_half = inputs_half + gate_attn[0] * branch_half
 
     norm_two, inverse_two = norm(hidden_half)
     normed_two_half = (norm_two * (1.0 + scale_mlp[0]) + shift_mlp[0]).astype(bf16)
+    normed_two_half = after(normed_two_half, cot_low)
     normed_two = gather_eight(normed_two_half)
-    pre_act = product(normed_two, fc1_full, "sd,df->sf") + fc1_bias_here
-    activated = tanh_gelu(pre_act).astype(bf16)
-    mlp_half = scatter_eight(product(activated, fc2_full, "sf,df->sd")) + fc2_bias_full
+    mlp_grad, keep, send, out_keep, out_send, fc1_bias_part, fc2_bias_part, _ = feed_forward(
+        normed_two, mlp_full, fc1_bias_here[None], cot_low, gate_mlp
+    )
+    mlp_grad = lax.psum_scatter(mlp_grad, "zz", scatter_dimension=0, tiled=True)
+    grad_normed_two = scatter_eight(keep, send)
+    grad_hidden_half = grad_out_half + norm_back(
+        grad_normed_two, norm_two, inverse_two, scale_mlp[0]
+    )
+    grad_branch_half = (gate_attn[0] * grad_hidden_half).astype(bf16)
+    grad_branch_all = gather_eight(grad_branch_half)
+
+    mlp_half = scatter_eight(out_keep, after(out_send, grad_branch_half)) + fc2_bias_full
     block_half = (hidden_half + gate_mlp[0] * mlp_half).astype(bf16)
 
     def token_sum(value):
@@ -214,44 +420,14 @@
         pairs = parts[0::2] + parts[1::2]
         return (pairs[0] + pairs[1]) + (pairs[2] + pairs[3])
 
-    grad_branch_mlp = (gate_mlp[:, None] * cot_all).reshape(total, width)
-    fc2_bias_part = token_sum(grad_branch_mlp)
-    grad_branch_low = grad_branch_mlp.astype(bf16)
-    fc2_grad = product(grad_branch_low, activated, "sd,sf->df").astype(bf16)
-    grad_activated = product(grad_branch_low, fc2_full, "sd,df->sf")
-    grad_pre = jax.vjp(tanh_gelu, pre_act)[1](grad_activated)[0]
-    fc1_bias_part = jnp.sum(grad_pre, axis=0)
-    grad_pre_low = grad_pre.astype(bf16)
-    fc1_grad = product(normed_two, grad_pre_low, "sd,sf->df").astype(bf16)
-    mlp_grad = lax.psum_scatter(
-        jnp.concatenate([fc1_grad, fc2_grad], axis=1), "zz", scatter_dimension=0, tiled=True
-    )
-    grad_normed_two = scatter_eight(product(grad_pre_low, fc1_full, "sf,df->sd"))
-    grad_hidden_half = grad_out_half + norm_back(
-        grad_normed_two, norm_two, inverse_two, scale_mlp[0]
-    )
-    grad_branch_half = (gate_attn[0] * grad_hidden_half).astype(bf16)
-
-    grad_branch_all = gather_eight(grad_branch_half)
     proj_bias_part = token_sum(grad_branch_all.astype(f32))
-    proj_grad = product(grad_branch_all, attended, "sd,sf->df").astype(bf16)
-    grad_attended = product(grad_branch_all, proj_full, "sd,df->sf").astype(bf16)
-    grad_attended = grad_attended.reshape(head_shape)
-    grad_values = product(probs_low, grad_attended, "lhqk,lqhd->lkhd")
-    grad_probs = product(grad_attended, values, "lqhd,lkhd->lhqk")
-    grad_scores = probs * (grad_probs - jnp.sum(probs * grad_probs, axis=-1, keepdims=True))
-    grad_scores = grad_scores.astype(bf16)
-    grad_queries = product(grad_scores, keys, "lhqk,lkhd->lqhd") * factor
-    grad_keys = product(grad_scores, queries, "lhqk,lqhd->lkhd") * factor
-    grad_queries = grad_queries.reshape(total, feats)
-    grad_keys = grad_keys.reshape(total, feats)
-    grad_values = grad_values.reshape(total, feats)
-    grad_qkv_low = jnp.concatenate([grad_queries, grad_keys, grad_values], axis=1).astype(bf16)
-    qkv_grad = product(normed_one, grad_qkv_low, "sd,sf->df").astype(bf16)
+    attn_grad, keep, send, qv_bias_part, _ = attention_backward(
+        grad_branch_all, normed_one, queries, keys, values, attended, attn_full
+    )
     attn_grad = lax.psum_scatter(
-        jnp.concatenate([qkv_grad, proj_grad], axis=1), "zz", scatter_dimension=0, tiled=True
-    )
-    grad_normed_one = scatter_eight(product(grad_qkv_low, qkv_full, "sf,df->sd"))
+        after(attn_grad, mlp_grad), "zz", scatter_dimension=0, tiled=True
+    )
+    grad_normed_one = scatter_eight(keep, send)
     norm_one, inverse_one = norm(inputs_half)
     tokens_grad_half = grad_hidden_half + norm_back(
         grad_normed_one, norm_one, inverse_one, scale_attn[0]
@@ -276,24 +452,18 @@
     )
     mod_bias_grad = jnp.sum(grad_mod_columns.astype(f32), axis=0)
     mod_weight_grad = product(all_silu, grad_mod_columns, "ld,lc->dc")
-    grad_silu = lax.psum_scatter(
-        product(grad_mod_columns, mod_weight, "lc,dc->ld"),
-        ("zz", "xx", "core"),
-        scatter_dimension=0,
-        tiled=True,
-    )
+    grad_silu = scatter_dp(reorder(product(grad_mod_columns, mod_weight, "lc,dc->ld"), dp))
     conditions_grad = jax.vjp(jax.nn.silu, cond_values)[1](grad_silu)[0]
 
     biases = jnp.concatenate(
         [
-            jnp.sum(grad_queries, axis=0),
-            jnp.sum(grad_values, axis=0),
-            fc1_bias_part,
+            qv_bias_part.reshape(-1),
+            fc1_bias_part[0],
             proj_bias_part,
-            fc2_bias_part,
+            fc2_bias_part[0],
         ]
     )
-    biases = lax.psum(biases, "zz")
+    biases = sum_zz(biases)
     own = 2 * feats + units
     group_biases = biases[None, :own]
     for axis in ("core", "xx"):

time: 454 us -> 335 us (0.74)
  waiting for transfers between devices: 235 us -> 144 us
  matrix products: 34.4 us -> 2.35 us
  Pallas kernels: 0 us -> 22.5 us
  blocking collectives: 15.9 us -> 0 us
  local copies, waits for them, and re-layouts: 51.2 us -> 40.4 us
    reduce_scatter x2, waiting for transfers between devices: 76.2 us -> 19.8 us  [the longest x1 19.8 us: local(): lax.psum_scatter(after(attn_grad, mlp_grad), 'zz', scatter_dimension=0, t...]
    unnamed x6 -> x4, waiting for transfers between devices: 34.9 us -> 0.07 us
    dot_general x20 -> x3, matrix products: 33.3 us -> 2.35 us  [product(): return jnp.einsum(form, left, right, preferred_element_type=f32)]
    pallas_call x0 -> x7, Pallas kernels: none -> 22.5 us  [the longest x3 22.5 us: call(): pl.pallas_call(kernel, out_shape=[jax.ShapeDtypeStruct(shape, dtype) for...]
    psum x1 -> x0, blocking collectives: 15.9 us -> none  [local(): biases = lax.psum(biases, 'zz')]
    another operation x6 -> x3, local copies, waits for them, and re-layouts: 5.71 us -> 0.77 us  [swap_four(): return reorder(jnp.stack(got), place)]
    ppermute x51 -> x57, starting transfers between devices: 45.5 us -> 47.4 us  [exchange(): return lax.ppermute(value, axis, [(i, i ^ mask) for i in range(size)])]
    ppermute x51 -> x57, waiting for transfers between devices: 69.6 us -> 68.3 us  [exchange(): return lax.ppermute(value, axis, [(i, i ^ mask) for i in range(size)])]
  transfers between devices with their start and end apart: 58 -> 63, of which waited for: 37 -> 37; matrix products, arithmetic and copies ran while one was open for 17% -> 19% of each run, Pallas kernels for 0% -> 4%
where the time goes in v2:
time: 335 us; the launch traced here: 328 us
  waiting for transfers between devices  144 us (43%)
  starting transfers between devices  57.8 us (17%)
  other arithmetic  45.4 us (14%)
  local copies, waits for them, and re-layouts  40.4 us (12%)
  Pallas kernels  22.5 us (7%)
  between operations  15.5 us (5%)
    ppermute x57, waiting for transfers between devices, exchange(): return lax.ppermute(value, axis, [(i, i ^ mask) for i in range(size)])  68.3 us
    ppermute x57, starting transfers between devices, exchange(): return lax.ppermute(value, axis, [(i, i ^ mask) for i in range(size)])  47.4 us
    all_gather x1, waiting for transfers between devices, local(): mlp_full = lax.all_gather(mlp_part, 'zz', axis=0, tiled=True)  25.5 us
    pallas_call x3, Pallas kernels, call(): pl.pallas_call(kernel, out_shape=[jax.ShapeDtypeStruct(shape, dtype) for...  22.5 us
    all_gather x1, waiting for transfers between devices, local(): attn_full = lax.all_gather(attn_part, 'zz', axis=0, tiled=True)  22.4 us
    reduce_scatter x1, waiting for transfers between devices, local(): lax.psum_scatter(after(attn_grad, mlp_grad), 'zz', scatter_dimension=0, t...  19.8 us
    unnamed x164, local copies, waits for them, and re-layouts  19 us
    all_to_all x1, waiting for transfers between devices, local(): lax.all_to_all(grad_mod, ('zz', 'xx', 'core'), split_axis=1, concat_axis=...  6.71 us
  transfers between devices with their start and end apart: 63, of which 37 were waited for; matrix products, arithmetic and copies ran while one was open for 19% of the time, Pallas kernels for 4%

profile of v2, /device:TPU:0, one launch (start us, length us, event | category | flops | bytes accessed | tf_op | source)
XLA Modules:
  0.0 328.4 jit_solution(4740279993543481464)
XLA Ops:
  15.3 2.5 collective-permute-start.4
  21.3 3.7 %fusion.8 = (bf16[1,72,1152]{2,0,1:T(2,128)(2,1)}, bf16[1,72,1152]{2,0,1:T(2,128)(2,1)S(1)}, bf16[1,72,1152]{2,0,1:T(2,128)(2,1)S(1)}, bf16[1,72,1152]{2,0,1:T(2,128)(2,1)S(1)}) fusion(s32[]{:T(128)S(6)} %select_n.455, bf16[4,72,576]{2,0,1:T(4,128)(2,1)S(1)} %bitcast.162, bf16[4,72,576]{2,0,1:T(4,128)(2,1)S(1)} %bitcast.163, s32[]{:T(128)S(6)} %select_n.456, ...), kind=kLoop, calls=%fused_computation.58 | loop fusion | flops 1327104 | bytes 1327120 | tf_op jit(solution)/shard_map/concatenate | solution.py:344
  25.4 4.3 %collective-permute-done.1 = bf16[2,1512]{1,0:T(2,128)(2,1)S(1)} collective-permute-done((bf16[2,1512]{1,0:T(2,128)(2,1)S(1)}, bf16[2,1512]{1,0:T(2,128)(2,1)S(1)}, u32[]{:S(2)}, u32[]{:S(2)}) %collective-permute-start.1) | collective-permute-done | bytes 6080 | tf_op jit(solution)/shard_map/ppermute | solution.py:24
  33.6 2.9 collective-permute-start.3
  42.8 5.1 %all-to-all-start = ((f32[16,1,432]{2,1,0:T(1,128)}), f32[16,1,432]{2,1,0:T(1,128)S(1)}, u32[]{:S(2)}, u32[]{:S(2)}) async-start(f32[16,1,432]{2,1,0:T(1,128)} %copy.95), calls=%async_computation | async-start | bytes 65536 | tf_op jit(solution)/shard_map/all_to_all | solution.py:366
  55.9 3.3 %collective-permute-done.6 = f32[1,6912]{1,0:T(1,128)S(1)} collective-permute-done((f32[1,6912]{1,0:T(1,128)S(1)}, f32[1,6912]{1,0:T(1,128)S(1)}, u32[]{:S(2)}, u32[]{:S(2)}) %collective-permute-start.6) | collective-permute-done | bytes 27680 | tf_op jit(solution)/shard_map/ppermute | solution.py:24
  66.7 22.4 %all-gather.3.cloned.1.call-done.w = bf16[1152,576]{1,0:T(8,128)(2,1)} async-done(((bf16[288,576]{1,0:T(8,128)(2,1)}), bf16[1152,576]{1,0:T(8,128)(2,1)}) %all-gather.3.cloned.1.call-update) | async-done | bytes 1327120 | tf_op jit(solution)/shard_map/all_gather | solution.py:347
  89.1 5.0 %shard_map.229 = (bf16[512,1152]{1,0:T(8,128)(2,1)S(1)}, bf16[512,144]{1,0:T(8,128)(2,1)S(1)}, bf16[512,144]{1,0:T(8,128)(2,1)S(1)}, bf16[512,144]{1,0:T(8,128)(...) custom-call(bf16[512,1152]{1,0:T(8,128)(2,1)S(1)} %pad_maximum_fusion.tok, ...), custom_call_target="tpu_custom_call" | custom-call | tf_op jit(solution)/shard_map/pallas_call | solution.py:145
  98.3 2.4 collective-permute-start.14
  101.9 2.1 pad_maximum_fusion.1.refs_1_.c
  105.9 2.8 collective-permute-done.13
  117.1 2.3 collective-permute-done.18
  119.4 2.0 collective-permute-done.19
  124.6 25.5 %all-gather.5.cloned.1.call-done.w = bf16[1152,1152]{1,0:T(8,128)(2,1)} async-done(((bf16[288,1152]{1,0:T(8,128)(2,1)}), bf16[1152,1152]{1,0:T(8,128)(2,1)}) %all-gather.5.cloned.1.call-update) | async-done | bytes 2654224 | tf_op jit(solution)/shard_map/all_gather | solution.py:348
  150.0 8.3 %shard_map.231 = (bf16[1152,1152]{1,0:T(8,128)(2,1)}, f32[256,1152]{1,0:T(8,128)S(1)}, bf16[256,1152]{1,0:T(8,128)(2,1)S(1)}, f32[256,1152]{1,0:T(8,128)S(1)}, b...) custom-call(bf16[512,1152]{1,0:T(8,128)(2,1)S(1)} %constant_dynamic-upda, ...), custom_call_target="tpu_custom_call" | custom-call | tf_op jit(solution)/shard_map/pallas_call | solution.py:145
  160.6 2.4 collective-permute-start.27
  164.2 4.1 %collective-permute-done.27 = bf16[64,1152]{1,0:T(8,128)(2,1)S(1)} collective-permute-done((bf16[64,1152]{1,0:T(8,128)(2,1)S(1)}, bf16[64,1152]{1,0:T(8,128)(2,1)S(1)}, u32[]{:S(2)}, u32[]{:S(2)}) %collective-permute-start.27) | collective-permute-done | bytes 147488 | tf_op jit(solution)/shard_map/ppermute | solution.py:24
  168.3 2.4 collective-permute-done.26
  180.6 2.6 collective-permute-done.34
  196.5 9.3 %shard_map.233 = (bf16[1152,576]{1,0:T(8,128)(2,1)}, f32[256,1152]{1,0:T(8,128)S(1)}, bf16[256,1152]{1,0:T(8,128)(2,1)S(1)}, f32[2,144]{1,0:T(2,128)S(1)}, bf16[512,432]{1,0:T(8,128)(2,1)}) custom-call(bf16[512,1152]{1,0:T(8,128)(2,1)S(1)} %constant_dynamic-update-slice_fusion.7.g, bf16[512,1152]{1,0:T(8,128)(2,1)S(1)} %copy-done.4, ...), custom_call_target="tpu_custom_call" | custom-call | tf_op jit(solution)/shard_map/pallas_call | solution.py:145
  213.5 2.3 fusion.50
  217.9 2.5 collective-permute-start.31
  224.2 4.6 %collective-permute-done.53 = f32[2,864]{1,0:T(2,128)S(1)} collective-permute-done((f32[2,864]{1,0:T(2,128)S(1)}, f32[2,864]{1,0:T(2,128)S(1)}, u32[]{:S(2)}, u32[]{:S(2)}) %collective-permute-start.53) | collective-permute-done | bytes 6944 | tf_op jit(solution)/shard_map/ppermute | solution.py:24
  229.8 2.3 fusion.49
  235.9 3.9 %collective-permute-done.40 = bf16[64,1152]{1,0:T(8,128)(2,1)S(1)} collective-permute-done((bf16[64,1152]{1,0:T(8,128)(2,1)S(1)}, bf16[64,1152]{1,0:T(8,128)(2,1)S(1)}, u32[]{:S(2)}, u32[]{:S(2)}) %collective-permute-start.40) | collective-permute-done | bytes 147488 | tf_op jit(solution)/shard_map/ppermute | solution.py:24
  249.8 4.5 %all-to-all-start.1 = ((bf16[16,2,216]{2,1,0:T(2,128)(2,1)}), bf16[16,2,216]{2,1,0:T(2,128)(2,1)S(1)}, u32[]{:S(2)}, u32[]{:S(2)}) async-start(bf16[16,2,216]{2,1,0:T(2,128)(2,1)} %reshape.417), calls=%async_computation.1 | async-start | bytes 32768 | tf_op jit(solution)/shard_map/all_to_all | solution.py:450
  254.3 6.7 %all-to-all-done.1 = bf16[16,2,216]{2,1,0:T(2,128)(2,1)S(1)} async-done(((bf16[16,2,216]{2,1,0:T(2,128)(2,1)}), bf16[16,2,216]{2,1,0:T(2,128)(2,1)S(1)}, u32[]{:S(2)}, u32[]{:S(2)}) %all-to-all-start.1) | async-done | bytes 13856 | tf_op jit(solution)/shard_map/all_to_all | solution.py:450
  262.4 4.6 %collective-permute-done.43 = f32[8,1152]{1,0:T(8,128)S(1)} collective-permute-done((f32[8,1152]{1,0:T(8,128)S(1)}, f32[8,1152]{1,0:T(8,128)S(1)}, u32[]{:S(2)}, u32[]{:S(2)}) %collective-permute-start.43) | collective-permute-done | bytes 36896 | tf_op jit(solution)/shard_map/ppermute | solution.py:24
  268.1 2.8 collective-permute-done.44
  281.2 3.7 %collective-permute-done.56 = bf16[72,1152]{1,0:T(8,128)(2,1)S(1)} collective-permute-done((bf16[72,1152]{1,0:T(8,128)(2,1)S(1)}, bf16[72,1152]{1,0:T(8,128)(2,1)S(1)}, u32[]{:S(2)}, u32[]{:S(2)}) %collective-permute-start.56) | collective-permute-done | bytes 165920 | tf_op jit(solution)/shard_map/ppermute | solution.py:24
  284.9 3.8 %collective-permute-done.55 = bf16[72,1152]{1,0:T(8,128)(2,1)S(1)} collective-permute-done((bf16[72,1152]{1,0:T(8,128)(2,1)S(1)}, bf16[72,1152]{1,0:T(8,128)(2,1)S(1)}, u32[]{:S(2)}, u32[]{:S(2)}) %collective-permute-start.55) | collective-permute-done | bytes 165920 | tf_op jit(solution)/shard_map/ppermute | solution.py:24
  289.2 19.8 %reduce-scatter.5.cloned.1.call-done = bf16[288,576]{1,0:T(8,128)(2,1)} async-done(((bf16[1152,576]{1,0:T(8,128)(2,1)}), bf16[288,576]{1,0:T(8,128)(2,1)}) %reduce-scatter.5.cloned.1.call-update) | async-done | bytes 331792 | tf_op jit(solution)/shard_map/reduce_scatter | solution.py:427
  (457 shorter events, 135.9 us)
Async XLA Ops:
  13.8 11.2 %collective-permute-start = (bf16[1,1512]{1,0:T(2,128)(2,1)S(1)}, bf16[1,1512]{1,0:T(2,128)(2,1)S(1)}, u32[]{:S(2)}, u32[]{:S(2)}) collective-permute-start(bf16[1,1512]{1,0:T(2,128)(2,1)S(1)} %concatenate.102), channel_id=1, source_target_pairs={{0,2},{2,0},{1,3},{3,1},{4,6},{6,4},{5,7},{7,5},{8,10},{10,8},{9,1... | collective-permute-start | bytes 9080 | tf_op jit(solution)/shard_map/ppermute | solution.py:24
  15.3 47.3 %collective-permute-start.4 = (bf16[128,1152]{1,0:T(8,128)(2,1)}, bf16[128,1152]{1,0:T(8,128)(2,1)}, u32[]{:S(2)}, u32[]{:S(2)}) collective-permute-start(bf16[128,1152]{1,0:T(8,128)(2,1)} %pad_maximum_fusion.14), channel_id=1, source_target_pairs={{0,4},{4,0},{1,5},{5,1},{2,6},{6,2},{3,7},{7,3},{8,12},{12,8},{9,1... | collective-permute-start | bytes 884744 | tf_op jit(solution)/shard_map/ppermute | solution.py:24
  18.6 29.6 %collective-permute-start.10 = (bf16[72,576]{1,0:T(8,128)(2,1)}, bf16[72,576]{1,0:T(8,128)(2,1)}, u32[]{:S(2)}, u32[]{:S(2)}) collective-permute-start(bf16[72,576]{1,0:T(8,128)(2,1)} %get-tuple-element.117), channel_id=1, source_target_pairs={{0,6},{2,4},{4,2},{6,0},{1,7},{3,5},{5,3},{7,1},{8,14},{10,12},{12... | collective-permute-start | bytes 248840 | tf_op jit(solution)/shard_map/ppermute | solution.py:24
  18.7 31.3 %collective-permute-start.9 = (bf16[72,576]{1,0:T(8,128)(2,1)}, bf16[72,576]{1,0:T(8,128)(2,1)}, u32[]{:S(2)}, u32[]{:S(2)}) collective-permute-start(bf16[72,576]{1,0:T(8,128)(2,1)} %get-tuple-element.116), channel_id=1, source_target_pairs={{0,4},{4,0},{1,5},{5,1},{2,6},{6,2},{3,7},{7,3},{8,12},{12,8},{9,1... | collective-permute-start | bytes 248840 | tf_op jit(solution)/shard_map/ppermute | solution.py:24
  20.4 29.9 %collective-permute-start.8 = (bf16[72,576]{1,0:T(8,128)(2,1)S(1)}, bf16[72,576]{1,0:T(8,128)(2,1)}, u32[]{:S(2)}, u32[]{:S(2)}) collective-permute-start(bf16[72,576]{1,0:T(8,128)(2,1)S(1)} %get-tuple-element.115), channel_id=1, source_target_pairs={{0,2},{2,0},{1,3},{3,1},{4,6},{6,4},{5,7},{7,5},{8,10},{10,8},{9,1... | collective-permute-start | bytes 248840 | tf_op jit(solution)/shard_map/ppermute | solution.py:24
  38.4 57.5 %collective-permute-start.15 = (bf16[128,1152]{1,0:T(8,128)(2,1)}, bf16[128,1152]{1,0:T(8,128)(2,1)}, u32[]{:S(2)}, u32[]{:S(2)}) collective-permute-start(bf16[128,1152]{1,0:T(8,128)(2,1)} %pad_maximum_fusion.15), channel_id=1, source_target_pairs={{0,4},{4,0},{1,5},{5,1},{2,6},{6,2},{3,7},{7,3},{8,12},{12,8},{9,1... | collective-permute-start | bytes 884744 | tf_op jit(solution)/shard_map/ppermute | solution.py:24
  42.8 11.8 %all-to-all-start = ((f32[16,1,432]{2,1,0:T(1,128)}), f32[16,1,432]{2,1,0:T(1,128)S(1)}, u32[]{:S(2)}, u32[]{:S(2)}) async-start(f32[16,1,432]{2,1,0:T(1,128)} %copy.95), calls=%async_computation | async-start | bytes 65536 | tf_op jit(solution)/shard_map/all_to_all | solution.py:366
  47.9 41.1 %all-gather.3.cloned.1.call-start = ((), (), s32[]{:S(2)}) async-start(), calls=%async_computation.4 | async-start | bytes 1843200 | tf_op jit(solution)/shard_map/all_gather | solution.py:347
  48.2 11.1 %collective-permute-start.23 = (bf16[72,1152]{1,0:T(8,128)(2,1)S(1)}, bf16[72,1152]{1,0:T(8,128)(2,1)S(1)}, u32[]{:S(2)}, u32[]{:S(2)}) collective-permute-start(bf16[72,1152]{1,0:T(8,128)(2,1)S(1)} %bitcast.174), channel_id=1, source_target_pairs={{0,6},{2,4},{4,2},{6,0},{1,7},{3,5},{5,3},{7,1},{8,14},{10,12},{12... | collective-permute-start | bytes 497672 | tf_op jit(solution)/shard_map/ppermute | solution.py:24
  49.9 10.2 %collective-permute-start.22 = (bf16[72,1152]{1,0:T(8,128)(2,1)}, bf16[72,1152]{1,0:T(8,128)(2,1)S(1)}, u32[]{:S(2)}, u32[]{:S(2)}) collective-permute-start(bf16[72,1152]{1,0:T(8,128)(2,1)} %bitcast.144), channel_id=1, source_target_pairs={{0,4},{4,0},{1,5},{5,1},{2,6},{6,2},{3,7},{7,3},{8,12},{12,8},{9,1... | collective-permute-start | bytes 497672 | tf_op jit(solution)/shard_map/ppermute | solution.py:24
  52.3 97.7 %all-gather.5.cloned.1.call-start = ((), (), s32[]{:S(2)}) async-start(), calls=%async_computation.5 | async-start | bytes 3317760 | tf_op jit(solution)/shard_map/all_gather | solution.py:348
  95.6 181.7 %reduce-scatter.3.cloned.1.call-start = ((), (), s32[]{:S(2)}) async-start(), calls=%async_computation.6 | async-start | bytes 3317760 | tf_op jit(solution)/shard_map/reduce_scatter | solution.py:407
  98.3 7.6 %collective-permute-start.14 = (bf16[64,1152]{1,0:T(8,128)(2,1)S(1)}, bf16[64,1152]{1,0:T(8,128)(2,1)S(1)}, u32[]{:S(2)}, u32[]{:S(2)}) collective-permute-start(bf16[64,1152]{1,0:T(8,128)(2,1)S(1)} %get-tuple-element.112), channel_id=1, source_target_pairs={{0,5},{1,4},{4,1},{5,0},{2,7},{3,6},{6,3},{7,2},{8,13},{9,12},{12,... | collective-permute-start | bytes 442376 | tf_op jit(solution)/shard_map/ppermute | solution.py:24
  100.7 7.9 %collective-permute-start.13 = (bf16[64,1152]{1,0:T(8,128)(2,1)S(1)}, bf16[64,1152]{1,0:T(8,128)(2,1)S(1)}, u32[]{:S(2)}, u32[]{:S(2)}) collective-permute-start(bf16[64,1152]{1,0:T(8,128)(2,1)S(1)} %get-tuple-element.113), channel_id=1, source_target_pairs={{0,4},{4,0},{1,5},{5,1},{2,6},{6,2},{3,7},{7,3},{8,12},{12,8},{9,1... | collective-permute-start | bytes 442376 | tf_op jit(solution)/shard_map/ppermute | solution.py:24
  101.3 7.4 %collective-permute-start.12 = (bf16[64,1152]{1,0:T(8,128)(2,1)S(1)}, bf16[64,1152]{1,0:T(8,128)(2,1)S(1)}, u32[]{:S(2)}, u32[]{:S(2)}) collective-permute-start(bf16[64,1152]{1,0:T(8,128)(2,1)S(1)} %get-tuple-element.111), channel_id=1, source_target_pairs={{0,1},{1,0},{2,3},{3,2},{4,5},{5,4},{6,7},{7,6},{8,9},{9,8},{10,11... | collective-permute-start | bytes 442376 | tf_op jit(solution)/shard_map/ppermute | solution.py:24
  114.0 7.5 %collective-permute-start.19 = (bf16[64,1152]{1,0:T(8,128)(2,1)}, bf16[64,1152]{1,0:T(8,128)(2,1)S(1)}, u32[]{:S(2)}, u32[]{:S(2)}) collective-permute-start(bf16[64,1152]{1,0:T(8,128)(2,1)} %shard_map.230), channel_id=1, source_target_pairs={{0,5},{1,4},{4,1},{5,0},{2,7},{3,6},{6,3},{7,2},{8,13},{9,12},{12,... | collective-permute-start | bytes 442376 | tf_op jit(solution)/shard_map/ppermute | solution.py:24
  160.6 7.7 %collective-permute-start.27 = (bf16[64,1152]{1,0:T(8,128)(2,1)S(1)}, bf16[64,1152]{1,0:T(8,128)(2,1)S(1)}, u32[]{:S(2)}, u32[]{:S(2)}) collective-permute-start(bf16[64,1152]{1,0:T(8,128)(2,1)S(1)} %get-tuple-element.109), channel_id=1, source_target_pairs={{0,5},{1,4},{4,1},{5,0},{2,7},{3,6},{6,3},{7,2},{8,13},{9,12},{12,... | collective-permute-start | bytes 442376 | tf_op jit(solution)/shard_map/ppermute | solution.py:24
  163.1 7.6 %collective-permute-start.26 = (bf16[64,1152]{1,0:T(8,128)(2,1)S(1)}, bf16[64,1152]{1,0:T(8,128)(2,1)S(1)}, u32[]{:S(2)}, u32[]{:S(2)}) collective-permute-start(bf16[64,1152]{1,0:T(8,128)(2,1)S(1)} %get-tuple-element.110), channel_id=1, source_target_pairs={{0,4},{4,0},{1,5},{5,1},{2,6},{6,2},{3,7},{7,3},{8,12},{12,8},{9,1... | collective-permute-start | bytes 442376 | tf_op jit(solution)/shard_map/ppermute | solution.py:24
  180.1 33.4 %collective-permute-start.28 = (bf16[256,1152]{1,0:T(8,128)(2,1)}, bf16[256,1152]{1,0:T(8,128)(2,1)}, u32[]{:S(2)}, u32[]{:S(2)}) collective-permute-start(bf16[256,1152]{1,0:T(8,128)(2,1)} %shard_map.232), channel_id=1, source_target_pairs={{0,2},{2,0},{1,3},{3,1},{4,6},{6,4},{5,7},{7,5},{8,10},{10,8},{9,1... | collective-permute-start | bytes 1769480 | tf_op jit(solution)/shard_map/ppermute | solution.py:24
  217.9 16.1 %collective-permute-start.31 = (bf16[64,1152]{1,0:T(8,128)(2,1)}, bf16[64,1152]{1,0:T(8,128)(2,1)}, u32[]{:S(2)}, u32[]{:S(2)}) collective-permute-start(bf16[64,1152]{1,0:T(8,128)(2,1)} %get-tuple-element.106), channel_id=1, source_target_pairs={{0,5},{1,4},{4,1},{5,0},{2,7},{3,6},{6,3},{7,2},{8,13},{9,12},{12,... | collective-permute-start | bytes 442376 | tf_op jit(solution)/shard_map/ppermute | solution.py:24
  220.4 15.5 %collective-permute-start.30 = (bf16[64,1152]{1,0:T(8,128)(2,1)}, bf16[64,1152]{1,0:T(8,128)(2,1)}, u32[]{:S(2)}, u32[]{:S(2)}) collective-permute-start(bf16[64,1152]{1,0:T(8,128)(2,1)} %get-tuple-element.107), channel_id=1, source_target_pairs={{0,4},{4,0},{1,5},{5,1},{2,6},{6,2},{3,7},{7,3},{8,12},{12,8},{9,1... | collective-permute-start | bytes 442376 | tf_op jit(solution)/shard_map/ppermute | solution.py:24
  221.0 15.0 %collective-permute-start.29 = (bf16[64,1152]{1,0:T(8,128)(2,1)}, bf16[64,1152]{1,0:T(8,128)(2,1)}, u32[]{:S(2)}, u32[]{:S(2)}) collective-permute-start(bf16[64,1152]{1,0:T(8,128)(2,1)} %get-tuple-element.105), channel_id=1, source_target_pairs={{0,1},{1,0},{2,3},{3,2},{4,5},{5,4},{6,7},{7,6},{8,9},{9,8},{10,11... | collective-permute-start | bytes 442376 | tf_op jit(solution)/shard_map/ppermute | solution.py:24
  221.4 7.6 %collective-permute-start.37 = (bf16[256,1152]{1,0:T(8,128)(2,1)S(1)}, bf16[256,1152]{1,0:T(8,128)(2,1)S(1)}, u32[]{:S(2)}, u32[]{:S(2)}) collective-permute-start(bf16[256,1152]{1,0:T(8,128)(2,1)S(1)} %copy-done.15), channel_id=1, source_target_pairs={{0,2},{2,0},{1,3},{3,1},{4,6},{6,4},{5,7},{7,5},{8,10},{10,8},{9,1... | collective-permute-start | bytes 1769480 | tf_op jit(solution)/shard_map/ppermute | solution.py:24
  221.4 7.4 %collective-permute-start.53 = (f32[2,864]{1,0:T(2,128)S(1)}, f32[2,864]{1,0:T(2,128)S(1)}, u32[]{:S(2)}, u32[]{:S(2)}) collective-permute-start(f32[2,864]{1,0:T(2,128)S(1)} %pad_maximum_fusion.27), channel_id=1, source_target_pairs={{0,4},{4,0},{1,5},{5,1},{2,6},{6,2},{3,7},{7,3},{8,12},{12,8},{9,1... | collective-permute-start | bytes 20744 | tf_op jit(solution)/shard_map/ppermute | solution.py:24
  232.1 7.7 %collective-permute-start.40 = (bf16[64,1152]{1,0:T(8,128)(2,1)S(1)}, bf16[64,1152]{1,0:T(8,128)(2,1)S(1)}, u32[]{:S(2)}, u32[]{:S(2)}) collective-permute-start(bf16[64,1152]{1,0:T(8,128)(2,1)S(1)} %get-tuple-element.103), channel_id=1, source_target_pairs={{0,5},{1,4},{4,1},{5,0},{2,7},{3,6},{6,3},{7,2},{8,13},{9,12},{12,... | collective-permute-start | bytes 442376 | tf_op jit(solution)/shard_map/ppermute | solution.py:24
  234.0 7.8 %collective-permute-start.38 = (bf16[64,1152]{1,0:T(8,128)(2,1)S(1)}, bf16[64,1152]{1,0:T(8,128)(2,1)S(1)}, u32[]{:S(2)}, u32[]{:S(2)}) collective-permute-start(bf16[64,1152]{1,0:T(8,128)(2,1)S(1)} %get-tuple-element.102), channel_id=1, source_target_pairs={{0,1},{1,0},{2,3},{3,2},{4,5},{5,4},{6,7},{7,6},{8,9},{9,8},{10,11... | collective-permute-start | bytes 442376 | tf_op jit(solution)/shard_map/ppermute | solution.py:24
  245.7 34.7 %collective-permute-start.32 = (bf16[64,1152]{1,0:T(8,128)(2,1)S(1)}, bf16[64,1152]{1,0:T(8,128)(2,1)S(1)}, u32[]{:S(2)}, u32[]{:S(2)}) collective-permute-start(bf16[64,1152]{1,0:T(8,128)(2,1)S(1)} %get-tuple-element.163), channel_id=1, source_target_pairs={{0,1},{1,0},{2,3},{3,2},{4,5},{5,4},{6,7},{7,6},{8,9},{9,8},{10,11... | collective-permute-start | bytes 442376 | tf_op jit(solution)/shard_map/ppermute | solution.py:24
  249.8 11.3 %all-to-all-start.1 = ((bf16[16,2,216]{2,1,0:T(2,128)(2,1)}), bf16[16,2,216]{2,1,0:T(2,128)(2,1)S(1)}, u32[]{:S(2)}, u32[]{:S(2)}) async-start(bf16[16,2,216]{2,1,0:T(2,128)(2,1)} %reshape.417), calls=%async_computation.1 | async-start | bytes 32768 | tf_op jit(solution)/shard_map/all_to_all | solution.py:450
  254.3 54.8 %reduce-scatter.5.cloned.1.call-start = ((), (), s32[]{:S(2)}) async-start(), calls=%async_computation.7 | async-start | bytes 1843200 | tf_op jit(solution)/shard_map/reduce_scatter | solution.py:427
  267.5 9.0 %collective-permute-start.41 = (bf16[64,1152]{1,0:T(8,128)(2,1)S(1)}, bf16[64,1152]{1,0:T(8,128)(2,1)S(1)}, u32[]{:S(2)}, u32[]{:S(2)}) collective-permute-start(bf16[64,1152]{1,0:T(8,128)(2,1)S(1)} %fusion.15), channel_id=1, source_target_pairs={{0,1},{1,0},{2,3},{3,2},{4,5},{5,4},{6,7},{7,6},{8,9},{9,8},{10,11... | collective-permute-start | bytes 442376 | tf_op jit(solution)/shard_map/ppermute | solution.py:24
  278.9 9.8 %collective-permute-start.55 = (bf16[72,1152]{1,0:T(8,128)(2,1)S(1)}, bf16[72,1152]{1,0:T(8,128)(2,1)S(1)}, u32[]{:S(2)}, u32[]{:S(2)}) collective-permute-start(bf16[72,1152]{1,0:T(8,128)(2,1)S(1)} %get-tuple-element.96), channel_id=1, source_target_pairs={{0,4},{4,0},{1,5},{5,1},{2,6},{6,2},{3,7},{7,3},{8,12},{12,8},{9,1... | collective-permute-start | bytes 497672 | tf_op jit(solution)/shard_map/ppermute | solution.py:24
  280.4 8.3 %collective-permute-start.54 = (bf16[72,1152]{1,0:T(8,128)(2,1)S(1)}, bf16[72,1152]{1,0:T(8,128)(2,1)S(1)}, u32[]{:S(2)}, u32[]{:S(2)}) collective-permute-start(bf16[72,1152]{1,0:T(8,128)(2,1)S(1)} %get-tuple-element.97), channel_id=1, source_target_pairs={{0,2},{2,0},{1,3},{3,1},{4,6},{6,4},{5,7},{7,5},{8,10},{10,8},{9,1... | collective-permute-start | bytes 497672 | tf_op jit(solution)/shard_map/ppermute | solution.py:24
  (103 other events, 775.7 us)
Sparse Core Ops, SparseCore 0:
  52.5 36.5 all-gather.2
  95.8 54.2 all-gather.4
  210.0 53.2 reduce-scatter.2
  277.5 31.4 reduce-scatter.4

commit v3 on v2

v3 whole, which is shorter than its diff:
```python
import jax
import jax.numpy as jnp
from jax import lax
from jax.experimental import pallas as pl
from jax.experimental.pallas import tpu as pltpu
from jax.sharding import Mesh, PartitionSpec as P

HEAD = 72
EPSILON = 1e-06
GROUP = 4
ROOT = 0.7978845608028654
VMEM_LIMIT = 48 * 1024 * 1024

bf16 = jnp.bfloat16
f32 = jnp.float32


def product(left, right, form):
    return jnp.einsum(form, left, right, preferred_element_type=f32)


def exchange(value, axis, mask=1):
    size = lax.axis_size(axis)
    return lax.ppermute(value, axis, [(i, i ^ mask) for i in range(size)])


def reorder(value, position):
    count = value.shape[0]
    bit = 1
    while bit < count:
        parts = value.reshape((count // (2 * bit), 2, bit) + value.shape[1:])
        flip = (position // bit) % 2 == 1
        first = jnp.where(flip, parts[:, 1], parts[:, 0])
        second = jnp.where(flip, parts[:, 0], parts[:, 1])
        value = jnp.stack([first, second], axis=1).reshape(value.shape)
        bit *= 2
    return value


def after(value, *others):
    def nothing(*refs):
        pass

    return pl.pallas_call(
        nothing,
        out_shape=jax.ShapeDtypeStruct(value.shape, value.dtype),
        in_specs=[pl.BlockSpec(memory_space=pl.ANY)] * (1 + len(others)),
        out_specs=pl.BlockSpec(memory_space=pl.ANY),
        input_output_aliases={0: 0},
    )(value, *others)


def send_four(parts):
    return [
        parts[0],
        exchange(parts[1], "core"),
        exchange(parts[2], "xx"),
        exchange(parts[3], ("xx", "core"), 3),
    ]


def send_zz(parts):
    return [parts[0]] + [exchange(parts[m], "zz", m) for m in range(1, len(parts))]


def gather_dp(value):
    four = jnp.concatenate(send_four([value] * GROUP), axis=0)
    return jnp.concatenate(send_zz([four] * lax.axis_size("zz")), axis=0)


def scatter_dp(value, *others):
    steps = lax.axis_size("zz")
    four = sum(send_zz([value[m * GROUP : (m + 1) * GROUP] for m in range(steps)]))
    four = after(four, *others)
    return sum(send_four([four[d : d + 1] for d in range(GROUP)]))


def gather_four(value):
    near = jnp.concatenate([value, exchange(value, "xx")], axis=0)
    return near, exchange(near, "core")


def gather_eight(value, *others):
    parts = send_plane([value] * 4)

    def kernel(*refs):
        rows = value.shape[0]
        for i in range(4):
            refs[4][i * rows : (i + 1) * rows, :] = refs[i][...]

    near = call(kernel, [((4 * value.shape[0], value.shape[1]), bf16)], parts)[0]
    if others:
        near = after(near, *others)
    return near, exchange(near, "core")


def send_plane(parts):
    return [
        parts[0],
        exchange(parts[1], "tensor"),
        exchange(parts[2], "xx"),
        exchange(parts[3], ("xx", "tensor"), 3),
    ]


def scatter_eight(keep, send):
    rows = keep.shape[0] // 4
    shape = (rows, keep.shape[1])

    def kernel(a, b, own, *sent):
        own[...] = a[:rows, :] + b[:rows, :].astype(f32)
        for i in range(1, 4):
            part = slice(i * rows, (i + 1) * rows)
            sent[i - 1][...] = (a[part, :] + b[part, :].astype(f32)).astype(bf16)

    got = exchange(send, "core")
    return send_plane(call(kernel, [(shape, f32)] + [(shape, bf16)] * 3, (keep, got)))


def total_of(refs):
    own, one, two, three = [ref[...].astype(f32) for ref in refs]
    return (own + one) + (two + three)


def norm(values):
    mean = jnp.mean(values, axis=-1, keepdims=True)
    centered = values - mean
    variance = jnp.mean(centered * centered, axis=-1, keepdims=True)
    inverse = lax.rsqrt(variance + EPSILON)
    return centered * inverse, inverse


def norm_back(grad, normed, inverse, scale):
    scaled = grad * (1.0 + scale)
    mean_scaled = jnp.mean(scaled, axis=-1, keepdims=True)
    mean_product = jnp.mean(scaled * normed, axis=-1, keepdims=True)
    return inverse * (scaled - mean_scaled - normed * mean_product)


def transposed_dot(left, right):
    return lax.dot_general(left, right, (((0,), (0,)), ((), ())), preferred_element_type=f32)


def dot_rows(left, right):
    return lax.dot_general(left, right, (((1,), (1,)), ((), ())), preferred_element_type=f32)


def dot(left, right):
    return lax.dot_general(left, right, (((1,), (0,)), ((), ())), preferred_element_type=f32)


def call(kernel, outs, args, flops=0):
    return pl.pallas_call(
        kernel,
        out_shape=[jax.ShapeDtypeStruct(shape, dtype) for shape, dtype in outs],
        in_specs=[pl.BlockSpec(memory_space=pltpu.VMEM)] * len(args),
        out_specs=[pl.BlockSpec(memory_space=pltpu.VMEM)] * len(outs),
        compiler_params=pltpu.CompilerParams(vmem_limit_bytes=VMEM_LIMIT),
        cost_estimate=pl.CostEstimate(flops=flops, bytes_accessed=0, transcendentals=0),
    )(*args)


def place_call(kernel, outs, args, place, *scratch):
    return pl.pallas_call(
        kernel,
        out_shape=[jax.ShapeDtypeStruct(shape, dtype) for shape, dtype in outs],
        in_specs=[pl.BlockSpec(memory_space=pltpu.SMEM)]
        + [pl.BlockSpec(memory_space=pltpu.VMEM)] * len(args),
        out_specs=[pl.BlockSpec(memory_space=pltpu.VMEM)] * len(outs),
        scratch_shapes=scratch,
        compiler_params=pltpu.CompilerParams(vmem_limit_bytes=VMEM_LIMIT),
        cost_estimate=pl.CostEstimate(flops=0, bytes_accessed=0, transcendentals=0),
    )(place.reshape(1), *args)


def pack(arrays, place):
    rows, width = arrays[0].shape[-2], arrays[0].shape[-1] // GROUP
    counts = [1 if value.ndim == 2 else value.shape[0] for value in arrays]
    total = sum(counts)

    def kernel(at, *refs):
        chunks = refs[-1]
        i = 0
        for ref, count in zip(refs, counts):
            for j in range(count):
                for s in range(GROUP):
                    columns = slice(s * width, (s + 1) * width)
                    value = ref[:, columns] if len(ref.shape) == 2 else ref[j, :, columns]
                    chunks[s, :, i * width : (i + 1) * width] = value
                i += 1
        for d in range(GROUP):
            refs[len(arrays) + d][...] = chunks[at[0] ^ d]

    shape = (rows, total * width)
    return place_call(
        kernel,
        [(shape, bf16)] * GROUP,
        arrays,
        place,
        pltpu.VMEM((GROUP,) + shape, bf16),
    )


def join(parts, place):
    def kernel(at, *refs):
        for d in range(GROUP):
            refs[GROUP][at[0] ^ d] = refs[d][...]

    rows, width = parts[0].shape
    joined = place_call(kernel, [((GROUP, rows, width), bf16)], parts, place)[0]
    return joined.reshape(GROUP * rows, width)


def unpack(parts, counts, place):
    rows, width = parts[0].shape
    width = width // sum(counts)

    def kernel(at, *refs):
        chunks = refs[-1]
        for d in range(GROUP):
            chunks[at[0] ^ d] = refs[d][...].astype(f32)
        i = 0
        for ref, count in zip(refs[GROUP:], counts):
            for j in range(count):
                for s in range(GROUP):
                    columns = slice(s * width, (s + 1) * width)
                    ref[j, :, columns] = chunks[s, :, i * width : (i + 1) * width]
                i += 1

    return place_call(
        kernel,
        [((count, rows, GROUP * width), f32) for count in counts],
        parts,
        place,
        pltpu.VMEM((GROUP, rows, sum(counts) * width), f32),
    )


def collect_rows(pieces, dp, width):
    steps, _, columns = pieces[0].shape

    def kernel(at, *refs):
        blocks, flat = refs[-2], refs[-1]
        for d in range(GROUP):
            for m in range(steps):
                rows = [refs[d][m, i ^ d : (i ^ d) + 1, :] for i in (0, 2, 1, 3)]
                blocks[at[0] ^ (m * GROUP + d)] = jnp.concatenate(rows, axis=0)
        for k in range(steps * GROUP):
            flat[:, k * columns : (k + 1) * columns] = blocks[k]
        for i in range(6):
            refs[GROUP + i][...] = flat[:, i * width : (i + 1) * width]

    return place_call(
        kernel,
        [((GROUP, width), f32)] * 6,
        pieces,
        dp,
        pltpu.VMEM((steps * GROUP, GROUP, columns), f32),
        pltpu.VMEM((GROUP, 6 * width), f32),
    )


def deal_columns(own, other, dp, steps):
    width = own.shape[1]
    columns = 6 * width // (steps * GROUP)

    def kernel(at, a, b, out, blocks, flat):
        for i in range(6):
            flat[:, i * width : (i + 1) * width] = a[i : i + 1, :] + b[i : i + 1, :]
        for k in range(steps * GROUP):
            blocks[k] = flat[:, k * columns : (k + 1) * columns]
        for m in range(steps):
            for d in range(GROUP):
                out[m, d : d + 1, :] = blocks[at[0] ^ (m * GROUP + d)]

    return place_call(
        kernel,
        [((steps, GROUP, columns), f32)],
        (own, other),
        dp,
        pltpu.VMEM((steps * GROUP, 1, columns), f32),
        pltpu.VMEM((1, 6 * width), f32),
    )[0]


def split_four(value, place):
    rows = value.shape[0] // GROUP
    chunks = value.reshape(GROUP, rows, value.shape[1])

    def kernel(at, *refs):
        for d in range(GROUP):
            refs[1 + d][...] = refs[0][at[0] ^ d]

    return place_call(kernel, [((rows, value.shape[1]), bf16)] * GROUP, [chunks], place)


def row_sum(value):
    return jnp.sum(value, axis=0, keepdims=True)


def first_branch(parts, bias, inputs, gate, scale, shift):
    shape = inputs.shape

    def kernel(a, b, c, d, bi, x, g, sc, sh, branch_out, hidden_out, normed_out):
        branch = total_of((a, b, c, d)) + bi[...]
        hidden = x[...].astype(f32) + g[0:1, :] * branch
        branch_out[...] = branch
        hidden_out[...] = hidden
        normed_out[...] = (norm(hidden)[0] * (1.0 + sc[0:1, :]) + sh[0:1, :]).astype(bf16)

    return call(
        kernel,
        [(shape, f32), (shape, f32), (shape, bf16)],
        (*parts, bias, inputs, gate, scale, shift),
    )


def second_backward(parts, hidden, branch, cot, scale, gate):
    shape = hidden.shape

    def kernel(a, b, c, d, h, br, g, sc, gt, hidden_out, branch_out, sums):
        grad = total_of((a, b, c, d))
        normed, inverse = norm(h[...])
        grad_hidden = g[...].astype(f32) + norm_back(grad, normed, inverse, sc[0:1, :])
        hidden_out[...] = grad_hidden
        branch_out[...] = (gt[0:1, :] * grad_hidden).astype(bf16)
        sums[0:1, :] = row_sum(grad_hidden * br[...])
        sums[1:2, :] = row_sum(grad)
        sums[2:3, :] = row_sum(grad * normed)

    return call(
        kernel,
        [(shape, f32), (shape, bf16), ((3, shape[1]), f32)],
        (*parts, hidden, branch, cot, scale, gate),
    )


def second_branch(parts, bias, hidden, gate, cot):
    shape = hidden.shape

    def kernel(a, b, c, d, bi, h, gt, g, out, gate_sum):
        branch = total_of((a, b, c, d)) + bi[...]
        out[...] = (h[...] + gt[0:1, :] * branch).astype(bf16)
        gate_sum[...] = row_sum(g[...].astype(f32) * branch)

    return call(
        kernel, [(shape, bf16), ((1, shape[1]), f32)], (*parts, bias, hidden, gate, cot)
    )


def first_backward(parts, inputs, grad_hidden, scale, sums, gate_sum):
    shape = inputs.shape

    def kernel(a, b, c, d, x, gh, sc, s, gs, out, mod):
        grad = total_of((a, b, c, d))
        normed, inverse = norm(x[...].astype(f32))
        out[...] = (gh[...] + norm_back(grad, normed, inverse, sc[0:1, :])).astype(bf16)
        mod[0:1, :] = row_sum(grad)
        mod[1:2, :] = row_sum(grad * normed)
        mod[2:5, :] = s[...]
        mod[5:6, :] = gs[...]

    return call(
        kernel,
        [(shape, bf16), ((6, shape[1]), f32)],
        (*parts, inputs, grad_hidden, scale, sums, gate_sum),
    )


def head_masks(feats):
    lane = lax.broadcasted_iota(jnp.int32, (1, feats), 1)
    return [(lane >= h * HEAD) & (lane < (h + 1) * HEAD) for h in range(feats // HEAD)]


def only(mask, value):
    return jnp.where(mask, value, jnp.zeros_like(value))


def split_store(keep_ref, send_ref, value):
    half = value.shape[0] // 2
    keep_ref[...] = value[:half]
    send_ref[...] = value[half:].astype(bf16)


def attention_forward(near, far, shift, scale, weights, biases):
    total, width = 2 * near.shape[0], near.shape[1]
    feats = biases.shape[1]
    seq = total // GROUP
    factor = HEAD ** (-0.5)

    def kernel(t_near, t_far, sh, sc, w, b, normed, q_out, k_out, v_out, att, keep, send):
        for i in range(GROUP):
            rows = slice(i * seq, (i + 1) * seq)
            tok = t_near if i < GROUP // 2 else t_far
            value = norm(tok[i % 2 * seq : (i % 2 + 1) * seq, :].astype(f32))[0]
            normed[rows, :] = (value * (1.0 + sc[i : i + 1, :]) + sh[i : i + 1, :]).astype(bf16)
        projected = dot(normed[...], w[:, : 3 * feats])
        q_out[...] = (projected[:, :feats] + b[0:1, :]).astype(bf16)
        k_out[...] = projected[:, feats : 2 * feats].astype(bf16)
        v_out[...] = (projected[:, 2 * feats :] + b[1:2, :]).astype(bf16)
        masks = head_masks(feats)
        for i in range(GROUP):
            rows = slice(i * seq, (i + 1) * seq)
            q, k, v = q_out[rows, :], k_out[rows, :], v_out[rows, :]
            result = jnp.zeros((seq, feats), f32)
            for mask in masks:
                probs = softmax(dot_rows(only(mask, q), k) * factor)
                result += dot(probs.astype(bf16), only(mask, v))
            att[rows, :] = result.astype(bf16)
        split_store(keep, send, dot_rows(att[...], w[:, 3 * feats :]))

    return call(
        kernel,
        [
            ((total, width), bf16),
            ((total, feats), bf16),
            ((total, feats), bf16),
            ((total, feats), bf16),
            ((total, feats), bf16),
            ((total // 2, width), f32),
            ((total // 2, width), bf16),
        ],
        (near, far, shift, scale, weights, biases),
    )


def softmax(scores):
    exponent = jnp.exp(scores - jnp.max(scores, axis=-1, keepdims=True))
    return exponent / jnp.sum(exponent, axis=-1, keepdims=True)


def symmetric_sum(parts):
    pairs = [parts[2 * i] + parts[2 * i + 1] for i in range(GROUP)]
    return (pairs[0] + pairs[1]) + (pairs[2] + pairs[3])


def attention_backward(near, far, q_all, k_all, v_all, weights):
    total = q_all.shape[0]
    width, feats = weights.shape[0], q_all.shape[1]
    seq = total // GROUP
    factor = HEAD ** (-0.5)

    def kernel(g_near, g_far, q_in, k_in, v_in, w, grad_in, keep, send, bias, g, proj_bias):
        masks = head_masks(feats)
        g[: total // 2, :] = g_near[...]
        g[total // 2 :, :] = g_far[...]
        half = seq // 2
        proj_bias[...] = symmetric_sum(
            [row_sum(g[i * half : (i + 1) * half, :].astype(f32)) for i in range(2 * GROUP)]
        )
        grad_att = dot(g[...], w[:, 3 * feats :]).astype(bf16)
        q_sum = jnp.zeros((1, feats), f32)
        v_sum = jnp.zeros((1, feats), f32)
        for i in range(GROUP):
            rows = slice(i * seq, (i + 1) * seq)
            q, k, v = q_in[rows, :], k_in[rows, :], v_in[rows, :]
            ga = grad_att[rows, :]
            gq = jnp.zeros((seq, feats), f32)
            gk = jnp.zeros((seq, feats), f32)
            gv = jnp.zeros((seq, feats), f32)
            for mask in masks:
                probs = softmax(dot_rows(only(mask, q), k) * factor)
                gv += only(mask, transposed_dot(probs.astype(bf16), ga))
                gp = dot_rows(only(mask, ga), v)
                gs = probs * (gp - jnp.sum(probs * gp, axis=-1, keepdims=True))
                gs = gs.astype(bf16)
                gq += only(mask, dot(gs, k))
                gk += only(mask, transposed_dot(gs, q))
            gq, gk = gq * factor, gk * factor
            q_sum += jnp.sum(gq, axis=0, keepdims=True)
            v_sum += jnp.sum(gv, axis=0, keepdims=True)
            grad_in[rows, :] = jnp.concatenate([gq, gk, gv], axis=1).astype(bf16)
        bias[0:1, :] = q_sum
        bias[1:2, :] = v_sum
        split_store(keep, send, dot_rows(grad_in[...], w[:, : 3 * feats]))

    return call(
        kernel,
        [
            ((total, 3 * feats), bf16),
            ((total // 2, width), f32),
            ((total // 2, width), bf16),
            ((2, feats), f32),
            ((total, width), bf16),
            ((1, width), f32),
        ],
        (near, far, q_all, k_all, v_all, weights),
    )


def attention_weights(grad_in, normed, grad_branch, att):
    width, feats = normed.shape[1], att.shape[1]

    def kernel(gi, n, g, a, grads):
        grads[:, : 3 * feats] = transposed_dot(n[...], gi[...]).astype(bf16)
        grads[:, 3 * feats :] = transposed_dot(g[...], a[...]).astype(bf16)

    return call(kernel, [((width, 4 * feats), bf16)], (grad_in, normed, grad_branch, att))[0]


def feed_forward(near, far, weights, bias, cot_near, cot_far, gate):
    total, width = 2 * near.shape[0], near.shape[1]
    units = weights.shape[1] // 2
    seq = total // GROUP

    def kernel(
        n_near, n_far, w, b, c_near, c_far, gt, grads, keep, send, act_out, bias_out, fc2_out, grad_out, n
    ):
        n[: total // 2, :] = n_near[...]
        n[total // 2 :, :] = n_far[...]
        sums = []
        half = seq // 2
        for i in range(2 * GROUP):
            c = c_near if i < GROUP else c_far
            value = c[i % GROUP * half : (i % GROUP + 1) * half, :].astype(f32)
            value = value * gt[i // 2 : i // 2 + 1, :]
            sums.append(row_sum(value))
            grad_out[i * half : (i + 1) * half, :] = value.astype(bf16)
        fc2_out[...] = symmetric_sum(sums)
        pre = dot(n[...], w[:, :units]) + b[...]
        inner = ROOT * (pre + 0.044715 * (pre * pre * pre))
        tanh = jnp.tanh(inner)
        act = (0.5 * pre * (1.0 + tanh)).astype(bf16)
        slope = 0.5 * (1.0 + tanh) + 0.5 * pre * (1.0 - tanh * tanh) * (
            ROOT * (1.0 + 3 * 0.044715 * (pre * pre))
        )
        grad_pre = dot(grad_out[...], w[:, units:]) * slope
        bias_out[...] = jnp.sum(grad_pre, axis=0, keepdims=True)
        grad_pre = grad_pre.astype(bf16)
        grads[:, units:] = transposed_dot(grad_out[...], act).astype(bf16)
        grads[:, :units] = transposed_dot(n[...], grad_pre).astype(bf16)
        split_store(keep, send, dot_rows(grad_pre, w[:, :units]))
        act_out[...] = act

    return call(
        kernel,
        [
            ((width, 2 * units), bf16),
            ((total // 2, width), f32),
            ((total // 2, width), bf16),
            ((total, units), bf16),
            ((1, units), f32),
            ((1, width), f32),
            ((total, width), bf16),
            ((total, width), bf16),
        ],
        (near, far, weights, bias, cot_near, cot_far, gate),
    )


def feed_forward_out(act, weights):
    total, units = act.shape
    width = weights.shape[0]

    def kernel(a, w, keep, send):
        split_store(keep, send, dot_rows(a[...], w[:, units:]))

    return call(
        kernel,
        [((total // 2, width), f32), ((total // 2, width), bf16)],
        (act, weights),
    )


def local(
    tokens,
    conditions,
    mod_weight,
    mod_bias,
    qkv_weight,
    qv_bias,
    proj_weight,
    proj_bias,
    fc1_weight,
    fc1_bias,
    fc2_weight,
    fc2_bias,
    cotangent,
):
    seq, width = tokens.shape
    rows = seq // 2
    d_rows = qkv_weight.shape[0]
    t_width = qkv_weight.shape[2]
    hidden = fc1_weight.shape[1]
    feats = t_width // GROUP
    units = hidden // GROUP
    n_dp = width // d_rows
    t = lax.axis_index("tensor")
    place = lax.axis_index("xx") * 2 + lax.axis_index("core")
    dp = lax.axis_index("zz") * GROUP + place

    attn_arrays = [qkv_weight.transpose(1, 0, 2), proj_weight.T]
    attn_part = join(send_four(pack(attn_arrays, place)), place)
    attn_full = lax.all_gather(attn_part, "zz", axis=0, tiled=True)

    cond_values = after(conditions, attn_part).astype(f32)
    silu_conds = jax.nn.silu(cond_values).astype(bf16)
    small = jnp.concatenate(
        [silu_conds, qv_bias, proj_bias[None], fc1_bias, fc2_bias[None]], axis=1
    )
    small = gather_dp(small)
    all_silu = small[:, :width]
    spots = jnp.arange(n_dp)
    order = ((spots[:, None] ^ dp) == spots[None]).astype(bf16)
    biases = product(order, small[:, width:], "ij,jc->ic")
    n_qv, n_b, n_f = qv_bias.shape[1], proj_bias.shape[0], fc1_bias.shape[1]
    cuts = [n_qv, n_qv + n_b, n_qv + n_b + n_f]
    qv_full = biases[:, : cuts[0]].reshape(2, GROUP, feats)
    proj_bias_full = biases[:, cuts[0] : cuts[1]].reshape(width)
    fc1_bias_full = biases[:, cuts[1] : cuts[2]].reshape(GROUP, units)
    fc2_bias_full = biases[:, cuts[2] :].reshape(width)
    qv_here = lax.dynamic_index_in_dim(qv_full, place, 1, keepdims=False)
    fc1_bias_here = lax.dynamic_index_in_dim(fc1_bias_full, place, 0, keepdims=False)
    mod_columns = product(all_silu, mod_weight, "ld,dc->lc") + mod_bias.astype(f32)
    n_zz = n_dp // GROUP
    mod_parts = send_zz([mod_columns[m * GROUP : (m + 1) * GROUP] for m in range(n_zz)])
    mod_parts = after(jnp.stack(mod_parts), attn_full)
    mod_parts = send_four([mod_parts] * GROUP)
    modulation = collect_rows(mod_parts, dp, width)
    shift_attn, scale_attn, gate_attn, shift_mlp, scale_mlp, gate_mlp = modulation
    mlp_arrays = [after(fc1_weight, mod_columns), fc2_weight.T]
    mlp_part = join(send_four(pack(mlp_arrays, place)), place)
    mlp_full = lax.all_gather(mlp_part, "zz", axis=0, tiled=True)
    def own_order(value):
        first = lax.dynamic_slice_in_dim(value, t * rows, rows, 0)
        second = lax.dynamic_slice_in_dim(value, (1 - t) * rows, rows, 0)
        return jnp.concatenate([first, second], axis=0)

    def true_order(own, other):
        return jnp.where(
            t == 0,
            jnp.concatenate([own, other], axis=0),
            jnp.concatenate([other, own], axis=0),
        )

    tokens_own = own_order(tokens)
    cot_own = own_order(after(cotangent, mod_columns))
    tokens_near, tokens_far = gather_four(tokens_own)
    cot_near, cot_far = gather_four(cot_own)
    inputs_half = tokens_own[:rows]
    grad_out_half = cot_own[:rows]

    normed_one, queries, keys, values, attended, keep, send = attention_forward(
        tokens_near, tokens_far, shift_attn, scale_attn, attn_full, qv_here
    )
    branch_half, hidden_half, normed_two_half = first_branch(
        scatter_eight(keep, send),
        proj_bias_full[None],
        inputs_half,
        gate_attn,
        scale_mlp,
        shift_mlp,
    )

    normed_two_half = after(normed_two_half, cot_far)
    near, far = gather_eight(normed_two_half, mlp_full)
    mlp_grad, keep, send, activated, fc1_bias_part, fc2_bias_part, _, _ = feed_forward(
        near, far, mlp_full, fc1_bias_here[None], cot_near, cot_far, gate_mlp
    )
    mlp_grad = lax.psum_scatter(mlp_grad, "zz", scatter_dimension=0, tiled=True)
    grad_hidden_half, grad_branch_half, mod_sums = second_backward(
        scatter_eight(keep, send), hidden_half, branch_half, grad_out_half, scale_mlp, gate_attn
    )
    near, far = gather_eight(grad_branch_half)

    grad_in, keep, send, qv_bias_part, grad_branch_all, proj_bias_part = attention_backward(
        near, far, queries, keys, values, attn_full
    )

    out_keep, out_send = feed_forward_out(after(activated, grad_branch_half), mlp_full)
    block_half, gate_sum = second_branch(
        scatter_eight(out_keep, out_send),
        fc2_bias_full[None],
        hidden_half,
        gate_mlp,
        grad_out_half,
    )

    biases = jnp.concatenate(
        [
            qv_bias_part.reshape(-1),
            fc1_bias_part[0],
            proj_bias_part[0],
            fc2_bias_part[0],
        ]
    )
    biases = sum(send_zz([after(biases, gate_sum)] * n_zz))
    own = 2 * feats + units
    group_biases = jnp.concatenate(send_four([biases[None, :own]] * GROUP), axis=0)
    group_biases = reorder(group_biases, place)
    qv_all = jnp.concatenate(
        [group_biases[:, :feats].reshape(-1), group_biases[:, feats : 2 * feats].reshape(-1)]
    )
    fc1_all = group_biases[:, 2 * feats :].reshape(-1)
    proj_all = biases[own : own + width]
    fc2_all = biases[own + width :]

    attn_grads = attention_weights(
        after(grad_in, mlp_grad, biases, group_biases),
        normed_one,
        grad_branch_all,
        attended,
    )
    attn_grad = lax.psum_scatter(attn_grads, "zz", scatter_dimension=0, tiled=True)
    tokens_grad_half, grad_mod = first_backward(
        scatter_eight(keep, after(send, attn_grads)),
        inputs_half,
        grad_hidden_half,
        scale_attn,
        mod_sums,
        gate_sum,
    )

    block_out = true_order(block_half, exchange(block_half, "tensor"))
    tokens_grad = true_order(tokens_grad_half, exchange(tokens_grad_half, "tensor")).astype(f32)
    mlp_parts = send_four(split_four(mlp_grad, place))
    fc1_weight_grad, fc2_weight_grad = unpack(mlp_parts, (1, 1), place)
    grad_mod_other = exchange(after(grad_mod, fc1_weight_grad), "tensor")
    dealt = deal_columns(grad_mod, grad_mod_other, dp, n_zz)
    dealt = jnp.stack(send_zz([dealt[m] for m in range(n_zz)]))
    attn_parts = split_four(after(attn_grad, fc1_weight_grad), place)
    dealt = jnp.stack(send_four([dealt[:, d] for d in range(GROUP)]), axis=1)
    grad_mod_columns = dealt.reshape(n_dp, dealt.shape[2]).astype(bf16)
    mod_bias_grad = jnp.sum(grad_mod_columns.astype(f32), axis=0)
    mod_weight_grad = product(all_silu, grad_mod_columns, "ld,lc->dc")
    late_columns = after(grad_mod_columns, attn_parts[0])
    grad_silu = product(late_columns, mod_weight, "lc,dc->ld")
    attn_parts = send_four(attn_parts)
    grad_silu = scatter_dp(grad_silu, *attn_parts)
    conditions_grad = jax.vjp(jax.nn.silu, cond_values)[1](grad_silu)[0]

    def piece(vector):
        size = vector.shape[0] // n_dp
        return lax.dynamic_slice_in_dim(vector, dp * size, size, 0)

    qkv_weight_grad, proj_weight_grad = unpack(attn_parts, (3, 1), place)
    qkv_weight_grad = qkv_weight_grad.transpose(1, 0, 2)
    fc1_weight_grad = fc1_weight_grad[0]
    fc2_weight_grad = fc2_weight_grad[0].T
    proj_weight_grad = proj_weight_grad[0].T
    return (
        block_out,
        tokens_grad,
        conditions_grad,
        mod_weight_grad,
        mod_bias_grad,
        qkv_weight_grad,
        piece(qv_all)[None],
        proj_weight_grad,
        piece(proj_all),
        fc1_weight_grad,
        piece(fc1_all)[None],
        fc2_weight_grad,
        piece(fc2_all),
    )


def solution(mesh):
    n_dp, n_tensor = mesh.shape["dp"], mesh.shape["tensor"]
    cut = Mesh(
        mesh.devices.reshape(n_dp // GROUP, 2, 2, n_tensor), ("zz", "xx", "core", "tensor")
    )
    dp = ("zz", "xx", "core")
    return jax.shard_map(
        local,
        mesh=cut,
        in_specs=(
            P(dp, None),
            P(dp, None),
            P(None, dp),
            P(dp),
            P(dp, None, "tensor"),
            P("tensor", dp),
            P("tensor", dp),
            P(dp),
            P(dp, "tensor"),
            P("tensor", dp),
            P("tensor", dp),
            P(dp),
            P(dp, None),
        ),
        out_specs=(
            P(dp, None),
            P(dp, None),
            P(dp, None),
            P(None, dp),
            P(dp),
            P(dp, None, "tensor"),
            P("tensor", dp),
            P("tensor", dp),
            P(dp),
            P(dp, "tensor"),
            P("tensor", dp),
            P("tensor", dp),
            P(dp),
        ),
        check_vma=False,
    )
```

time: 335 us -> 262 us (0.78); the launches traced: 328 us -> 261 us
  waiting for transfers between devices: 144 us -> 85.8 us
  other arithmetic: 45.4 us -> 8.52 us
  Pallas kernels: 22.5 us -> 33.7 us
  starting transfers between devices: 57.8 us -> 66.6 us
  local copies, waits for them, and re-layouts: 40.4 us -> 47.6 us
    all_gather x1, waiting for transfers between devices: 22.4 us -> 0.01 us  [local(): attn_full = lax.all_gather(attn_part, 'zz', axis=0, tiled=True)]
    unnamed x164 -> x179, local copies, waits for them, and re-layouts: 19 us -> 39.4 us
    reduce_scatter x1, waiting for transfers between devices: 19.8 us -> 0.01 us  [local(): lax.psum_scatter(attn_grads, 'zz', scatter_dimension=0, tiled=True)]
    ppermute x57 -> x73, starting transfers between devices: 47.4 us -> 66.2 us  [exchange(): return lax.ppermute(value, axis, [(i, i ^ mask) for i in range(size)])]
    all_gather x1, waiting for transfers between devices: 25.5 us -> 12.4 us  [local(): mlp_full = lax.all_gather(mlp_part, 'zz', axis=0, tiled=True)]
    concatenate x15 -> x4, other arithmetic: 12.8 us -> 0.15 us  [the longest x2 0.09 us: gather_four(): near = jnp.concatenate([value, exchange(value, 'xx')], axis=0)]
    all_to_all x2 -> x0, starting transfers between devices: 9.61 us -> none  [the longest x1 5.13 us: local(): lax.all_to_all(mod_columns, ('zz', 'xx', 'core'), split_axis=0, concat_ax...]
    all_to_all x2 -> x0, waiting for transfers between devices: 8.4 us -> none  [the longest x1 6.71 us: local(): lax.all_to_all(grad_mod, ('zz', 'xx', 'core'), split_axis=1, concat_axis=...]
  transfers between devices with their start and end apart: 63 -> 77, of which waited for: 37 -> 42; matrix products, arithmetic and copies ran while one was open for 19% -> 8% of each run, Pallas kernels for 4% -> 9%
where the time goes in v3:
time: 262 us; the launch traced here: 261 us
  waiting for transfers between devices  85.8 us (33%)
  starting transfers between devices  66.6 us (25%)
  local copies, waits for them, and re-layouts  47.6 us (18%)
  Pallas kernels  33.7 us (13%)
  between operations  14.6 us (6%)
  other arithmetic  8.52 us (3%)
  matrix products  3.89 us (1%)
    ppermute x73, waiting for transfers between devices, exchange(): return lax.ppermute(value, axis, [(i, i ^ mask) for i in range(size)])  73.3 us
    ppermute x73, starting transfers between devices, exchange(): return lax.ppermute(value, axis, [(i, i ^ mask) for i in range(size)])  66.2 us
    unnamed x179, local copies, waits for them, and re-layouts  39.4 us
    pallas_call x15, Pallas kernels, call(): pl.pallas_call(kernel, out_shape=[jax.ShapeDtypeStruct(shape, dtype) for...  27.1 us
    all_gather x1, waiting for transfers between devices, local(): mlp_full = lax.all_gather(mlp_part, 'zz', axis=0, tiled=True)  12.4 us
    pallas_call x10, Pallas kernels, place_call(): pl.pallas_call(kernel, out_shape=[jax.ShapeDtypeStruct(shape, dtype) for...  6.57 us
  transfers between devices with their start and end apart: 77, of which 42 were waited for; matrix products, arithmetic and copies ran while one was open for 8% of the time, Pallas kernels for 9%

profile of v3, /device:TPU:0, one launch (start us, length us, event | category | flops | bytes accessed | tf_op | source)
XLA Modules:
  0.0 260.7 jit_solution(5370582117166248427)
XLA Ops:
  12.9 2.6 collective-permute-start.3
  15.5 3.4 %collective-permute-done.3.refs_2_ = bf16[72,576]{1,0:T(8,128)(2,1)S(1)} collective-permute-done((bf16[72,576]{1,0:T(8,128)(2,1)S(1)}, bf16[72,576]{1,0:T(8,128)(2,1)S(1)}, u32[]{:S(2)}, u32[]{:S(2)}) %collective-permute-start.3) | collective-permute-done | bytes 82976 | tf_op jit(solution)/shard_map/ppermute | solution.py:24
  25.8 2.0 collective-permute-done.6
  27.9 3.7 %collective-permute-start.10 = (bf16[4,1512]{1,0:T(4,128)(2,1)S(1)}, bf16[4,1512]{1,0:T(4,128)(2,1)S(1)}, u32[]{:S(2)}, u32[]{:S(2)}) collective-permute-start(bf16[4,1512]{1,0:T(4,128)(2,1)S(1)} %pad_maximum_fusion.8), channel_id=1, source_target_pairs={{0,24},{8,16},{16,8},{24,0},{1,25},{9,17},{17,9},{25,1},{2,26},{10... | collective-permute-start | bytes 36296 | tf_op jit(solution)/shard_map/ppermute | solution.py:24
  33.6 3.0 %collective-permute-done.9 = bf16[4,1512]{1,0:T(4,128)(2,1)S(1)} collective-permute-done((bf16[4,1512]{1,0:T(4,128)(2,1)S(1)}, bf16[4,1512]{1,0:T(4,128)(2,1)S(1)}, u32[]{:S(2)}, u32[]{:S(2)}) %collective-permute-start.9) | collective-permute-done | bytes 12128 | tf_op jit(solution)/shard_map/ppermute | solution.py:24
  40.8 5.2 %collective-permute-done.27.refs_2_ = bf16[72,1152]{1,0:T(8,128)(2,1)S(1)} collective-permute-done((bf16[72,1152]{1,0:T(8,128)(2,1)S(1)}, bf16[72,1152]{1,0:T(8,128)(2,1)S(1)}, u32[]{:S(2)}, u32[]{:S(2)}) %collective-permute-start.27) | collective-permute-done | bytes 165920 | tf_op jit(solution)/shard_map/ppermute | solution.py:24
  46.0 2.6 %collective-permute-done.28.refs_3_ = bf16[72,1152]{1,0:T(8,128)(2,1)S(1)} collective-permute-done((bf16[72,1152]{1,0:T(8,128)(2,1)S(1)}, bf16[72,1152]{1,0:T(8,128)(2,1)S(1)}, u32[]{:S(2)}, u32[]{:S(2)}) %collective-permute-start.28) | collective-permute-done | bytes 165920 | tf_op jit(solution)/shard_map/ppermute | solution.py:24
  53.8 3.1 %collective-permute-start.11 = (f32[4,432]{1,0:T(4,128)}, f32[4,432]{1,0:T(4,128)}, u32[]{:S(2)}, u32[]{:S(2)}) collective-permute-start(f32[4,432]{1,0:T(4,128)} %get-tuple-element.177), channel_id=1, source_target_pairs={{0,8},{8,0},{16,24},{24,16},{1,9},{9,1},{17,25},{25,17},{2,10},{10... | collective-permute-start | bytes 20744 | tf_op jit(solution)/shard_map/ppermute | solution.py:24
  70.1 4.1 %shard_map.233 = (bf16[512,1152]{1,0:T(8,128)(2,1)S(1)}, bf16[512,144]{1,0:T(8,128)(2,1)S(1)}, bf16[512,144]{1,0:T(8,128)(2,1)S(1)}, bf16[512,144]{1,0:T(8,128)(...) custom-call(bf16[256,1152]{1,0:T(8,128)(2,1)S(1)} %pad_maximum_fusion.t_near, ...), custom_call_target="tpu_custom_call" | custom-call | tf_op jit(solution)/shard_map/pallas_call | solution.py:153
  84.1 2.3 collective-permute-done.19.c
  86.4 2.0 collective-permute-done.20.d
  92.3 2.0 collective-permute-start.25
  95.8 4.1 %collective-permute-done.25.refs_3_ = bf16[64,1152]{1,0:T(8,128)(2,1)S(1)} collective-permute-done((bf16[64,1152]{1,0:T(8,128)(2,1)}, bf16[64,1152]{1,0:T(8,128)(2,1)S(1)}, u32[]{:S(2)}, u32[]{:S(2)}) %collective-permute-start.25) | collective-permute-done | bytes 147488 | tf_op jit(solution)/shard_map/ppermute | solution.py:24
  103.2 12.4 %all-gather.5.cloned.1.call-done.refs_1_.w = bf16[1152,1152]{1,0:T(8,128)(2,1)} async-done(((bf16[288,1152]{1,0:T(8,128)(2,1)}), bf16[1152,1152]{1,0:T(8,128)(2,1)}) %all-gather.5.cloned.1.call-update) | async-done | bytes 2654224 | tf_op jit(solution)/shard_map/all_gather | solution.py:623
  115.8 2.0 collective-permute-done.29.n_far
  118.9 7.7 %shard_map.243 = (bf16[1152,1152]{1,0:T(8,128)(2,1)}, f32[256,1152]{1,0:T(8,128)S(1)}, bf16[256,1152]{1,0:T(8,128)(2,1)S(1)}, bf16[512,576]{1,0:T(8,128)(2,1)S(1...) custom-call(bf16[256,1152]{1,0:T(8,128)(2,1)S(1)} %copy-done.3, ...), custom_call_target="tpu_custom_call" | custom-call | tf_op jit(solution)/shard_map/pallas_call | solution.py:153
  130.4 1.9 collective-permute-done.30.b
  135.9 2.4 collective-permute-done.31.b
  138.3 2.3 collective-permute-done.32.c
  140.7 2.0 collective-permute-done.33.d
  143.1 2.4 collective-permute-start.41
  160.0 7.0 %shard_map.251 = (bf16[512,432]{1,0:T(8,128)(2,1)S(1)}, f32[256,1152]{1,0:T(8,128)S(1)}, bf16[256,1152]{1,0:T(8,128)(2,1)S(1)}, f32[2,144]{1,0:T(2,128)S(1)}, bf...) custom-call(bf16[256,1152]{1,0:T(8,128)(2,1)S(1)} %shard_map.250.g_near, ...), custom_call_target="tpu_custom_call" | custom-call | tf_op jit(solution)/shard_map/pallas_call | solution.py:153
  176.0 3.1 %collective-permute-start.43 = (f32[3168]{0:T(1024)}, f32[3168]{0:T(1024)S(1)}, u32[]{:S(2)}, u32[]{:S(2)}) collective-permute-start(f32[3168]{0:T(1024)} %shard_map.252), channel_id=1, source_target_pairs={{0,8},{8,0},{16,24},{24,16},{1,9},{9,1},{17,25},{25,17},{2,10},{10... | collective-permute-start | bytes 38024 | tf_op jit(solution)/shard_map/ppermute | solution.py:24
  179.2 1.9 collective-permute-done.45
  188.8 2.3 shard_map.254.refs_1_
  202.9 2.3 shard_map.259
  205.1 2.2 collective-permute-done.51.c
  207.3 3.4 %collective-permute-done.52.d = bf16[64,1152]{1,0:T(8,128)(2,1)S(1)} collective-permute-done((bf16[64,1152]{1,0:T(8,128)(2,1)}, bf16[64,1152]{1,0:T(8,128)(2,1)S(1)}, u32[]{:S(2)}, u32[]{:S(2)}) %collective-permute-start.52) | collective-permute-done | bytes 147488 | tf_op jit(solution)/shard_map/ppermute | solution.py:24
  213.5 2.4 collective-permute-done.57.b
  216.0 2.3 collective-permute-start.60
  221.8 1.9 collective-permute-done.59
  233.8 2.6 collective-permute-start.66
  (407 shorter events, 141.5 us)
Async XLA Ops:
  7.2 55.6 %all-gather.3.cloned.1.call-start = ((), (), s32[]{:S(2)}) async-start(), calls=%async_computation.2 | async-start | bytes 1843200 | tf_op jit(solution)/shard_map/all_gather | solution.py:594
  21.2 94.4 %all-gather.5.cloned.1.call-start = ((), (), s32[]{:S(2)}) async-start(), calls=%async_computation.3 | async-start | bytes 3317760 | tf_op jit(solution)/shard_map/all_gather | solution.py:623
  38.9 7.1 %collective-permute-start.27 = (bf16[72,1152]{1,0:T(8,128)(2,1)S(1)}, bf16[72,1152]{1,0:T(8,128)(2,1)S(1)}, u32[]{:S(2)}, u32[]{:S(2)}) collective-permute-start(bf16[72,1152]{1,0:T(8,128)(2,1)S(1)} %get-tuple-element.104), channel_id=1, source_target_pairs={{0,4},{4,0},{1,5},{5,1},{2,6},{6,2},{3,7},{7,3},{8,12},{12,8},{9,1... | collective-permute-start | bytes 497672 | tf_op jit(solution)/shard_map/ppermute | solution.py:24
  40.0 8.7 %collective-permute-start.28 = (bf16[72,1152]{1,0:T(8,128)(2,1)S(1)}, bf16[72,1152]{1,0:T(8,128)(2,1)S(1)}, u32[]{:S(2)}, u32[]{:S(2)}) collective-permute-start(bf16[72,1152]{1,0:T(8,128)(2,1)S(1)} %get-tuple-element.105), channel_id=1, source_target_pairs={{0,6},{2,4},{4,2},{6,0},{1,7},{3,5},{5,3},{7,1},{8,14},{10,12},{12... | collective-permute-start | bytes 497672 | tf_op jit(solution)/shard_map/ppermute | solution.py:24
  49.6 136.9 %reduce-scatter.3.cloned.1.call-start = ((), (), s32[]{:S(2)}) async-start(), calls=%async_computation.4 | async-start | bytes 3317760 | tf_op jit(solution)/shard_map/reduce_scatter | solution.py:660
  49.8 9.9 %collective-permute-start = (bf16[128,1152]{1,0:T(8,128)(2,1)S(1)}, bf16[128,1152]{1,0:T(8,128)(2,1)S(1)}, u32[]{:S(2)}, u32[]{:S(2)}) collective-permute-start(bf16[128,1152]{1,0:T(8,128)(2,1)S(1)} %pad_maximum_fusion.2), channel_id=1, source_target_pairs={{0,4},{4,0},{1,5},{5,1},{2,6},{6,2},{3,7},{7,3},{8,12},{12,8},{9,1... | collective-permute-start | bytes 884744 | tf_op jit(solution)/shard_map/ppermute | solution.py:24
  52.5 8.9 %collective-permute-start.13 = (f32[4,432]{1,0:T(4,128)}, f32[4,432]{1,0:T(4,128)}, u32[]{:S(2)}, u32[]{:S(2)}) collective-permute-start(f32[4,432]{1,0:T(4,128)} %get-tuple-element.175), channel_id=1, source_target_pairs={{0,24},{8,16},{16,8},{24,0},{1,25},{9,17},{17,9},{25,1},{2,26},{10... | collective-permute-start | bytes 20744 | tf_op jit(solution)/shard_map/ppermute | solution.py:24
  53.4 8.0 %collective-permute-start.12 = (f32[4,432]{1,0:T(4,128)}, f32[4,432]{1,0:T(4,128)}, u32[]{:S(2)}, u32[]{:S(2)}) collective-permute-start(f32[4,432]{1,0:T(4,128)} %get-tuple-element.176), channel_id=1, source_target_pairs={{0,16},{8,24},{16,0},{24,8},{1,17},{9,25},{17,1},{25,9},{2,18},{10... | collective-permute-start | bytes 20744 | tf_op jit(solution)/shard_map/ppermute | solution.py:24
  53.8 7.6 %collective-permute-start.11 = (f32[4,432]{1,0:T(4,128)}, f32[4,432]{1,0:T(4,128)}, u32[]{:S(2)}, u32[]{:S(2)}) collective-permute-start(f32[4,432]{1,0:T(4,128)} %get-tuple-element.177), channel_id=1, source_target_pairs={{0,8},{8,0},{16,24},{24,16},{1,9},{9,1},{17,25},{25,17},{2,10},{10... | collective-permute-start | bytes 20744 | tf_op jit(solution)/shard_map/ppermute | solution.py:24
  56.9 18.4 %collective-permute-start.21 = (bf16[128,1152]{1,0:T(8,128)(2,1)S(1)}, bf16[128,1152]{1,0:T(8,128)(2,1)S(1)}, u32[]{:S(2)}, u32[]{:S(2)}) collective-permute-start(bf16[128,1152]{1,0:T(8,128)(2,1)S(1)} %pad_maximum_fusion.3), channel_id=1, source_target_pairs={{0,4},{4,0},{1,5},{5,1},{2,6},{6,2},{3,7},{7,3},{8,12},{12,8},{9,1... | collective-permute-start | bytes 884744 | tf_op jit(solution)/shard_map/ppermute | solution.py:24
  59.8 10.3 %collective-permute-start.1 = (bf16[256,1152]{1,0:T(8,128)(2,1)S(1)}, bf16[256,1152]{1,0:T(8,128)(2,1)S(1)}, u32[]{:S(2)}, u32[]{:S(2)}) collective-permute-start(bf16[256,1152]{1,0:T(8,128)(2,1)S(1)} %pad_maximum_fusion.t_near), channel_id=1, source_target_pairs={{0,2},{2,0},{1,3},{3,1},{4,6},{6,4},{5,7},{7,5},{8,10},{10,8},{9,1... | collective-permute-start | bytes 1769480 | tf_op jit(solution)/shard_map/ppermute | solution.py:24
  75.4 16.1 %collective-permute-start.22 = (bf16[256,1152]{1,0:T(8,128)(2,1)S(1)}, bf16[256,1152]{1,0:T(8,128)(2,1)S(1)}, u32[]{:S(2)}, u32[]{:S(2)}) collective-permute-start(bf16[256,1152]{1,0:T(8,128)(2,1)S(1)} %pad_maximum_fusion.1.c_near), channel_id=1, source_target_pairs={{0,2},{2,0},{1,3},{3,1},{4,6},{6,4},{5,7},{7,5},{8,10},{10,8},{9,1... | collective-permute-start | bytes 1769480 | tf_op jit(solution)/shard_map/ppermute | solution.py:24
  79.6 6.7 %collective-permute-start.19 = (bf16[64,1152]{1,0:T(8,128)(2,1)S(1)}, bf16[64,1152]{1,0:T(8,128)(2,1)S(1)}, u32[]{:S(2)}, u32[]{:S(2)}) collective-permute-start(bf16[64,1152]{1,0:T(8,128)(2,1)S(1)} %get-tuple-element.96), channel_id=1, source_target_pairs={{0,4},{4,0},{1,5},{5,1},{2,6},{6,2},{3,7},{7,3},{8,12},{12,8},{9,1... | collective-permute-start | bytes 442376 | tf_op jit(solution)/shard_map/ppermute | solution.py:24
  80.8 7.6 %collective-permute-start.20 = (bf16[64,1152]{1,0:T(8,128)(2,1)}, bf16[64,1152]{1,0:T(8,128)(2,1)S(1)}, u32[]{:S(2)}, u32[]{:S(2)}) collective-permute-start(bf16[64,1152]{1,0:T(8,128)(2,1)} %get-tuple-element.97), channel_id=1, source_target_pairs={{0,5},{1,4},{4,1},{5,0},{2,7},{3,6},{6,3},{7,2},{8,13},{9,12},{12,... | collective-permute-start | bytes 442376 | tf_op jit(solution)/shard_map/ppermute | solution.py:24
  92.3 7.6 %collective-permute-start.25 = (bf16[64,1152]{1,0:T(8,128)(2,1)}, bf16[64,1152]{1,0:T(8,128)(2,1)S(1)}, u32[]{:S(2)}, u32[]{:S(2)}) collective-permute-start(bf16[64,1152]{1,0:T(8,128)(2,1)} %shard_map.237.refs_0_), channel_id=1, source_target_pairs={{0,5},{1,4},{4,1},{5,0},{2,7},{3,6},{6,3},{7,2},{8,13},{9,12},{12,... | collective-permute-start | bytes 442376 | tf_op jit(solution)/shard_map/ppermute | solution.py:24
  94.4 7.1 %collective-permute-start.24 = (bf16[64,1152]{1,0:T(8,128)(2,1)}, bf16[64,1152]{1,0:T(8,128)(2,1)S(1)}, u32[]{:S(2)}, u32[]{:S(2)}) collective-permute-start(bf16[64,1152]{1,0:T(8,128)(2,1)} %shard_map.237.refs_0_), channel_id=1, source_target_pairs={{0,4},{4,0},{1,5},{5,1},{2,6},{6,2},{3,7},{7,3},{8,12},{12,8},{9,1... | collective-permute-start | bytes 442376 | tf_op jit(solution)/shard_map/ppermute | solution.py:24
  129.2 101.6 %reduce-scatter.5.cloned.1.call-start = ((), (), s32[]{:S(2)}) async-start(), calls=%async_computation.5 | async-start | bytes 1843200 | tf_op jit(solution)/shard_map/reduce_scatter | solution.py:704
  133.9 6.7 %collective-permute-start.32 = (bf16[64,1152]{1,0:T(8,128)(2,1)S(1)}, bf16[64,1152]{1,0:T(8,128)(2,1)S(1)}, u32[]{:S(2)}, u32[]{:S(2)}) collective-permute-start(bf16[64,1152]{1,0:T(8,128)(2,1)S(1)} %get-tuple-element.112), channel_id=1, source_target_pairs={{0,4},{4,0},{1,5},{5,1},{2,6},{6,2},{3,7},{7,3},{8,12},{12,8},{9,1... | collective-permute-start | bytes 442376 | tf_op jit(solution)/shard_map/ppermute | solution.py:24
  135.4 7.3 %collective-permute-start.33 = (bf16[64,1152]{1,0:T(8,128)(2,1)S(1)}, bf16[64,1152]{1,0:T(8,128)(2,1)S(1)}, u32[]{:S(2)}, u32[]{:S(2)}) collective-permute-start(bf16[64,1152]{1,0:T(8,128)(2,1)S(1)} %get-tuple-element.113), channel_id=1, source_target_pairs={{0,5},{1,4},{4,1},{5,0},{2,7},{3,6},{6,3},{7,2},{8,13},{9,12},{12,... | collective-permute-start | bytes 442376 | tf_op jit(solution)/shard_map/ppermute | solution.py:24
  143.1 7.8 %collective-permute-start.41 = (bf16[64,1152]{1,0:T(8,128)(2,1)S(1)}, bf16[64,1152]{1,0:T(8,128)(2,1)S(1)}, u32[]{:S(2)}, u32[]{:S(2)}) collective-permute-start(bf16[64,1152]{1,0:T(8,128)(2,1)S(1)} %get-tuple-element.116.refs_1_.refs_0_), channel_id=1, source_target_pairs={{0,5},{1,4},{4,1},{5,0},{2,7},{3,6},{6,3},{7,2},{8,13},{9,12},{12,... | collective-permute-start | bytes 442376 | tf_op jit(solution)/shard_map/ppermute | solution.py:24
  154.4 17.0 %collective-permute-start.35 = (bf16[64,1152]{1,0:T(8,128)(2,1)}, bf16[64,1152]{1,0:T(8,128)(2,1)S(1)}, u32[]{:S(2)}, u32[]{:S(2)}) collective-permute-start(bf16[64,1152]{1,0:T(8,128)(2,1)} %get-tuple-element.120), channel_id=1, source_target_pairs={{0,1},{1,0},{2,3},{3,2},{4,5},{5,4},{6,7},{7,6},{8,9},{9,8},{10,11... | collective-permute-start | bytes 442376 | tf_op jit(solution)/shard_map/ppermute | solution.py:24
  155.9 15.5 %collective-permute-start.36 = (bf16[64,1152]{1,0:T(8,128)(2,1)}, bf16[64,1152]{1,0:T(8,128)(2,1)}, u32[]{:S(2)}, u32[]{:S(2)}) collective-permute-start(bf16[64,1152]{1,0:T(8,128)(2,1)} %get-tuple-element.121), channel_id=1, source_target_pairs={{0,4},{4,0},{1,5},{5,1},{2,6},{6,2},{3,7},{7,3},{8,12},{12,8},{9,1... | collective-permute-start | bytes 442376 | tf_op jit(solution)/shard_map/ppermute | solution.py:24
  157.4 14.0 %collective-permute-start.37 = (bf16[64,1152]{1,0:T(8,128)(2,1)}, bf16[64,1152]{1,0:T(8,128)(2,1)}, u32[]{:S(2)}, u32[]{:S(2)}) collective-permute-start(bf16[64,1152]{1,0:T(8,128)(2,1)} %get-tuple-element.122), channel_id=1, source_target_pairs={{0,5},{1,4},{4,1},{5,0},{2,7},{3,6},{6,3},{7,2},{8,13},{9,12},{12,... | collective-permute-start | bytes 442376 | tf_op jit(solution)/shard_map/ppermute | solution.py:24
  193.3 7.3 %collective-permute-start.55 = (bf16[72,1152]{1,0:T(8,128)(2,1)}, bf16[72,1152]{1,0:T(8,128)(2,1)S(1)}, u32[]{:S(2)}, u32[]{:S(2)}) collective-permute-start(bf16[72,1152]{1,0:T(8,128)(2,1)} %get-tuple-element.149), channel_id=1, source_target_pairs={{0,4},{4,0},{1,5},{5,1},{2,6},{6,2},{3,7},{7,3},{8,12},{12,8},{9,1... | collective-permute-start | bytes 497672 | tf_op jit(solution)/shard_map/ppermute | solution.py:24
  194.4 8.5 %collective-permute-start.56 = (bf16[72,1152]{1,0:T(8,128)(2,1)}, bf16[72,1152]{1,0:T(8,128)(2,1)}, u32[]{:S(2)}, u32[]{:S(2)}) collective-permute-start(bf16[72,1152]{1,0:T(8,128)(2,1)} %get-tuple-element.150), channel_id=1, source_target_pairs={{0,6},{2,4},{4,2},{6,0},{1,7},{3,5},{5,3},{7,1},{8,14},{10,12},{12... | collective-permute-start | bytes 497672 | tf_op jit(solution)/shard_map/ppermute | solution.py:24
  195.7 9.4 %collective-permute-start.50 = (bf16[64,1152]{1,0:T(8,128)(2,1)}, bf16[64,1152]{1,0:T(8,128)(2,1)S(1)}, u32[]{:S(2)}, u32[]{:S(2)}) collective-permute-start(bf16[64,1152]{1,0:T(8,128)(2,1)} %get-tuple-element.140), channel_id=1, source_target_pairs={{0,1},{1,0},{2,3},{3,2},{4,5},{5,4},{6,7},{7,6},{8,9},{9,8},{10,11... | collective-permute-start | bytes 442376 | tf_op jit(solution)/shard_map/ppermute | solution.py:24
  197.2 10.1 %collective-permute-start.51 = (bf16[64,1152]{1,0:T(8,128)(2,1)}, bf16[64,1152]{1,0:T(8,128)(2,1)S(1)}, u32[]{:S(2)}, u32[]{:S(2)}) collective-permute-start(bf16[64,1152]{1,0:T(8,128)(2,1)} %get-tuple-element.141), channel_id=1, source_target_pairs={{0,4},{4,0},{1,5},{5,1},{2,6},{6,2},{3,7},{7,3},{8,12},{12,8},{9,1... | collective-permute-start | bytes 442376 | tf_op jit(solution)/shard_map/ppermute | solution.py:24
  198.6 12.1 %collective-permute-start.52 = (bf16[64,1152]{1,0:T(8,128)(2,1)}, bf16[64,1152]{1,0:T(8,128)(2,1)S(1)}, u32[]{:S(2)}, u32[]{:S(2)}) collective-permute-start(bf16[64,1152]{1,0:T(8,128)(2,1)} %get-tuple-element.142), channel_id=1, source_target_pairs={{0,5},{1,4},{4,1},{5,0},{2,7},{3,6},{6,3},{7,2},{8,13},{9,12},{12,... | collective-permute-start | bytes 442376 | tf_op jit(solution)/shard_map/ppermute | solution.py:24
  200.6 36.4 %collective-permute-start.38 = (bf16[64,1152]{1,0:T(8,128)(2,1)}, bf16[64,1152]{1,0:T(8,128)(2,1)S(1)}, u32[]{:S(2)}, u32[]{:S(2)}) collective-permute-start(bf16[64,1152]{1,0:T(8,128)(2,1)} %copy-done.49), channel_id=1, source_target_pairs={{0,1},{1,0},{2,3},{3,2},{4,5},{5,4},{6,7},{7,6},{8,9},{9,8},{10,11... | collective-permute-start | bytes 442376 | tf_op jit(solution)/shard_map/ppermute | solution.py:24
  237.8 10.3 %collective-permute-start.53 = (bf16[64,1152]{1,0:T(8,128)(2,1)S(1)}, bf16[64,1152]{1,0:T(8,128)(2,1)S(1)}, u32[]{:S(2)}, u32[]{:S(2)}) collective-permute-start(bf16[64,1152]{1,0:T(8,128)(2,1)S(1)} %get-tuple-element.145), channel_id=1, source_target_pairs={{0,1},{1,0},{2,3},{3,2},{4,5},{5,4},{6,7},{7,6},{8,9},{9,8},{10,11... | collective-permute-start | bytes 442376 | tf_op jit(solution)/shard_map/ppermute | solution.py:24
  245.9 6.9 %collective-permute-start.70 = (f32[1,1152]{1,0:T(1,128)S(1)}, f32[1,1152]{1,0:T(1,128)S(1)}, u32[]{:S(2)}, u32[]{:S(2)}) collective-permute-start(f32[1,1152]{1,0:T(1,128)S(1)} %get-tuple-element.181), channel_id=1, source_target_pairs={{0,2},{2,0},{1,3},{3,1},{4,6},{6,4},{5,7},{7,5},{8,10},{10,8},{9,1... | collective-permute-start | bytes 13832 | tf_op jit(solution)/shard_map/ppermute | solution.py:24
  246.2 6.6 %collective-permute-start.72 = (f32[1,1152]{1,0:T(1,128)S(1)}, f32[1,1152]{1,0:T(1,128)S(1)}, u32[]{:S(2)}, u32[]{:S(2)}) collective-permute-start(f32[1,1152]{1,0:T(1,128)S(1)} %get-tuple-element.182), channel_id=1, source_target_pairs={{0,6},{2,4},{4,2},{6,0},{1,7},{3,5},{5,3},{7,1},{8,14},{10,12},{12... | collective-permute-start | bytes 13832 | tf_op jit(solution)/shard_map/ppermute | solution.py:24
  (130 other events, 730.7 us)
Sparse Core Ops, SparseCore 0:
  21.3 37.8 all-gather.2
  61.4 54.1 all-gather.4
  129.4 51.7 reduce-scatter.2
  191.3 33.7 reduce-scatter.4

commit v4 on v3

--- a/solution.py
+++ b/solution.py
@@ -260,27 +260,63 @@
     )
 
 
-def deal_columns(own, other, dp, steps):
+def deal_columns(own, other, biases, dp, steps):
     width = own.shape[1]
     columns = 6 * width // (steps * GROUP)
-
-    def kernel(at, a, b, out, blocks, flat):
+    extra = -(-sum(value.size for value in biases) // columns)
+
+    def kernel(at, a, b, *refs):
+        out, blocks, flat, flat_bias = refs[-4:]
         for i in range(6):
             flat[:, i * width : (i + 1) * width] = a[i : i + 1, :] + b[i : i + 1, :]
         for k in range(steps * GROUP):
             blocks[k] = flat[:, k * columns : (k + 1) * columns]
+        flat_bias[...] = jnp.zeros_like(flat_bias)
+        start = 0
+        for ref in refs[: len(biases)]:
+            for i in range(ref.shape[0]):
+                flat_bias[:, start : start + ref.shape[1]] = ref[i : i + 1, :]
+                start += ref.shape[1]
         for m in range(steps):
             for d in range(GROUP):
                 out[m, d : d + 1, :] = blocks[at[0] ^ (m * GROUP + d)]
+            for r in range(extra):
+                part = flat_bias[:, r * columns : (r + 1) * columns]
+                out[m, GROUP + r : GROUP + r + 1, :] = part
 
     return place_call(
         kernel,
-        [((steps, GROUP, columns), f32)],
-        (own, other),
+        [((steps, GROUP + extra, columns), f32)],
+        (own, other, *biases),
         dp,
         pltpu.VMEM((steps * GROUP, 1, columns), f32),
         pltpu.VMEM((1, 6 * width), f32),
+        pltpu.VMEM((1, extra * columns), f32),
     )[0]
+
+
+def deal_again(pieces, count):
+    steps = len(pieces)
+    columns = pieces[0].shape[1]
+    extra = pieces[0].shape[0] - GROUP
+
+    def kernel(*refs):
+        sums = refs[0][GROUP:, :]
+        for m in range(1, steps):
+            sums = sums + refs[m][GROUP:, :]
+        refs[-1][...] = sums
+        for d in range(GROUP):
+            out = refs[steps + d]
+            for m in range(steps):
+                out[m : m + 1, :] = refs[m][d : d + 1, :]
+            out[steps:, :] = sums[:count, :]
+
+    outs = call(
+        kernel,
+        [((steps + count, columns), f32)] * GROUP + [((extra, columns), f32)],
+        pieces,
+    )
+    return outs[:GROUP], outs[GROUP]
 
 
 def split_four(value, place):
@@ -593,12 +629,12 @@
     attn_part = join(send_four(pack(attn_arrays, place)), place)
     attn_full = lax.all_gather(attn_part, "zz", axis=0, tiled=True)
 
-    cond_values = after(conditions, attn_part).astype(f32)
+    cond_values = conditions.astype(f32)
     silu_conds = jax.nn.silu(cond_values).astype(bf16)
     small = jnp.concatenate(
         [silu_conds, qv_bias, proj_bias[None], fc1_bias, fc2_bias[None]], axis=1
     )
-    small = gather_dp(small)
+    small = gather_dp(after(small, attn_part))
     all_silu = small[:, :width]
     spots = jnp.arange(n_dp)
     order = ((spots[:, None] ^ dp) == spots[None]).astype(bf16)
@@ -618,7 +654,7 @@
     mod_parts = send_four([mod_parts] * GROUP)
     modulation = collect_rows(mod_parts, dp, width)
     shift_attn, scale_attn, gate_attn, shift_mlp, scale_mlp, gate_mlp = modulation
-    mlp_arrays = [after(fc1_weight, mod_columns), fc2_weight.T]
+    mlp_arrays = [fc1_weight, fc2_weight.T]
     mlp_part = join(send_four(pack(mlp_arrays, place)), place)
     mlp_full = lax.all_gather(mlp_part, "zz", axis=0, tiled=True)
     def own_order(value):
@@ -634,7 +670,7 @@
         )
 
     tokens_own = own_order(tokens)
-    cot_own = own_order(after(cotangent, mod_columns))
+    cot_own = after(own_order(cotangent), mod_columns)
     tokens_near, tokens_far = gather_four(tokens_own)
     cot_near, cot_far = gather_four(cot_own)
     inputs_half = tokens_own[:rows]
@@ -676,27 +712,8 @@
         grad_out_half,
     )
 
-    biases = jnp.concatenate(
-        [
-            qv_bias_part.reshape(-1),
-            fc1_bias_part[0],
-            proj_bias_part[0],
-            fc2_bias_part[0],
-        ]
-    )
-    biases = sum(send_zz([after(biases, gate_sum)] * n_zz))
-    own = 2 * feats + units
-    group_biases = jnp.concatenate(send_four([biases[None, :own]] * GROUP), axis=0)
-    group_biases = reorder(group_biases, place)
-    qv_all = jnp.concatenate(
-        [group_biases[:, :feats].reshape(-1), group_biases[:, feats : 2 * feats].reshape(-1)]
-    )
-    fc1_all = group_biases[:, 2 * feats :].reshape(-1)
-    proj_all = biases[own : own + width]
-    fc2_all = biases[own + width :]
-
     attn_grads = attention_weights(
-        after(grad_in, mlp_grad, biases, group_biases),
+        after(grad_in, mlp_grad, gate_sum),
         normed_one,
         grad_branch_all,
         attended,
@@ -716,24 +733,37 @@
     mlp_parts = send_four(split_four(mlp_grad, place))
     fc1_weight_grad, fc2_weight_grad = unpack(mlp_parts, (1, 1), place)
     grad_mod_other = exchange(after(grad_mod, fc1_weight_grad), "tensor")
-    dealt = deal_columns(grad_mod, grad_mod_other, dp, n_zz)
-    dealt = jnp.stack(send_zz([dealt[m] for m in range(n_zz)]))
+    own = 2 * feats + units
+    bias_parts = (qv_bias_part, fc1_bias_part, proj_bias_part, fc2_bias_part)
+    dealt = deal_columns(grad_mod, grad_mod_other, bias_parts, dp, n_zz)
+    own_rows = -(-own // dealt.shape[2])
+    dealt = send_zz([dealt[m] for m in range(n_zz)])
     attn_parts = split_four(after(attn_grad, fc1_weight_grad), place)
-    dealt = jnp.stack(send_four([dealt[:, d] for d in range(GROUP)]), axis=1)
-    grad_mod_columns = dealt.reshape(n_dp, dealt.shape[2]).astype(bf16)
+    dealt, biases = deal_again([after(dealt[0], attn_parts[0])] + dealt[1:], own_rows)
+    dealt = jnp.stack(send_four(dealt), axis=1)
+    grad_mod_columns = dealt[:n_zz].reshape(n_dp, dealt.shape[2]).astype(bf16)
     mod_bias_grad = jnp.sum(grad_mod_columns.astype(f32), axis=0)
     mod_weight_grad = product(all_silu, grad_mod_columns, "ld,lc->dc")
-    late_columns = after(grad_mod_columns, attn_parts[0])
-    grad_silu = product(late_columns, mod_weight, "lc,dc->ld")
+    grad_silu = product(grad_mod_columns, mod_weight, "lc,dc->ld")
     attn_parts = send_four(attn_parts)
-    grad_silu = scatter_dp(grad_silu, *attn_parts)
+    qkv_weight_grad, proj_weight_grad = unpack(attn_parts, (3, 1), place)
+    grad_silu = scatter_dp(grad_silu, proj_weight_grad)
     conditions_grad = jax.vjp(jax.nn.silu, cond_values)[1](grad_silu)[0]
+
+    biases = biases.reshape(-1)
+    group_biases = dealt[n_zz:].transpose(1, 0, 2).reshape(GROUP, -1)[:, :own]
+    group_biases = reorder(group_biases, place)
+    qv_all = jnp.concatenate(
+        [group_biases[:, :feats].reshape(-1), group_biases[:, feats : 2 * feats].reshape(-1)]
+    )
+    fc1_all = group_biases[:, 2 * feats :].reshape(-1)
+    proj_all = biases[own : own + width]
+    fc2_all = biases[own + width : own + 2 * width]
 
     def piece(vector):
         size = vector.shape[0] // n_dp
         return lax.dynamic_slice_in_dim(vector, dp * size, size, 0)
 
-    qkv_weight_grad, proj_weight_grad = unpack(attn_parts, (3, 1), place)
     qkv_weight_grad = qkv_weight_grad.transpose(1, 0, 2)
     fc1_weight_grad = fc1_weight_grad[0]
     fc2_weight_grad = fc2_weight_grad[0].T

time: 262 us -> 254 us (0.969)
  waiting for transfers between devices: 85.8 us -> 79.5 us
  starting transfers between devices: 66.6 us -> 62.8 us
    ppermute x73 -> x67, waiting for transfers between devices: 73.3 us -> 60.8 us  [exchange(): return lax.ppermute(value, axis, [(i, i ^ mask) for i in range(size)])]
    reduce_scatter x1, waiting for transfers between devices: 0.01 us -> 5.2 us  [local(): lax.psum_scatter(attn_grads, 'zz', scatter_dimension=0, tiled=True)]
    reduce_scatter x1, waiting for transfers between devices: 0.01 us -> 4.48 us  [local(): mlp_grad = lax.psum_scatter(mlp_grad, 'zz', scatter_dimension=0, tiled=True)]
    ppermute x73 -> x67, starting transfers between devices: 66.2 us -> 62.5 us  [exchange(): return lax.ppermute(value, axis, [(i, i ^ mask) for i in range(size)])]
    unnamed x179 -> x166, local copies, waits for them, and re-layouts: 39.4 us -> 35.9 us
    all_gather x1, waiting for transfers between devices: 12.4 us -> 9 us  [local(): mlp_full = lax.all_gather(mlp_part, 'zz', axis=0, tiled=True)]
    pallas_call x15 -> x16, Pallas kernels: 27.1 us -> 29.2 us  [call(): pl.pallas_call(kernel, out_shape=[jax.ShapeDtypeStruct(shape, dtype) for...]
  transfers between devices with their start and end apart: 77 -> 71, of which waited for: 42 -> 35; matrix products, arithmetic and copies ran while one was open for 8% -> 9% of each run, Pallas kernels for 9% -> 9%
where the time goes in v4:
time: 254 us; the launch traced here: 253 us
  waiting for transfers between devices  79.5 us (31%)
  starting transfers between devices  62.8 us (25%)
  local copies, waits for them, and re-layouts  46.7 us (18%)
  Pallas kernels  35.9 us (14%)
  between operations  14.6 us (6%)
  other arithmetic  9.86 us (4%)
  matrix products  3.17 us (1%)
    ppermute x67, starting transfers between devices, exchange(): return lax.ppermute(value, axis, [(i, i ^ mask) for i in range(size)])  62.5 us
    ppermute x67, waiting for transfers between devices, exchange(): return lax.ppermute(value, axis, [(i, i ^ mask) for i in range(size)])  60.8 us
    unnamed x166, local copies, waits for them, and re-layouts  35.9 us
    pallas_call x16, Pallas kernels, call(): pl.pallas_call(kernel, out_shape=[jax.ShapeDtypeStruct(shape, dtype) for...  29.2 us
    all_gather x1, waiting for transfers between devices, local(): mlp_full = lax.all_gather(mlp_part, 'zz', axis=0, tiled=True)  9 us
    pallas_call x10, Pallas kernels, place_call(): pl.pallas_call(kernel, out_shape=[jax.ShapeDtypeStruct(shape, dtype) for...  6.59 us
    reduce_scatter x1, waiting for transfers between devices, local(): lax.psum_scatter(attn_grads, 'zz', scatter_dimension=0, tiled=True)  5.2 us
  transfers between devices with their start and end apart: 71, of which 35 were waited for; matrix products, arithmetic and copies ran while one was open for 9% of the time, Pallas kernels for 9%

profile of v4, /device:TPU:0, one launch (start us, length us, event | category | flops | bytes accessed | tf_op | source)
XLA Modules:
  0.0 252.5 jit_solution(5844598945190844214)
XLA Ops:
  10.0 2.6 %collective-permute-start.3 = (bf16[72,576]{1,0:T(8,128)(2,1)S(1)}, bf16[72,576]{1,0:T(8,128)(2,1)S(1)}, u32[]{:S(2)}, u32[]{:S(2)}) collective-permute-start(bf16[72,576]{1,0:T(8,128)(2,1)S(1)} %get-tuple-element.93), channel_id=1, source_target_pairs={{0,4},{4,0},{1,5},{5,1},{2,6},{6,2},{3,7},{7,3},{8,12},{12,8},{9,1... | collective-permute-start | bytes 248840 | tf_op jit(solution)/shard_map/ppermute | solution.py:24
  12.6 3.4 %collective-permute-done.3.refs_2_ = bf16[72,576]{1,0:T(8,128)(2,1)S(1)} collective-permute-done((bf16[72,576]{1,0:T(8,128)(2,1)S(1)}, bf16[72,576]{1,0:T(8,128)(2,1)S(1)}, u32[]{:S(2)}, u32[]{:S(2)}) %collective-permute-start.3) | collective-permute-done | bytes 82976 | tf_op jit(solution)/shard_map/ppermute | solution.py:24
  20.6 5.3 %collective-permute-done.27.refs_2_ = bf16[72,1152]{1,0:T(8,128)(2,1)S(1)} collective-permute-done((bf16[72,1152]{1,0:T(8,128)(2,1)S(1)}, bf16[72,1152]{1,0:T(8,128)(2,1)S(1)}, u32[]{:S(2)}, u32[]{:S(2)}) %collective-permute-start.27) | collective-permute-done | bytes 165920 | tf_op jit(solution)/shard_map/ppermute | solution.py:24
  25.9 2.5 collective-permute-done.28.refs_3_
  34.9 3.4 %collective-permute-done.7 = bf16[1,1512]{1,0:T(2,128)(2,1)S(1)} collective-permute-done((bf16[1,1512]{1,0:T(2,128)(2,1)}, bf16[1,1512]{1,0:T(2,128)(2,1)S(1)}, u32[]{:S(2)}, u32[]{:S(2)}) %collective-permute-start.7) | collective-permute-done | bytes 3056 | tf_op jit(solution)/shard_map/ppermute | solution.py:24
  39.8 3.7 %collective-permute-start.10 = (bf16[4,1512]{1,0:T(4,128)(2,1)S(1)}, bf16[4,1512]{1,0:T(4,128)(2,1)S(1)}, u32[]{:S(2)}, u32[]{:S(2)}) collective-permute-start(bf16[4,1512]{1,0:T(4,128)(2,1)S(1)} %pad_maximum_fusion.7), channel_id=1, source_target_pairs={{0,24},{8,16},{16,8},{24,0},{1,25},{9,17},{17,9},{25,1},{2,26},{10... | collective-permute-start | bytes 36296 | tf_op jit(solution)/shard_map/ppermute | solution.py:24
  45.6 3.0 %collective-permute-done.9 = bf16[4,1512]{1,0:T(4,128)(2,1)S(1)} collective-permute-done((bf16[4,1512]{1,0:T(4,128)(2,1)S(1)}, bf16[4,1512]{1,0:T(4,128)(2,1)S(1)}, u32[]{:S(2)}, u32[]{:S(2)}) %collective-permute-start.9) | collective-permute-done | bytes 12128 | tf_op jit(solution)/shard_map/ppermute | solution.py:24
  51.2 2.5 %collective-permute-start.13 = (f32[4,432]{1,0:T(4,128)S(1)}, f32[4,432]{1,0:T(4,128)S(1)}, u32[]{:S(2)}, u32[]{:S(2)}) collective-permute-start(f32[4,432]{1,0:T(4,128)S(1)} %get-tuple-element.185), channel_id=1, source_target_pairs={{0,24},{8,16},{16,8},{24,0},{1,25},{9,17},{17,9},{25,1},{2,26},{10... | collective-permute-start | bytes 20744 | tf_op jit(solution)/shard_map/ppermute | solution.py:24
  53.7 1.9 collective-permute-start.11
  61.0 2.3 collective-permute-done.16.refs_3_
  67.3 4.1 %shard_map.233 = (bf16[512,1152]{1,0:T(8,128)(2,1)S(1)}, bf16[512,144]{1,0:T(8,128)(2,1)S(1)}, bf16[512,144]{1,0:T(8,128)(2,1)S(1)}, bf16[512,144]{1,0:T(8,128)(...) custom-call(bf16[256,1152]{1,0:T(8,128)(2,1)S(1)} %pad_maximum_fusion.t_near, ...), custom_call_target="tpu_custom_call" | custom-call | tf_op jit(solution)/shard_map/pallas_call | solution.py:153
  79.4 1.9 collective-permute-done.18.b
  81.3 2.4 collective-permute-done.19.c
  83.7 2.0 collective-permute-done.20.d
  93.1 2.4 collective-permute-start.25
  96.6 4.1 %collective-permute-done.25.refs_3_ = bf16[64,1152]{1,0:T(8,128)(2,1)S(1)} collective-permute-done((bf16[64,1152]{1,0:T(8,128)(2,1)}, bf16[64,1152]{1,0:T(8,128)(2,1)S(1)}, u32[]{:S(2)}, u32[]{:S(2)}) %collective-permute-start.25) | collective-permute-done | bytes 147488 | tf_op jit(solution)/shard_map/ppermute | solution.py:24
  104.0 9.0 %all-gather.5.cloned.1.call-done.refs_1_.w = bf16[1152,1152]{1,0:T(8,128)(2,1)} async-done(((bf16[288,1152]{1,0:T(8,128)(2,1)}), bf16[1152,1152]{1,0:T(8,128)(2,1)}) %all-gather.5.cloned.1.call-update) | async-done | bytes 2654224 | tf_op jit(solution)/shard_map/all_gather | solution.py:659
  116.4 7.8 %shard_map.242 = (bf16[1152,1152]{1,0:T(8,128)(2,1)}, f32[256,1152]{1,0:T(8,128)S(1)}, bf16[256,1152]{1,0:T(8,128)(2,1)S(1)}, bf16[512,576]{1,0:T(8,128)(2,1)S(1...) custom-call(bf16[256,1152]{1,0:T(8,128)(2,1)S(1)} %copy-done.3, ...), custom_call_target="tpu_custom_call" | custom-call | tf_op jit(solution)/shard_map/pallas_call | solution.py:153
  128.2 1.8 collective-permute-done.30.b
  133.7 2.6 %collective-permute-done.31.b = bf16[64,1152]{1,0:T(8,128)(2,1)S(1)} collective-permute-done((bf16[64,1152]{1,0:T(8,128)(2,1)S(1)}, bf16[64,1152]{1,0:T(8,128)(2,1)S(1)}, u32[]{:S(2)}, u32[]{:S(2)}) %collective-permute-start.31) | collective-permute-done | bytes 147488 | tf_op jit(solution)/shard_map/ppermute | solution.py:24
  136.3 2.0 collective-permute-done.32.c
  138.4 2.3 collective-permute-done.33.d
  142.4 2.3 collective-permute-start.41
  160.1 7.2 %shard_map.250 = (bf16[512,432]{1,0:T(8,128)(2,1)S(1)}, f32[256,1152]{1,0:T(8,128)S(1)}, bf16[256,1152]{1,0:T(8,128)(2,1)S(1)}, f32[2,144]{1,0:T(2,128)S(1)}, bf...) custom-call(bf16[256,1152]{1,0:T(8,128)(2,1)S(1)} %shard_map.249.g_near, ...), custom_call_target="tpu_custom_call" | custom-call | tf_op jit(solution)/shard_map/pallas_call | solution.py:153
  174.5 4.5 %reduce-scatter.3.cloned.1.call-done.refs_1_ = bf16[288,1152]{1,0:T(8,128)(2,1)} async-done(((bf16[1152,1152]{1,0:T(8,128)(2,1)}), bf16[288,1152]{1,0:T(8,128)(2,1)}) %reduce-scatter.3.cloned.1.call-update) | async-done | bytes 663568 | tf_op jit(solution)/shard_map/reduce_scatter | solution.py:696
  181.0 2.3 shard_map.252.refs_1_
  195.0 2.3 shard_map.257
  198.9 3.7 %collective-permute-done.46.d = bf16[64,1152]{1,0:T(8,128)(2,1)S(1)} collective-permute-done((bf16[64,1152]{1,0:T(8,128)(2,1)}, bf16[64,1152]{1,0:T(8,128)(2,1)S(1)}, u32[]{:S(2)}, u32[]{:S(2)}) %collective-permute-start.46) | collective-permute-done | bytes 147488 | tf_op jit(solution)/shard_map/ppermute | solution.py:24
  208.6 2.0 collective-permute-start.54
  210.8 2.2 collective-permute-start.52
  213.9 5.2 %reduce-scatter.5.cloned.1.call-done.refs_0_ = bf16[288,576]{1,0:T(8,128)(2,1)} async-done(((bf16[1152,576]{1,0:T(8,128)(2,1)}), bf16[288,576]{1,0:T(8,128)(2,1)}) %reduce-scatter.5.cloned.1.call-update) | async-done | bytes 331792 | tf_op jit(solution)/shard_map/reduce_scatter | solution.py:721
  233.4 2.9 %collective-permute-done.60 = f32[4,1152]{1,0:T(4,128)S(1)} collective-permute-done((f32[4,1152]{1,0:T(4,128)S(1)}, f32[4,1152]{1,0:T(4,128)S(1)}, u32[]{:S(2)}, u32[]{:S(2)}) %collective-permute-start.60) | collective-permute-done | bytes 18464 | tf_op jit(solution)/shard_map/ppermute | solution.py:24
  (374 shorter events, 130.3 us)
Async XLA Ops:
  7.2 51.7 %all-gather.3.cloned.1.call-start = ((), (), s32[]{:S(2)}) async-start(), calls=%async_computation.2 | async-start | bytes 1843200 | tf_op jit(solution)/shard_map/all_gather | solution.py:630
  18.3 94.7 %all-gather.5.cloned.1.call-start = ((), (), s32[]{:S(2)}) async-start(), calls=%async_computation.3 | async-start | bytes 3317760 | tf_op jit(solution)/shard_map/all_gather | solution.py:659
  18.8 7.1 %collective-permute-start.27 = (bf16[72,1152]{1,0:T(8,128)(2,1)S(1)}, bf16[72,1152]{1,0:T(8,128)(2,1)S(1)}, u32[]{:S(2)}, u32[]{:S(2)}) collective-permute-start(bf16[72,1152]{1,0:T(8,128)(2,1)S(1)} %get-tuple-element.109), channel_id=1, source_target_pairs={{0,4},{4,0},{1,5},{5,1},{2,6},{6,2},{3,7},{7,3},{8,12},{12,8},{9,1... | collective-permute-start | bytes 497672 | tf_op jit(solution)/shard_map/ppermute | solution.py:24
  20.5 7.8 %collective-permute-start.28 = (bf16[72,1152]{1,0:T(8,128)(2,1)S(1)}, bf16[72,1152]{1,0:T(8,128)(2,1)S(1)}, u32[]{:S(2)}, u32[]{:S(2)}) collective-permute-start(bf16[72,1152]{1,0:T(8,128)(2,1)S(1)} %get-tuple-element.110), channel_id=1, source_target_pairs={{0,6},{2,4},{4,2},{6,0},{1,7},{3,5},{5,3},{7,1},{8,14},{10,12},{12... | collective-permute-start | bytes 497672 | tf_op jit(solution)/shard_map/ppermute | solution.py:24
  29.3 149.7 %reduce-scatter.3.cloned.1.call-start = ((), (), s32[]{:S(2)}) async-start(), calls=%async_computation.4 | async-start | bytes 3317760 | tf_op jit(solution)/shard_map/reduce_scatter | solution.py:696
  29.4 27.7 %collective-permute-start = (bf16[128,1152]{1,0:T(8,128)(2,1)S(1)}, bf16[128,1152]{1,0:T(8,128)(2,1)S(1)}, u32[]{:S(2)}, u32[]{:S(2)}) collective-permute-start(bf16[128,1152]{1,0:T(8,128)(2,1)S(1)} %pad_maximum_fusion.2), channel_id=1, source_target_pairs={{0,4},{4,0},{1,5},{5,1},{2,6},{6,2},{3,7},{7,3},{8,12},{12,8},{9,1... | collective-permute-start | bytes 884744 | tf_op jit(solution)/shard_map/ppermute | solution.py:24
  51.2 7.1 %collective-permute-start.13 = (f32[4,432]{1,0:T(4,128)S(1)}, f32[4,432]{1,0:T(4,128)S(1)}, u32[]{:S(2)}, u32[]{:S(2)}) collective-permute-start(f32[4,432]{1,0:T(4,128)S(1)} %get-tuple-element.185), channel_id=1, source_target_pairs={{0,24},{8,16},{16,8},{24,0},{1,25},{9,17},{17,9},{25,1},{2,26},{10... | collective-permute-start | bytes 20744 | tf_op jit(solution)/shard_map/ppermute | solution.py:24
  55.6 16.0 %collective-permute-start.21 = (bf16[128,1152]{1,0:T(8,128)(2,1)}, bf16[128,1152]{1,0:T(8,128)(2,1)}, u32[]{:S(2)}, u32[]{:S(2)}) collective-permute-start(bf16[128,1152]{1,0:T(8,128)(2,1)} %shard_map.236), channel_id=1, source_target_pairs={{0,4},{4,0},{1,5},{5,1},{2,6},{6,2},{3,7},{7,3},{8,12},{12,8},{9,1... | collective-permute-start | bytes 884744 | tf_op jit(solution)/shard_map/ppermute | solution.py:24
  57.2 10.1 %collective-permute-start.1 = (bf16[256,1152]{1,0:T(8,128)(2,1)S(1)}, bf16[256,1152]{1,0:T(8,128)(2,1)S(1)}, u32[]{:S(2)}, u32[]{:S(2)}) collective-permute-start(bf16[256,1152]{1,0:T(8,128)(2,1)S(1)} %pad_maximum_fusion.t_near), channel_id=1, source_target_pairs={{0,2},{2,0},{1,3},{3,1},{4,6},{6,4},{5,7},{7,5},{8,10},{10,8},{9,1... | collective-permute-start | bytes 1769480 | tf_op jit(solution)/shard_map/ppermute | solution.py:24
  72.9 19.4 %collective-permute-start.22 = (bf16[256,1152]{1,0:T(8,128)(2,1)S(1)}, bf16[256,1152]{1,0:T(8,128)(2,1)S(1)}, u32[]{:S(2)}, u32[]{:S(2)}) collective-permute-start(bf16[256,1152]{1,0:T(8,128)(2,1)S(1)} %pad_maximum_fusion.1.c_near), channel_id=1, source_target_pairs={{0,2},{2,0},{1,3},{3,1},{4,6},{6,4},{5,7},{7,5},{8,10},{10,8},{9,1... | collective-permute-start | bytes 1769480 | tf_op jit(solution)/shard_map/ppermute | solution.py:24
  76.6 7.1 %collective-permute-start.19 = (bf16[64,1152]{1,0:T(8,128)(2,1)}, bf16[64,1152]{1,0:T(8,128)(2,1)}, u32[]{:S(2)}, u32[]{:S(2)}) collective-permute-start(bf16[64,1152]{1,0:T(8,128)(2,1)} %get-tuple-element.101), channel_id=1, source_target_pairs={{0,4},{4,0},{1,5},{5,1},{2,6},{6,2},{3,7},{7,3},{8,12},{12,8},{9,1... | collective-permute-start | bytes 442376 | tf_op jit(solution)/shard_map/ppermute | solution.py:24
  78.1 7.6 %collective-permute-start.20 = (bf16[64,1152]{1,0:T(8,128)(2,1)}, bf16[64,1152]{1,0:T(8,128)(2,1)}, u32[]{:S(2)}, u32[]{:S(2)}) collective-permute-start(bf16[64,1152]{1,0:T(8,128)(2,1)} %get-tuple-element.102), channel_id=1, source_target_pairs={{0,5},{1,4},{4,1},{5,0},{2,7},{3,6},{6,3},{7,2},{8,13},{9,12},{12,... | collective-permute-start | bytes 442376 | tf_op jit(solution)/shard_map/ppermute | solution.py:24
  93.1 7.6 %collective-permute-start.25 = (bf16[64,1152]{1,0:T(8,128)(2,1)}, bf16[64,1152]{1,0:T(8,128)(2,1)S(1)}, u32[]{:S(2)}, u32[]{:S(2)}) collective-permute-start(bf16[64,1152]{1,0:T(8,128)(2,1)} %shard_map.237.refs_0_), channel_id=1, source_target_pairs={{0,5},{1,4},{4,1},{5,0},{2,7},{3,6},{6,3},{7,2},{8,13},{9,12},{12,... | collective-permute-start | bytes 442376 | tf_op jit(solution)/shard_map/ppermute | solution.py:24
  127.4 91.6 %reduce-scatter.5.cloned.1.call-start = ((), (), s32[]{:S(2)}) async-start(), calls=%async_computation.5 | async-start | bytes 1843200 | tf_op jit(solution)/shard_map/reduce_scatter | solution.py:721
  131.7 6.7 %collective-permute-start.32 = (bf16[64,1152]{1,0:T(8,128)(2,1)S(1)}, bf16[64,1152]{1,0:T(8,128)(2,1)S(1)}, u32[]{:S(2)}, u32[]{:S(2)}) collective-permute-start(bf16[64,1152]{1,0:T(8,128)(2,1)S(1)} %get-tuple-element.117), channel_id=1, source_target_pairs={{0,4},{4,0},{1,5},{5,1},{2,6},{6,2},{3,7},{7,3},{8,12},{12,8},{9,1... | collective-permute-start | bytes 442376 | tf_op jit(solution)/shard_map/ppermute | solution.py:24
  133.1 7.5 %collective-permute-start.33 = (bf16[64,1152]{1,0:T(8,128)(2,1)S(1)}, bf16[64,1152]{1,0:T(8,128)(2,1)S(1)}, u32[]{:S(2)}, u32[]{:S(2)}) collective-permute-start(bf16[64,1152]{1,0:T(8,128)(2,1)S(1)} %get-tuple-element.118), channel_id=1, source_target_pairs={{0,5},{1,4},{4,1},{5,0},{2,7},{3,6},{6,3},{7,2},{8,13},{9,12},{12,... | collective-permute-start | bytes 442376 | tf_op jit(solution)/shard_map/ppermute | solution.py:24
  142.4 7.8 %collective-permute-start.41 = (bf16[64,1152]{1,0:T(8,128)(2,1)S(1)}, bf16[64,1152]{1,0:T(8,128)(2,1)S(1)}, u32[]{:S(2)}, u32[]{:S(2)}) collective-permute-start(bf16[64,1152]{1,0:T(8,128)(2,1)S(1)} %get-tuple-element.121.refs_1_.refs_0_), channel_id=1, source_target_pairs={{0,5},{1,4},{4,1},{5,0},{2,7},{3,6},{6,3},{7,2},{8,13},{9,12},{12,... | collective-permute-start | bytes 442376 | tf_op jit(solution)/shard_map/ppermute | solution.py:24
  153.0 19.1 %collective-permute-start.35 = (bf16[64,1152]{1,0:T(8,128)(2,1)}, bf16[64,1152]{1,0:T(8,128)(2,1)S(1)}, u32[]{:S(2)}, u32[]{:S(2)}) collective-permute-start(bf16[64,1152]{1,0:T(8,128)(2,1)} %get-tuple-element.125), channel_id=1, source_target_pairs={{0,1},{1,0},{2,3},{3,2},{4,5},{5,4},{6,7},{7,6},{8,9},{9,8},{10,11... | collective-permute-start | bytes 442376 | tf_op jit(solution)/shard_map/ppermute | solution.py:24
  154.5 17.7 %collective-permute-start.36 = (bf16[64,1152]{1,0:T(8,128)(2,1)}, bf16[64,1152]{1,0:T(8,128)(2,1)}, u32[]{:S(2)}, u32[]{:S(2)}) collective-permute-start(bf16[64,1152]{1,0:T(8,128)(2,1)} %get-tuple-element.126), channel_id=1, source_target_pairs={{0,4},{4,0},{1,5},{5,1},{2,6},{6,2},{3,7},{7,3},{8,12},{12,8},{9,1... | collective-permute-start | bytes 442376 | tf_op jit(solution)/shard_map/ppermute | solution.py:24
  155.9 16.2 %collective-permute-start.37 = (bf16[64,1152]{1,0:T(8,128)(2,1)}, bf16[64,1152]{1,0:T(8,128)(2,1)}, u32[]{:S(2)}, u32[]{:S(2)}) collective-permute-start(bf16[64,1152]{1,0:T(8,128)(2,1)} %get-tuple-element.127), channel_id=1, source_target_pairs={{0,5},{1,4},{4,1},{5,0},{2,7},{3,6},{6,3},{7,2},{8,13},{9,12},{12,... | collective-permute-start | bytes 442376 | tf_op jit(solution)/shard_map/ppermute | solution.py:24
  185.1 7.0 %collective-permute-start.49 = (bf16[72,1152]{1,0:T(8,128)(2,1)S(1)}, bf16[72,1152]{1,0:T(8,128)(2,1)S(1)}, u32[]{:S(2)}, u32[]{:S(2)}) collective-permute-start(bf16[72,1152]{1,0:T(8,128)(2,1)S(1)} %get-tuple-element.150), channel_id=1, source_target_pairs={{0,4},{4,0},{1,5},{5,1},{2,6},{6,2},{3,7},{7,3},{8,12},{12,8},{9,1... | collective-permute-start | bytes 497672 | tf_op jit(solution)/shard_map/ppermute | solution.py:24
  186.6 8.5 %collective-permute-start.50 = (bf16[72,1152]{1,0:T(8,128)(2,1)}, bf16[72,1152]{1,0:T(8,128)(2,1)}, u32[]{:S(2)}, u32[]{:S(2)}) collective-permute-start(bf16[72,1152]{1,0:T(8,128)(2,1)} %get-tuple-element.151), channel_id=1, source_target_pairs={{0,6},{2,4},{4,2},{6,0},{1,7},{3,5},{5,3},{7,1},{8,14},{10,12},{12... | collective-permute-start | bytes 497672 | tf_op jit(solution)/shard_map/ppermute | solution.py:24
  187.8 9.5 %collective-permute-start.44 = (bf16[64,1152]{1,0:T(8,128)(2,1)}, bf16[64,1152]{1,0:T(8,128)(2,1)S(1)}, u32[]{:S(2)}, u32[]{:S(2)}) collective-permute-start(bf16[64,1152]{1,0:T(8,128)(2,1)} %get-tuple-element.141), channel_id=1, source_target_pairs={{0,1},{1,0},{2,3},{3,2},{4,5},{5,4},{6,7},{7,6},{8,9},{9,8},{10,11... | collective-permute-start | bytes 442376 | tf_op jit(solution)/shard_map/ppermute | solution.py:24
  189.3 9.6 %collective-permute-start.45 = (bf16[64,1152]{1,0:T(8,128)(2,1)}, bf16[64,1152]{1,0:T(8,128)(2,1)S(1)}, u32[]{:S(2)}, u32[]{:S(2)}) collective-permute-start(bf16[64,1152]{1,0:T(8,128)(2,1)} %get-tuple-element.142), channel_id=1, source_target_pairs={{0,4},{4,0},{1,5},{5,1},{2,6},{6,2},{3,7},{7,3},{8,12},{12,8},{9,1... | collective-permute-start | bytes 442376 | tf_op jit(solution)/shard_map/ppermute | solution.py:24
  190.8 11.8 %collective-permute-start.46 = (bf16[64,1152]{1,0:T(8,128)(2,1)}, bf16[64,1152]{1,0:T(8,128)(2,1)S(1)}, u32[]{:S(2)}, u32[]{:S(2)}) collective-permute-start(bf16[64,1152]{1,0:T(8,128)(2,1)} %get-tuple-element.143), channel_id=1, source_target_pairs={{0,5},{1,4},{4,1},{5,0},{2,7},{3,6},{6,3},{7,2},{8,13},{9,12},{12,... | collective-permute-start | bytes 442376 | tf_op jit(solution)/shard_map/ppermute | solution.py:24
  192.2 12.0 %collective-permute-start.38 = (bf16[64,1152]{1,0:T(8,128)(2,1)}, bf16[64,1152]{1,0:T(8,128)(2,1)S(1)}, u32[]{:S(2)}, u32[]{:S(2)}) collective-permute-start(bf16[64,1152]{1,0:T(8,128)(2,1)} %get-tuple-element.128), channel_id=1, source_target_pairs={{0,1},{1,0},{2,3},{3,2},{4,5},{5,4},{6,7},{7,6},{8,9},{9,8},{10,11... | collective-permute-start | bytes 442376 | tf_op jit(solution)/shard_map/ppermute | solution.py:24
  205.9 7.1 %collective-permute-start.47 = (bf16[64,1152]{1,0:T(8,128)(2,1)S(1)}, bf16[64,1152]{1,0:T(8,128)(2,1)S(1)}, u32[]{:S(2)}, u32[]{:S(2)}) collective-permute-start(bf16[64,1152]{1,0:T(8,128)(2,1)S(1)} %get-tuple-element.146), channel_id=1, source_target_pairs={{0,1},{1,0},{2,3},{3,2},{4,5},{5,4},{6,7},{7,6},{8,9},{9,8},{10,11... | collective-permute-start | bytes 442376 | tf_op jit(solution)/shard_map/ppermute | solution.py:24
  208.6 12.1 %collective-permute-start.54 = (f32[12,432]{1,0:T(8,128)S(1)}, f32[12,432]{1,0:T(8,128)S(1)}, u32[]{:S(2)}, u32[]{:S(2)}) collective-permute-start(f32[12,432]{1,0:T(8,128)S(1)} %get-tuple-element.177), channel_id=1, source_target_pairs={{0,24},{8,16},{16,8},{24,0},{1,25},{9,17},{17,9},{25,1},{2,26},{10... | collective-permute-start | bytes 62216 | tf_op jit(solution)/shard_map/ppermute | solution.py:24
  210.6 10.1 %collective-permute-start.53 = (f32[12,432]{1,0:T(8,128)S(1)}, f32[12,432]{1,0:T(8,128)S(1)}, u32[]{:S(2)}, u32[]{:S(2)}) collective-permute-start(f32[12,432]{1,0:T(8,128)S(1)} %get-tuple-element.178), channel_id=1, source_target_pairs={{0,16},{8,24},{16,0},{24,8},{1,17},{9,25},{17,1},{25,9},{2,18},{10... | collective-permute-start | bytes 62216 | tf_op jit(solution)/shard_map/ppermute | solution.py:24
  210.8 10.0 %collective-permute-start.52 = (f32[12,432]{1,0:T(8,128)S(1)}, f32[12,432]{1,0:T(8,128)S(1)}, u32[]{:S(2)}, u32[]{:S(2)}) collective-permute-start(f32[12,432]{1,0:T(8,128)S(1)} %get-tuple-element.179), channel_id=1, source_target_pairs={{0,8},{8,0},{16,24},{24,16},{1,9},{9,1},{17,25},{25,17},{2,10},{10... | collective-permute-start | bytes 62216 | tf_op jit(solution)/shard_map/ppermute | solution.py:24
  224.8 12.8 %collective-permute-start.61 = (bf16[72,576]{1,0:T(8,128)(2,1)S(1)}, bf16[72,576]{1,0:T(8,128)(2,1)S(1)}, u32[]{:S(2)}, u32[]{:S(2)}) collective-permute-start(bf16[72,576]{1,0:T(8,128)(2,1)S(1)} %get-tuple-element.162), channel_id=1, source_target_pairs={{0,2},{2,0},{1,3},{3,1},{4,6},{6,4},{5,7},{7,5},{8,10},{10,8},{9,1... | collective-permute-start | bytes 248840 | tf_op jit(solution)/shard_map/ppermute | solution.py:24
  225.1 12.5 %collective-permute-start.62 = (bf16[72,576]{1,0:T(8,128)(2,1)S(1)}, bf16[72,576]{1,0:T(8,128)(2,1)S(1)}, u32[]{:S(2)}, u32[]{:S(2)}) collective-permute-start(bf16[72,576]{1,0:T(8,128)(2,1)S(1)} %get-tuple-element.163), channel_id=1, source_target_pairs={{0,4},{4,0},{1,5},{5,1},{2,6},{6,2},{3,7},{7,3},{8,12},{12,8},{9,1... | collective-permute-start | bytes 248840 | tf_op jit(solution)/shard_map/ppermute | solution.py:24
  (121 other events, 562.9 us)
Sparse Core Ops, SparseCore 0:
  18.4 38.2 all-gather.2
  58.9 54.0 all-gather.4
  127.6 51.3 reduce-scatter.2
  183.4 35.5 reduce-scatter.4

commit v5 on v4

--- a/solution.py
+++ b/solution.py
@@ -72,7 +72,7 @@
     steps = lax.axis_size("zz")
     four = sum(send_zz([value[m * GROUP : (m + 1) * GROUP] for m in range(steps)]))
     four = after(four, *others)
-    return sum(send_four([four[d : d + 1] for d in range(GROUP)]))
+    return sum(send_four([four[d : d + 1] for d in range(GROUP)])), four
 
 
 def gather_four(value):
@@ -689,7 +689,7 @@
     )
 
     normed_two_half = after(normed_two_half, cot_far)
-    near, far = gather_eight(normed_two_half, mlp_full)
+    near, far = gather_eight(normed_two_half)
     mlp_grad, keep, send, activated, fc1_bias_part, fc2_bias_part, _, _ = feed_forward(
         near, far, mlp_full, fc1_bias_here[None], cot_near, cot_far, gate_mlp
     )
@@ -713,11 +713,9 @@
     )
 
     attn_grads = attention_weights(
-        after(grad_in, mlp_grad, gate_sum),
-        normed_one,
-        grad_branch_all,
-        attended,
-    )
+        after(grad_in, gate_sum), normed_one, grad_branch_all, attended
+    )
+    attn_grads = after(attn_grads, mlp_grad)
     attn_grad = lax.psum_scatter(attn_grads, "zz", scatter_dimension=0, tiled=True)
     tokens_grad_half, grad_mod = first_backward(
         scatter_eight(keep, after(send, attn_grads)),
@@ -739,15 +737,16 @@
     own_rows = -(-own // dealt.shape[2])
     dealt = send_zz([dealt[m] for m in range(n_zz)])
     attn_parts = split_four(after(attn_grad, fc1_weight_grad), place)
-    dealt, biases = deal_again([after(dealt[0], attn_parts[0])] + dealt[1:], own_rows)
-    dealt = jnp.stack(send_four(dealt), axis=1)
+    dealt, biases = deal_again(dealt, own_rows)
+    dealt = send_four(dealt)
+    dealt = jnp.stack([after(dealt[0], attn_parts[0])] + dealt[1:], axis=1)
     grad_mod_columns = dealt[:n_zz].reshape(n_dp, dealt.shape[2]).astype(bf16)
     mod_bias_grad = jnp.sum(grad_mod_columns.astype(f32), axis=0)
-    mod_weight_grad = product(all_silu, grad_mod_columns, "ld,lc->dc")
     grad_silu = product(grad_mod_columns, mod_weight, "lc,dc->ld")
     attn_parts = send_four(attn_parts)
     qkv_weight_grad, proj_weight_grad = unpack(attn_parts, (3, 1), place)
-    grad_silu = scatter_dp(grad_silu, proj_weight_grad)
+    grad_silu, near_sum = scatter_dp(grad_silu, proj_weight_grad)
+    mod_weight_grad = product(all_silu, after(grad_mod_columns, near_sum), "ld,lc->dc")
     conditions_grad = jax.vjp(jax.nn.silu, cond_values)[1](grad_silu)[0]
 
     biases = biases.reshape(-1)

time: 254 us -> 245 us (0.965)
  local copies, waits for them, and re-layouts: 46.7 us -> 36.4 us
  waiting for transfers between devices: 79.5 us -> 87.2 us
  Pallas kernels: 35.9 us -> 31.2 us
    ppermute x67, waiting for transfers between devices: 60.8 us -> 69.6 us  [exchange(): return lax.ppermute(value, axis, [(i, i ^ mask) for i in range(size)])]
    unnamed x166 -> x168, local copies, waits for them, and re-layouts: 35.9 us -> 29.6 us
    all_gather x1, waiting for transfers between devices: 9 us -> 14 us  [local(): mlp_full = lax.all_gather(mlp_part, 'zz', axis=0, tiled=True)]
    reduce_scatter x1, waiting for transfers between devices: 5.2 us -> 0.39 us  [local(): lax.psum_scatter(attn_grads, 'zz', scatter_dimension=0, tiled=True)]
    pallas_call x16, Pallas kernels: 29.2 us -> 26.1 us  [call(): pl.pallas_call(kernel, out_shape=[jax.ShapeDtypeStruct(shape, dtype) for...]
  transfers between devices with their start and end apart: 71 -> 71, of which waited for: 35 -> 37; matrix products, arithmetic and copies ran while one was open for 9% -> 6% of each run, Pallas kernels for 9% -> 9%
where the time goes in v5:
time: 245 us; the launch traced here: 244 us
  waiting for transfers between devices  87.2 us (36%)
  starting transfers between devices  61.5 us (25%)
  local copies, waits for them, and re-layouts  36.4 us (15%)
  Pallas kernels  31.2 us (13%)
  between operations  14.7 us (6%)
  other arithmetic  9.16 us (4%)
  matrix products  3.89 us (2%)
    ppermute x67, waiting for transfers between devices, exchange(): return lax.ppermute(value, axis, [(i, i ^ mask) for i in range(size)])  69.6 us
    ppermute x67, starting transfers between devices, exchange(): return lax.ppermute(value, axis, [(i, i ^ mask) for i in range(size)])  61.2 us
    unnamed x168, local copies, waits for them, and re-layouts  29.6 us
    pallas_call x16, Pallas kernels, call(): pl.pallas_call(kernel, out_shape=[jax.ShapeDtypeStruct(shape, dtype) for...  26.1 us
    all_gather x1, waiting for transfers between devices, local(): mlp_full = lax.all_gather(mlp_part, 'zz', axis=0, tiled=True)  14 us
    pallas_call x10, Pallas kernels, place_call(): pl.pallas_call(kernel, out_shape=[jax.ShapeDtypeStruct(shape, dtype) for...  5.01 us
  transfers between devices with their start and end apart: 71, of which 37 were waited for; matrix products, arithmetic and copies ran while one was open for 6% of the time, Pallas kernels for 9%

profile of v5, /device:TPU:0, one launch (start us, length us, event | category | flops | bytes accessed | tf_op | source)
XLA Modules:
  0.0 244.1 jit_solution(9668692653058195772)
XLA Ops:
  10.0 2.6 %collective-permute-start.3 = (bf16[72,576]{1,0:T(8,128)(2,1)S(1)}, bf16[72,576]{1,0:T(8,128)(2,1)S(1)}, u32[]{:S(2)}, u32[]{:S(2)}) collective-permute-start(bf16[72,576]{1,0:T(8,128)(2,1)S(1)} %get-tuple-element.93), channel_id=1, source_target_pairs={{0,4},{4,0},{1,5},{5,1},{2,6},{6,2},{3,7},{7,3},{8,12},{12,8},{9,1... | collective-permute-start | bytes 248840 | tf_op jit(solution)/shard_map/ppermute | solution.py:24
  12.6 3.4 %collective-permute-done.3.refs_2_ = bf16[72,576]{1,0:T(8,128)(2,1)S(1)} collective-permute-done((bf16[72,576]{1,0:T(8,128)(2,1)S(1)}, bf16[72,576]{1,0:T(8,128)(2,1)S(1)}, u32[]{:S(2)}, u32[]{:S(2)}) %collective-permute-start.3) | collective-permute-done | bytes 82976 | tf_op jit(solution)/shard_map/ppermute | solution.py:24
  22.3 3.6 %collective-permute-done.28.refs_2_ = bf16[72,1152]{1,0:T(8,128)(2,1)S(1)} collective-permute-done((bf16[72,1152]{1,0:T(8,128)(2,1)S(1)}, bf16[72,1152]{1,0:T(8,128)(2,1)S(1)}, u32[]{:S(2)}, u32[]{:S(2)}) %collective-permute-start.28) | collective-permute-done | bytes 165920 | tf_op jit(solution)/shard_map/ppermute | solution.py:24
  25.9 2.8 %collective-permute-done.29.refs_3_ = bf16[72,1152]{1,0:T(8,128)(2,1)S(1)} collective-permute-done((bf16[72,1152]{1,0:T(8,128)(2,1)S(1)}, bf16[72,1152]{1,0:T(8,128)(2,1)S(1)}, u32[]{:S(2)}, u32[]{:S(2)}) %collective-permute-start.29) | collective-permute-done | bytes 165920 | tf_op jit(solution)/shard_map/ppermute | solution.py:24
  34.8 2.0 collective-permute-done.6
  37.5 4.1 %collective-permute-start.10 = (bf16[4,1512]{1,0:T(4,128)(2,1)S(1)}, bf16[4,1512]{1,0:T(4,128)(2,1)S(1)}, u32[]{:S(2)}, u32[]{:S(2)}) collective-permute-start(bf16[4,1512]{1,0:T(4,128)(2,1)S(1)} %pad_maximum_fusion.7), channel_id=1, source_target_pairs={{0,24},{8,16},{16,8},{24,0},{1,25},{9,17},{17,9},{25,1},{2,26},{10... | collective-permute-start | bytes 36296 | tf_op jit(solution)/shard_map/ppermute | solution.py:24
  43.5 3.1 %collective-permute-done.9 = bf16[4,1512]{1,0:T(4,128)(2,1)S(1)} collective-permute-done((bf16[4,1512]{1,0:T(4,128)(2,1)S(1)}, bf16[4,1512]{1,0:T(4,128)(2,1)S(1)}, u32[]{:S(2)}, u32[]{:S(2)}) %collective-permute-start.9) | collective-permute-done | bytes 12128 | tf_op jit(solution)/shard_map/ppermute | solution.py:24
  49.3 2.5 %collective-permute-start.13 = (f32[4,432]{1,0:T(4,128)S(1)}, f32[4,432]{1,0:T(4,128)S(1)}, u32[]{:S(2)}, u32[]{:S(2)}) collective-permute-start(f32[4,432]{1,0:T(4,128)S(1)} %get-tuple-element.185), channel_id=1, source_target_pairs={{0,24},{8,16},{16,8},{24,0},{1,25},{9,17},{17,9},{25,1},{2,26},{10... | collective-permute-start | bytes 20744 | tf_op jit(solution)/shard_map/ppermute | solution.py:24
  58.9 2.1 collective-permute-done.16.refs_3_
  63.7 4.2 %shard_map.233 = (bf16[512,1152]{1,0:T(8,128)(2,1)S(1)}, bf16[512,144]{1,0:T(8,128)(2,1)S(1)}, bf16[512,144]{1,0:T(8,128)(2,1)S(1)}, bf16[512,144]{1,0:T(8,128)(...) custom-call(bf16[256,1152]{1,0:T(8,128)(2,1)S(1)} %pad_maximum_fusion.t_near, ...), custom_call_target="tpu_custom_call" | custom-call | tf_op jit(solution)/shard_map/pallas_call | solution.py:153
  75.5 2.5 %collective-permute-done.18.b = bf16[64,1152]{1,0:T(8,128)(2,1)S(1)} collective-permute-done((bf16[64,1152]{1,0:T(8,128)(2,1)}, bf16[64,1152]{1,0:T(8,128)(2,1)S(1)}, u32[]{:S(2)}, u32[]{:S(2)}) %collective-permute-start.18) | collective-permute-done | bytes 147488 | tf_op jit(solution)/shard_map/ppermute | solution.py:24
  78.0 2.3 collective-permute-done.19.c
  80.3 2.0 collective-permute-done.20.d
  90.6 4.1 %collective-permute-done.25.refs_3_ = bf16[64,1152]{1,0:T(8,128)(2,1)S(1)} collective-permute-done((bf16[64,1152]{1,0:T(8,128)(2,1)}, bf16[64,1152]{1,0:T(8,128)(2,1)S(1)}, u32[]{:S(2)}, u32[]{:S(2)}) %collective-permute-start.25) | collective-permute-done | bytes 147488 | tf_op jit(solution)/shard_map/ppermute | solution.py:24
  99.4 14.0 %all-gather.5.cloned.1.call-done.w = bf16[1152,1152]{1,0:T(8,128)(2,1)} async-done(((bf16[288,1152]{1,0:T(8,128)(2,1)}), bf16[1152,1152]{1,0:T(8,128)(2,1)}) %all-gather.5.cloned.1.call-update) | async-done | bytes 2654224 | tf_op jit(solution)/shard_map/all_gather | solution.py:659
  113.4 7.8 %shard_map.241 = (bf16[1152,1152]{1,0:T(8,128)(2,1)}, f32[256,1152]{1,0:T(8,128)S(1)}, bf16[256,1152]{1,0:T(8,128)(2,1)S(1)}, bf16[512,576]{1,0:T(8,128)(2,1)S(1...) custom-call(bf16[256,1152]{1,0:T(8,128)(2,1)S(1)} %shard_map.238.n_near, ...), custom_call_target="tpu_custom_call" | custom-call | tf_op jit(solution)/shard_map/pallas_call | solution.py:153
  124.3 2.2 collective-permute-done.30.b
  130.2 2.4 collective-permute-done.31.b
  132.6 2.3 collective-permute-done.32.c
  134.9 2.0 collective-permute-done.33.d
  137.4 2.4 %collective-permute-start.41 = (bf16[64,1152]{1,0:T(8,128)(2,1)S(1)}, bf16[64,1152]{1,0:T(8,128)(2,1)S(1)}, u32[]{:S(2)}, u32[]{:S(2)}) collective-permute-start(bf16[64,1152]{1,0:T(8,128)(2,1)S(1)} %get-tuple-element.121.refs_1_.refs_0_), channel_id=1, source_target_pairs={{0,5},{1,4},{4,1},{5,0},{2,7},{3,6},{6,3},{7,2},{8,13},{9,12},{12,... | collective-permute-start | bytes 442376 | tf_op jit(solution)/shard_map/ppermute | solution.py:24
  155.1 7.0 %shard_map.249 = (bf16[512,432]{1,0:T(8,128)(2,1)S(1)}, f32[256,1152]{1,0:T(8,128)S(1)}, bf16[256,1152]{1,0:T(8,128)(2,1)S(1)}, f32[2,144]{1,0:T(2,128)S(1)}, bf...) custom-call(bf16[256,1152]{1,0:T(8,128)(2,1)S(1)} %shard_map.248.g_near, ...), custom_call_target="tpu_custom_call" | custom-call | tf_op jit(solution)/shard_map/pallas_call | solution.py:153
  172.4 3.2 %reduce-scatter.3.cloned.1.call-done.refs_1_ = bf16[288,1152]{1,0:T(8,128)(2,1)} async-done(((bf16[1152,1152]{1,0:T(8,128)(2,1)}), bf16[288,1152]{1,0:T(8,128)(2,1)}) %reduce-scatter.3.cloned.1.call-update) | async-done | bytes 663568 | tf_op jit(solution)/shard_map/reduce_scatter | solution.py:696
  183.9 2.6 %collective-permute-done.50.refs_3_ = bf16[72,1152]{1,0:T(8,128)(2,1)S(1)} collective-permute-done((bf16[72,1152]{1,0:T(8,128)(2,1)S(1)}, bf16[72,1152]{1,0:T(8,128)(2,1)S(1)}, u32[]{:S(2)}, u32[]{:S(2)}) %collective-permute-start.50) | collective-permute-done | bytes 165920 | tf_op jit(solution)/shard_map/ppermute | solution.py:24
  187.9 2.7 %collective-permute-done.45.c = bf16[64,1152]{1,0:T(8,128)(2,1)S(1)} collective-permute-done((bf16[64,1152]{1,0:T(8,128)(2,1)S(1)}, bf16[64,1152]{1,0:T(8,128)(2,1)S(1)}, u32[]{:S(2)}, u32[]{:S(2)}) %collective-permute-start.45) | collective-permute-done | bytes 147488 | tf_op jit(solution)/shard_map/ppermute | solution.py:24
  190.6 3.6 %collective-permute-done.46.d = bf16[64,1152]{1,0:T(8,128)(2,1)S(1)} collective-permute-done((bf16[64,1152]{1,0:T(8,128)(2,1)S(1)}, bf16[64,1152]{1,0:T(8,128)(2,1)S(1)}, u32[]{:S(2)}, u32[]{:S(2)}) %collective-permute-start.46) | collective-permute-done | bytes 147488 | tf_op jit(solution)/shard_map/ppermute | solution.py:24
  197.3 2.6 %collective-permute-done.51.b = f32[6,1152]{1,0:T(8,128)S(1)} collective-permute-done((f32[6,1152]{1,0:T(8,128)}, f32[6,1152]{1,0:T(8,128)S(1)}, u32[]{:S(2)}, u32[]{:S(2)}) %collective-permute-start.51) | collective-permute-done | bytes 27680 | tf_op jit(solution)/shard_map/ppermute | solution.py:24
  200.0 2.0 collective-permute-start.54
  202.3 2.2 collective-permute-start.52
  206.9 2.4 %collective-permute-done.53.refs_2_ = f32[12,432]{1,0:T(8,128)S(1)} collective-permute-done((f32[12,432]{1,0:T(8,128)S(1)}, f32[12,432]{1,0:T(8,128)S(1)}, u32[]{:S(2)}, u32[]{:S(2)}) %collective-permute-start.53) | collective-permute-done | bytes 20768 | tf_op jit(solution)/shard_map/ppermute | solution.py:24
  227.0 2.4 collective-permute-done.63.refs_3_
  233.7 2.5 %fusion.1 = f32[1152,432]{0,1:T(8,128)} fusion(bf16[16,432]{1,0:T(8,128)(2,1)} %shard_map.266, bf16[16,1512]{1,0:T(8,128)(2,1)S(1)} %copy-done.68), kind=kOutput, calls=%fused_computation.16 | convolution fusion | flops 15925248 | bytes 2041344 | tf_op jit(solution)/shard_map/ld,lc->dc/dot_general | solution.py:19
  (377 shorter events, 121.5 us)
Async XLA Ops:
  7.2 49.8 %all-gather.3.cloned.1.call-start = ((), (), s32[]{:S(2)}) async-start(), calls=%async_computation.2 | async-start | bytes 1843200 | tf_op jit(solution)/shard_map/all_gather | solution.py:630
  18.3 95.1 %all-gather.5.cloned.1.call-start = ((), (), s32[]{:S(2)}) async-start(), calls=%async_computation.3 | async-start | bytes 3317760 | tf_op jit(solution)/shard_map/all_gather | solution.py:659
  18.8 7.1 %collective-permute-start.28 = (bf16[72,1152]{1,0:T(8,128)(2,1)S(1)}, bf16[72,1152]{1,0:T(8,128)(2,1)S(1)}, u32[]{:S(2)}, u32[]{:S(2)}) collective-permute-start(bf16[72,1152]{1,0:T(8,128)(2,1)S(1)} %get-tuple-element.109), channel_id=1, source_target_pairs={{0,4},{4,0},{1,5},{5,1},{2,6},{6,2},{3,7},{7,3},{8,12},{12,8},{9,1... | collective-permute-start | bytes 497672 | tf_op jit(solution)/shard_map/ppermute | solution.py:24
  20.5 8.2 %collective-permute-start.29 = (bf16[72,1152]{1,0:T(8,128)(2,1)S(1)}, bf16[72,1152]{1,0:T(8,128)(2,1)S(1)}, u32[]{:S(2)}, u32[]{:S(2)}) collective-permute-start(bf16[72,1152]{1,0:T(8,128)(2,1)S(1)} %get-tuple-element.110), channel_id=1, source_target_pairs={{0,6},{2,4},{4,2},{6,0},{1,7},{3,5},{5,3},{7,1},{8,14},{10,12},{12... | collective-permute-start | bytes 497672 | tf_op jit(solution)/shard_map/ppermute | solution.py:24
  20.7 33.6 %collective-permute-start = (bf16[128,1152]{1,0:T(8,128)(2,1)S(1)}, bf16[128,1152]{1,0:T(8,128)(2,1)S(1)}, u32[]{:S(2)}, u32[]{:S(2)}) collective-permute-start(bf16[128,1152]{1,0:T(8,128)(2,1)S(1)} %pad_maximum_fusion.2), channel_id=1, source_target_pairs={{0,4},{4,0},{1,5},{5,1},{2,6},{6,2},{3,7},{7,3},{8,12},{12,8},{9,1... | collective-permute-start | bytes 884744 | tf_op jit(solution)/shard_map/ppermute | solution.py:24
  29.6 145.9 %reduce-scatter.3.cloned.1.call-start = ((), (), s32[]{:S(2)}) async-start(), calls=%async_computation.4 | async-start | bytes 3317760 | tf_op jit(solution)/shard_map/reduce_scatter | solution.py:696
  53.7 15.3 %collective-permute-start.21 = (bf16[128,1152]{1,0:T(8,128)(2,1)}, bf16[128,1152]{1,0:T(8,128)(2,1)S(1)}, u32[]{:S(2)}, u32[]{:S(2)}) collective-permute-start(bf16[128,1152]{1,0:T(8,128)(2,1)} %shard_map.236), channel_id=1, source_target_pairs={{0,4},{4,0},{1,5},{5,1},{2,6},{6,2},{3,7},{7,3},{8,12},{12,8},{9,1... | collective-permute-start | bytes 884744 | tf_op jit(solution)/shard_map/ppermute | solution.py:24
  54.4 9.3 %collective-permute-start.1 = (bf16[256,1152]{1,0:T(8,128)(2,1)S(1)}, bf16[256,1152]{1,0:T(8,128)(2,1)S(1)}, u32[]{:S(2)}, u32[]{:S(2)}) collective-permute-start(bf16[256,1152]{1,0:T(8,128)(2,1)S(1)} %pad_maximum_fusion.t_near), channel_id=1, source_target_pairs={{0,2},{2,0},{1,3},{3,1},{4,6},{6,4},{5,7},{7,5},{8,10},{10,8},{9,1... | collective-permute-start | bytes 1769480 | tf_op jit(solution)/shard_map/ppermute | solution.py:24
  69.1 17.2 %collective-permute-start.22 = (bf16[256,1152]{1,0:T(8,128)(2,1)S(1)}, bf16[256,1152]{1,0:T(8,128)(2,1)S(1)}, u32[]{:S(2)}, u32[]{:S(2)}) collective-permute-start(bf16[256,1152]{1,0:T(8,128)(2,1)S(1)} %pad_maximum_fusion.1.c_near), channel_id=1, source_target_pairs={{0,2},{2,0},{1,3},{3,1},{4,6},{6,4},{5,7},{7,5},{8,10},{10,8},{9,1... | collective-permute-start | bytes 1769480 | tf_op jit(solution)/shard_map/ppermute | solution.py:24
  73.4 6.9 %collective-permute-start.19 = (bf16[64,1152]{1,0:T(8,128)(2,1)}, bf16[64,1152]{1,0:T(8,128)(2,1)S(1)}, u32[]{:S(2)}, u32[]{:S(2)}) collective-permute-start(bf16[64,1152]{1,0:T(8,128)(2,1)} %get-tuple-element.101), channel_id=1, source_target_pairs={{0,4},{4,0},{1,5},{5,1},{2,6},{6,2},{3,7},{7,3},{8,12},{12,8},{9,1... | collective-permute-start | bytes 442376 | tf_op jit(solution)/shard_map/ppermute | solution.py:24
  74.2 8.1 %collective-permute-start.20 = (bf16[64,1152]{1,0:T(8,128)(2,1)S(1)}, bf16[64,1152]{1,0:T(8,128)(2,1)S(1)}, u32[]{:S(2)}, u32[]{:S(2)}) collective-permute-start(bf16[64,1152]{1,0:T(8,128)(2,1)S(1)} %get-tuple-element.102), channel_id=1, source_target_pairs={{0,5},{1,4},{4,1},{5,0},{2,7},{3,6},{6,3},{7,2},{8,13},{9,12},{12,... | collective-permute-start | bytes 442376 | tf_op jit(solution)/shard_map/ppermute | solution.py:24
  87.1 7.6 %collective-permute-start.25 = (bf16[64,1152]{1,0:T(8,128)(2,1)}, bf16[64,1152]{1,0:T(8,128)(2,1)S(1)}, u32[]{:S(2)}, u32[]{:S(2)}) collective-permute-start(bf16[64,1152]{1,0:T(8,128)(2,1)} %shard_map.237.refs_0_), channel_id=1, source_target_pairs={{0,5},{1,4},{4,1},{5,0},{2,7},{3,6},{6,3},{7,2},{8,13},{9,12},{12,... | collective-permute-start | bytes 442376 | tf_op jit(solution)/shard_map/ppermute | solution.py:24
  88.9 7.3 %collective-permute-start.24 = (bf16[64,1152]{1,0:T(8,128)(2,1)}, bf16[64,1152]{1,0:T(8,128)(2,1)S(1)}, u32[]{:S(2)}, u32[]{:S(2)}) collective-permute-start(bf16[64,1152]{1,0:T(8,128)(2,1)} %shard_map.237.refs_0_), channel_id=1, source_target_pairs={{0,4},{4,0},{1,5},{5,1},{2,6},{6,2},{3,7},{7,3},{8,12},{12,8},{9,1... | collective-permute-start | bytes 442376 | tf_op jit(solution)/shard_map/ppermute | solution.py:24
  124.0 89.9 %reduce-scatter.5.cloned.1.call-start = ((), (), s32[]{:S(2)}) async-start(), calls=%async_computation.5 | async-start | bytes 1843200 | tf_op jit(solution)/shard_map/reduce_scatter | solution.py:719
  128.2 6.7 %collective-permute-start.32 = (bf16[64,1152]{1,0:T(8,128)(2,1)S(1)}, bf16[64,1152]{1,0:T(8,128)(2,1)S(1)}, u32[]{:S(2)}, u32[]{:S(2)}) collective-permute-start(bf16[64,1152]{1,0:T(8,128)(2,1)S(1)} %get-tuple-element.117), channel_id=1, source_target_pairs={{0,4},{4,0},{1,5},{5,1},{2,6},{6,2},{3,7},{7,3},{8,12},{12,8},{9,1... | collective-permute-start | bytes 442376 | tf_op jit(solution)/shard_map/ppermute | solution.py:24
  129.6 7.3 %collective-permute-start.33 = (bf16[64,1152]{1,0:T(8,128)(2,1)S(1)}, bf16[64,1152]{1,0:T(8,128)(2,1)S(1)}, u32[]{:S(2)}, u32[]{:S(2)}) collective-permute-start(bf16[64,1152]{1,0:T(8,128)(2,1)S(1)} %get-tuple-element.118), channel_id=1, source_target_pairs={{0,5},{1,4},{4,1},{5,0},{2,7},{3,6},{6,3},{7,2},{8,13},{9,12},{12,... | collective-permute-start | bytes 442376 | tf_op jit(solution)/shard_map/ppermute | solution.py:24
  137.4 7.8 %collective-permute-start.41 = (bf16[64,1152]{1,0:T(8,128)(2,1)S(1)}, bf16[64,1152]{1,0:T(8,128)(2,1)S(1)}, u32[]{:S(2)}, u32[]{:S(2)}) collective-permute-start(bf16[64,1152]{1,0:T(8,128)(2,1)S(1)} %get-tuple-element.121.refs_1_.refs_0_), channel_id=1, source_target_pairs={{0,5},{1,4},{4,1},{5,0},{2,7},{3,6},{6,3},{7,2},{8,13},{9,12},{12,... | collective-permute-start | bytes 442376 | tf_op jit(solution)/shard_map/ppermute | solution.py:24
  139.8 6.5 %collective-permute-start.40 = (bf16[64,1152]{1,0:T(8,128)(2,1)S(1)}, bf16[64,1152]{1,0:T(8,128)(2,1)S(1)}, u32[]{:S(2)}, u32[]{:S(2)}) collective-permute-start(bf16[64,1152]{1,0:T(8,128)(2,1)S(1)} %get-tuple-element.121.refs_1_.refs_0_), channel_id=1, source_target_pairs={{0,4},{4,0},{1,5},{5,1},{2,6},{6,2},{3,7},{7,3},{8,12},{12,8},{9,1... | collective-permute-start | bytes 442376 | tf_op jit(solution)/shard_map/ppermute | solution.py:24
  148.7 16.1 %collective-permute-start.35 = (bf16[64,1152]{1,0:T(8,128)(2,1)}, bf16[64,1152]{1,0:T(8,128)(2,1)S(1)}, u32[]{:S(2)}, u32[]{:S(2)}) collective-permute-start(bf16[64,1152]{1,0:T(8,128)(2,1)} %get-tuple-element.125), channel_id=1, source_target_pairs={{0,1},{1,0},{2,3},{3,2},{4,5},{5,4},{6,7},{7,6},{8,9},{9,8},{10,11... | collective-permute-start | bytes 442376 | tf_op jit(solution)/shard_map/ppermute | solution.py:24
  150.2 14.6 %collective-permute-start.36 = (bf16[64,1152]{1,0:T(8,128)(2,1)}, bf16[64,1152]{1,0:T(8,128)(2,1)}, u32[]{:S(2)}, u32[]{:S(2)}) collective-permute-start(bf16[64,1152]{1,0:T(8,128)(2,1)} %get-tuple-element.126), channel_id=1, source_target_pairs={{0,4},{4,0},{1,5},{5,1},{2,6},{6,2},{3,7},{7,3},{8,12},{12,8},{9,1... | collective-permute-start | bytes 442376 | tf_op jit(solution)/shard_map/ppermute | solution.py:24
  151.6 13.2 %collective-permute-start.37 = (bf16[64,1152]{1,0:T(8,128)(2,1)}, bf16[64,1152]{1,0:T(8,128)(2,1)}, u32[]{:S(2)}, u32[]{:S(2)}) collective-permute-start(bf16[64,1152]{1,0:T(8,128)(2,1)} %get-tuple-element.127), channel_id=1, source_target_pairs={{0,5},{1,4},{4,1},{5,0},{2,7},{3,6},{6,3},{7,2},{8,13},{9,12},{12,... | collective-permute-start | bytes 442376 | tf_op jit(solution)/shard_map/ppermute | solution.py:24
  176.8 7.1 %collective-permute-start.49 = (bf16[72,1152]{1,0:T(8,128)(2,1)S(1)}, bf16[72,1152]{1,0:T(8,128)(2,1)S(1)}, u32[]{:S(2)}, u32[]{:S(2)}) collective-permute-start(bf16[72,1152]{1,0:T(8,128)(2,1)S(1)} %get-tuple-element.150), channel_id=1, source_target_pairs={{0,4},{4,0},{1,5},{5,1},{2,6},{6,2},{3,7},{7,3},{8,12},{12,8},{9,1... | collective-permute-start | bytes 497672 | tf_op jit(solution)/shard_map/ppermute | solution.py:24
  178.3 8.2 %collective-permute-start.50 = (bf16[72,1152]{1,0:T(8,128)(2,1)S(1)}, bf16[72,1152]{1,0:T(8,128)(2,1)S(1)}, u32[]{:S(2)}, u32[]{:S(2)}) collective-permute-start(bf16[72,1152]{1,0:T(8,128)(2,1)S(1)} %get-tuple-element.151), channel_id=1, source_target_pairs={{0,6},{2,4},{4,2},{6,0},{1,7},{3,5},{5,3},{7,1},{8,14},{10,12},{12... | collective-permute-start | bytes 497672 | tf_op jit(solution)/shard_map/ppermute | solution.py:24
  178.8 9.1 %collective-permute-start.44 = (bf16[64,1152]{1,0:T(8,128)(2,1)S(1)}, bf16[64,1152]{1,0:T(8,128)(2,1)S(1)}, u32[]{:S(2)}, u32[]{:S(2)}) collective-permute-start(bf16[64,1152]{1,0:T(8,128)(2,1)S(1)} %get-tuple-element.141), channel_id=1, source_target_pairs={{0,1},{1,0},{2,3},{3,2},{4,5},{5,4},{6,7},{7,6},{8,9},{9,8},{10,11... | collective-permute-start | bytes 442376 | tf_op jit(solution)/shard_map/ppermute | solution.py:24
  180.3 10.3 %collective-permute-start.45 = (bf16[64,1152]{1,0:T(8,128)(2,1)S(1)}, bf16[64,1152]{1,0:T(8,128)(2,1)S(1)}, u32[]{:S(2)}, u32[]{:S(2)}) collective-permute-start(bf16[64,1152]{1,0:T(8,128)(2,1)S(1)} %get-tuple-element.142), channel_id=1, source_target_pairs={{0,4},{4,0},{1,5},{5,1},{2,6},{6,2},{3,7},{7,3},{8,12},{12,8},{9,1... | collective-permute-start | bytes 442376 | tf_op jit(solution)/shard_map/ppermute | solution.py:24
  181.8 12.4 %collective-permute-start.46 = (bf16[64,1152]{1,0:T(8,128)(2,1)S(1)}, bf16[64,1152]{1,0:T(8,128)(2,1)S(1)}, u32[]{:S(2)}, u32[]{:S(2)}) collective-permute-start(bf16[64,1152]{1,0:T(8,128)(2,1)S(1)} %get-tuple-element.143), channel_id=1, source_target_pairs={{0,5},{1,4},{4,1},{5,0},{2,7},{3,6},{6,3},{7,2},{8,13},{9,12},{12,... | collective-permute-start | bytes 442376 | tf_op jit(solution)/shard_map/ppermute | solution.py:24
  195.8 8.7 %collective-permute-start.38 = (bf16[64,1152]{1,0:T(8,128)(2,1)S(1)}, bf16[64,1152]{1,0:T(8,128)(2,1)S(1)}, u32[]{:S(2)}, u32[]{:S(2)}) collective-permute-start(bf16[64,1152]{1,0:T(8,128)(2,1)S(1)} %copy-done.44), channel_id=1, source_target_pairs={{0,1},{1,0},{2,3},{3,2},{4,5},{5,4},{6,7},{7,6},{8,9},{9,8},{10,11... | collective-permute-start | bytes 442376 | tf_op jit(solution)/shard_map/ppermute | solution.py:24
  200.0 6.9 %collective-permute-start.54 = (f32[12,432]{1,0:T(8,128)S(1)}, f32[12,432]{1,0:T(8,128)S(1)}, u32[]{:S(2)}, u32[]{:S(2)}) collective-permute-start(f32[12,432]{1,0:T(8,128)S(1)} %get-tuple-element.177), channel_id=1, source_target_pairs={{0,24},{8,16},{16,8},{24,0},{1,25},{9,17},{17,9},{25,1},{2,26},{10... | collective-permute-start | bytes 62216 | tf_op jit(solution)/shard_map/ppermute | solution.py:24
  202.1 7.3 %collective-permute-start.53 = (f32[12,432]{1,0:T(8,128)S(1)}, f32[12,432]{1,0:T(8,128)S(1)}, u32[]{:S(2)}, u32[]{:S(2)}) collective-permute-start(f32[12,432]{1,0:T(8,128)S(1)} %get-tuple-element.178), channel_id=1, source_target_pairs={{0,16},{8,24},{16,0},{24,8},{1,17},{9,25},{17,1},{25,9},{2,18},{10... | collective-permute-start | bytes 62216 | tf_op jit(solution)/shard_map/ppermute | solution.py:24
  202.3 7.1 %collective-permute-start.52 = (f32[12,432]{1,0:T(8,128)S(1)}, f32[12,432]{1,0:T(8,128)S(1)}, u32[]{:S(2)}, u32[]{:S(2)}) collective-permute-start(f32[12,432]{1,0:T(8,128)S(1)} %get-tuple-element.179), channel_id=1, source_target_pairs={{0,8},{8,0},{16,24},{24,16},{1,9},{9,1},{17,25},{25,17},{2,10},{10... | collective-permute-start | bytes 62216 | tf_op jit(solution)/shard_map/ppermute | solution.py:24
  205.3 7.3 %collective-permute-start.47 = (bf16[64,1152]{1,0:T(8,128)(2,1)S(1)}, bf16[64,1152]{1,0:T(8,128)(2,1)S(1)}, u32[]{:S(2)}, u32[]{:S(2)}) collective-permute-start(bf16[64,1152]{1,0:T(8,128)(2,1)S(1)} %get-tuple-element.146), channel_id=1, source_target_pairs={{0,1},{1,0},{2,3},{3,2},{4,5},{5,4},{6,7},{7,6},{8,9},{9,8},{10,11... | collective-permute-start | bytes 442376 | tf_op jit(solution)/shard_map/ppermute | solution.py:24
  218.4 6.4 %collective-permute-start.58 = (f32[4,1152]{1,0:T(4,128)S(1)}, f32[4,1152]{1,0:T(4,128)S(1)}, u32[]{:S(2)}, u32[]{:S(2)}) collective-permute-start(f32[4,1152]{1,0:T(4,128)S(1)} %get-tuple-element.181), channel_id=1, source_target_pairs={{0,8},{8,0},{16,24},{24,16},{1,9},{9,1},{17,25},{25,17},{2,10},{10... | collective-permute-start | bytes 55304 | tf_op jit(solution)/shard_map/ppermute | solution.py:24
  (122 other events, 745.0 us)
Sparse Core Ops, SparseCore 0:
  18.4 38.5 all-gather.2
  59.1 54.2 all-gather.4
  124.1 51.3 reduce-scatter.2
  178.3 35.5 reduce-scatter.4

commit v6 on v5

--- a/solution.py
+++ b/solution.py
@@ -149,14 +149,15 @@
     return lax.dot_general(left, right, (((1,), (0,)), ((), ())), preferred_element_type=f32)
 
 
-def call(kernel, outs, args, flops=0):
+def call(kernel, outs, args, *scratch):
     return pl.pallas_call(
         kernel,
         out_shape=[jax.ShapeDtypeStruct(shape, dtype) for shape, dtype in outs],
         in_specs=[pl.BlockSpec(memory_space=pltpu.VMEM)] * len(args),
         out_specs=[pl.BlockSpec(memory_space=pltpu.VMEM)] * len(outs),
+        scratch_shapes=scratch,
         compiler_params=pltpu.CompilerParams(vmem_limit_bytes=VMEM_LIMIT),
-        cost_estimate=pl.CostEstimate(flops=flops, bytes_accessed=0, transcendentals=0),
+        cost_estimate=pl.CostEstimate(flops=0, bytes_accessed=0, transcendentals=0),
     )(*args)
 
 
@@ -540,7 +541,7 @@
     seq = total // GROUP
 
     def kernel(
-        n_near, n_far, w, b, c_near, c_far, gt, grads, keep, send, act_out, bias_out, fc2_out, grad_out, n
+        n_near, n_far, w, b, c_near, c_far, gt, grads, pre_out, act_out, bias_out, fc2_out, grad_out, n
     ):
         n[: total // 2, :] = n_near[...]
         n[total // 2 :, :] = n_far[...]
@@ -565,36 +566,35 @@
         grad_pre = grad_pre.astype(bf16)
         grads[:, units:] = transposed_dot(grad_out[...], act).astype(bf16)
         grads[:, :units] = transposed_dot(n[...], grad_pre).astype(bf16)
-        split_store(keep, send, dot_rows(grad_pre, w[:, :units]))
+        pre_out[...] = grad_pre
         act_out[...] = act
 
     return call(
         kernel,
         [
             ((width, 2 * units), bf16),
-            ((total // 2, width), f32),
-            ((total // 2, width), bf16),
+            ((total, units), bf16),
             ((total, units), bf16),
             ((1, units), f32),
             ((1, width), f32),
-            ((total, width), bf16),
-            ((total, width), bf16),
         ],
         (near, far, weights, bias, cot_near, cot_far, gate),
-    )
-
-
-def feed_forward_out(act, weights):
-    total, units = act.shape
+        pltpu.VMEM((total, width), bf16),
+        pltpu.VMEM((total, width), bf16),
+    )
+
+
+def feed_forward_rows(value, weights, start):
+    total, units = value.shape
     width = weights.shape[0]
 
     def kernel(a, w, keep, send):
-        split_store(keep, send, dot_rows(a[...], w[:, units:]))
+        split_store(keep, send, dot_rows(a[...], w[:, start : start + units]))
 
     return call(
         kernel,
         [((total // 2, width), f32), ((total // 2, width), bf16)],
-        (act, weights),
+        (value, weights),
     )
 
 
@@ -690,10 +690,11 @@
 
     normed_two_half = after(normed_two_half, cot_far)
     near, far = gather_eight(normed_two_half)
-    mlp_grad, keep, send, activated, fc1_bias_part, fc2_bias_part, _, _ = feed_forward(
+    mlp_grad, grad_pre, activated, fc1_bias_part, fc2_bias_part = feed_forward(
         near, far, mlp_full, fc1_bias_here[None], cot_near, cot_far, gate_mlp
     )
     mlp_grad = lax.psum_scatter(mlp_grad, "zz", scatter_dimension=0, tiled=True)
+    keep, send = feed_forward_rows(grad_pre, mlp_full, 0)
     grad_hidden_half, grad_branch_half, mod_sums = second_backward(
         scatter_eight(keep, send), hidden_half, branch_half, grad_out_half, scale_mlp, gate_attn
     )
@@ -703,7 +704,9 @@
         near, far, queries, keys, values, attn_full
     )
 
-    out_keep, out_send = feed_forward_out(after(activated, grad_branch_half), mlp_full)
+    out_keep, out_send = feed_forward_rows(
+        after(activated, grad_branch_half), mlp_full, units
+    )
     block_half, gate_sum = second_branch(
         scatter_eight(out_keep, out_send),
         fc2_bias_full[None],

time: 245 us -> 244 us (level)
  waiting for transfers between devices: 87.2 us -> 83.5 us
    reduce_scatter x1, waiting for transfers between devices: 3.16 us -> 0.01 us  [local(): mlp_grad = lax.psum_scatter(mlp_grad, 'zz', scatter_dimension=0, tiled=True)]
    pallas_call x16 -> x17, Pallas kernels: 26.1 us -> 27.2 us  [call(): pl.pallas_call(kernel, out_shape=[jax.ShapeDtypeStruct(shape, dtype) for...]
  transfers between devices with their start and end apart: 71 -> 71, of which waited for: 37 -> 38; matrix products, arithmetic and copies ran while one was open for 6% -> 7% of each run, Pallas kernels for 9% -> 9%
where the time goes in v6:
time: 244 us; the launch traced here: 243 us
  waiting for transfers between devices  83.5 us (34%)
  starting transfers between devices  61.2 us (25%)
  local copies, waits for them, and re-layouts  38.5 us (16%)
  Pallas kernels  32.2 us (13%)
  between operations  14.7 us (6%)
  other arithmetic  9.11 us (4%)
  matrix products  3.89 us (2%)
    ppermute x67, waiting for transfers between devices, exchange(): return lax.ppermute(value, axis, [(i, i ^ mask) for i in range(size)])  69.2 us
    ppermute x67, starting transfers between devices, exchange(): return lax.ppermute(value, axis, [(i, i ^ mask) for i in range(size)])  60.9 us
    unnamed x168, local copies, waits for them, and re-layouts  31.7 us
    pallas_call x17, Pallas kernels, call(): pl.pallas_call(kernel, out_shape=[jax.ShapeDtypeStruct(shape, dtype) for...  27.2 us
    all_gather x1, waiting for transfers between devices, local(): mlp_full = lax.all_gather(mlp_part, 'zz', axis=0, tiled=True)  14.1 us
    pallas_call x10, Pallas kernels, place_call(): pl.pallas_call(kernel, out_shape=[jax.ShapeDtypeStruct(shape, dtype) for...  5.01 us
  transfers between devices with their start and end apart: 71, of which 38 were waited for; matrix products, arithmetic and copies ran while one was open for 7% of the time, Pallas kernels for 9%

profile of v6, /device:TPU:0, one launch (start us, length us, event | category | flops | bytes accessed | tf_op | source)
XLA Modules:
  0.0 243.1 jit_solution(18055243470324117212)
XLA Ops:
  10.0 2.6 %collective-permute-start.3 = (bf16[72,576]{1,0:T(8,128)(2,1)S(1)}, bf16[72,576]{1,0:T(8,128)(2,1)S(1)}, u32[]{:S(2)}, u32[]{:S(2)}) collective-permute-start(bf16[72,576]{1,0:T(8,128)(2,1)S(1)} %get-tuple-element.94), channel_id=1, source_target_pairs={{0,4},{4,0},{1,5},{5,1},{2,6},{6,2},{3,7},{7,3},{8,12},{12,8},{9,1... | collective-permute-start | bytes 248840 | tf_op jit(solution)/shard_map/ppermute | solution.py:24
  12.6 3.4 %collective-permute-done.3.refs_2_ = bf16[72,576]{1,0:T(8,128)(2,1)S(1)} collective-permute-done((bf16[72,576]{1,0:T(8,128)(2,1)S(1)}, bf16[72,576]{1,0:T(8,128)(2,1)S(1)}, u32[]{:S(2)}, u32[]{:S(2)}) %collective-permute-start.3) | collective-permute-done | bytes 82976 | tf_op jit(solution)/shard_map/ppermute | solution.py:24
  22.3 3.6 %collective-permute-done.28.refs_2_ = bf16[72,1152]{1,0:T(8,128)(2,1)S(1)} collective-permute-done((bf16[72,1152]{1,0:T(8,128)(2,1)S(1)}, bf16[72,1152]{1,0:T(8,128)(2,1)S(1)}, u32[]{:S(2)}, u32[]{:S(2)}) %collective-permute-start.28) | collective-permute-done | bytes 165920 | tf_op jit(solution)/shard_map/ppermute | solution.py:24
  25.9 2.8 %collective-permute-done.29.refs_3_ = bf16[72,1152]{1,0:T(8,128)(2,1)S(1)} collective-permute-done((bf16[72,1152]{1,0:T(8,128)(2,1)S(1)}, bf16[72,1152]{1,0:T(8,128)(2,1)S(1)}, u32[]{:S(2)}, u32[]{:S(2)}) %collective-permute-start.29) | collective-permute-done | bytes 165920 | tf_op jit(solution)/shard_map/ppermute | solution.py:24
  31.0 2.0 collective-permute-start.7
  34.8 2.0 collective-permute-done.6
  37.5 4.1 %collective-permute-start.10 = (bf16[4,1512]{1,0:T(4,128)(2,1)S(1)}, bf16[4,1512]{1,0:T(4,128)(2,1)S(1)}, u32[]{:S(2)}, u32[]{:S(2)}) collective-permute-start(bf16[4,1512]{1,0:T(4,128)(2,1)S(1)} %pad_maximum_fusion.7), channel_id=1, source_target_pairs={{0,24},{8,16},{16,8},{24,0},{1,25},{9,17},{17,9},{25,1},{2,26},{10... | collective-permute-start | bytes 36296 | tf_op jit(solution)/shard_map/ppermute | solution.py:24
  43.5 3.1 %collective-permute-done.9 = bf16[4,1512]{1,0:T(4,128)(2,1)S(1)} collective-permute-done((bf16[4,1512]{1,0:T(4,128)(2,1)S(1)}, bf16[4,1512]{1,0:T(4,128)(2,1)S(1)}, u32[]{:S(2)}, u32[]{:S(2)}) %collective-permute-start.9) | collective-permute-done | bytes 12128 | tf_op jit(solution)/shard_map/ppermute | solution.py:24
  49.3 2.5 %collective-permute-start.13 = (f32[4,432]{1,0:T(4,128)S(1)}, f32[4,432]{1,0:T(4,128)S(1)}, u32[]{:S(2)}, u32[]{:S(2)}) collective-permute-start(f32[4,432]{1,0:T(4,128)S(1)} %get-tuple-element.187), channel_id=1, source_target_pairs={{0,24},{8,16},{16,8},{24,0},{1,25},{9,17},{17,9},{25,1},{2,26},{10... | collective-permute-start | bytes 20744 | tf_op jit(solution)/shard_map/ppermute | solution.py:24
  51.7 2.0 collective-permute-start.11
  58.9 2.1 collective-permute-done.16.refs_3_
  63.7 4.2 %shard_map.233 = (bf16[512,1152]{1,0:T(8,128)(2,1)S(1)}, bf16[512,144]{1,0:T(8,128)(2,1)S(1)}, bf16[512,144]{1,0:T(8,128)(2,1)S(1)}, bf16[512,144]{1,0:T(8,128)(...) custom-call(bf16[256,1152]{1,0:T(8,128)(2,1)S(1)} %pad_maximum_fusion.t_near, ...), custom_call_target="tpu_custom_call" | custom-call | tf_op jit(solution)/shard_map/pallas_call | solution.py:153
  75.4 2.5 %collective-permute-done.18.b = bf16[64,1152]{1,0:T(8,128)(2,1)S(1)} collective-permute-done((bf16[64,1152]{1,0:T(8,128)(2,1)}, bf16[64,1152]{1,0:T(8,128)(2,1)S(1)}, u32[]{:S(2)}, u32[]{:S(2)}) %collective-permute-start.18) | collective-permute-done | bytes 147488 | tf_op jit(solution)/shard_map/ppermute | solution.py:24
  77.9 2.3 collective-permute-done.19.c
  80.3 2.0 collective-permute-done.20.d
  87.1 1.8 collective-permute-start.25
  90.6 4.1 %collective-permute-done.25.refs_3_ = bf16[64,1152]{1,0:T(8,128)(2,1)S(1)} collective-permute-done((bf16[64,1152]{1,0:T(8,128)(2,1)}, bf16[64,1152]{1,0:T(8,128)(2,1)S(1)}, u32[]{:S(2)}, u32[]{:S(2)}) %collective-permute-start.25) | collective-permute-done | bytes 147488 | tf_op jit(solution)/shard_map/ppermute | solution.py:24
  97.4 1.9 collective-permute-done.26.n_far
  99.4 14.1 %all-gather.5.cloned.1.call-done.w = bf16[1152,1152]{1,0:T(8,128)(2,1)} async-done(((bf16[288,1152]{1,0:T(8,128)(2,1)}), bf16[1152,1152]{1,0:T(8,128)(2,1)}) %all-gather.5.cloned.1.call-update) | async-done | bytes 2654224 | tf_op jit(solution)/shard_map/all_gather | solution.py:659
  113.4 7.7 %shard_map.241 = (bf16[1152,1152]{1,0:T(8,128)(2,1)}, bf16[512,576]{1,0:T(8,128)(2,1)S(1)}, bf16[512,576]{1,0:T(8,128)(2,1)S(1)}, f32[1,576]{1,0:T(1,128)S(1)}, f32[1,1152]{1,0:T(1,128)S(1)}) custom-call(bf16[256,1152]{1,0:T(8,128)(2,1)S(1)} %shard_map.238.n_near, bf16[256,1152]{1,0:T(8,128)(2,1)} %collective-permute-done.26.n_far, ...), custom_call_target="tpu_custom_call" | custom-call | tf_op jit(solution)/shard_map/pallas_call | solution.py:153
  127.0 2.0 collective-permute-done.30.b
  132.6 2.4 collective-permute-done.31.b
  135.0 2.3 collective-permute-done.32.c
  137.3 2.0 collective-permute-done.33.d
  140.4 2.4 collective-permute-start.41
  158.1 7.0 %shard_map.250 = (bf16[512,432]{1,0:T(8,128)(2,1)S(1)}, f32[256,1152]{1,0:T(8,128)S(1)}, bf16[256,1152]{1,0:T(8,128)(2,1)S(1)}, f32[2,144]{1,0:T(2,128)S(1)}, bf...) custom-call(bf16[256,1152]{1,0:T(8,128)(2,1)S(1)} %shard_map.249.g_near, ...), custom_call_target="tpu_custom_call" | custom-call | tf_op jit(solution)/shard_map/pallas_call | solution.py:153
  183.6 2.6 %collective-permute-done.50.refs_3_ = bf16[72,1152]{1,0:T(8,128)(2,1)S(1)} collective-permute-done((bf16[72,1152]{1,0:T(8,128)(2,1)S(1)}, bf16[72,1152]{1,0:T(8,128)(2,1)S(1)}, u32[]{:S(2)}, u32[]{:S(2)}) %collective-permute-start.50) | collective-permute-done | bytes 165920 | tf_op jit(solution)/shard_map/ppermute | solution.py:24
  187.6 2.7 %collective-permute-done.45.c = bf16[64,1152]{1,0:T(8,128)(2,1)S(1)} collective-permute-done((bf16[64,1152]{1,0:T(8,128)(2,1)S(1)}, bf16[64,1152]{1,0:T(8,128)(2,1)S(1)}, u32[]{:S(2)}, u32[]{:S(2)}) %collective-permute-start.45) | collective-permute-done | bytes 147488 | tf_op jit(solution)/shard_map/ppermute | solution.py:24
  190.4 3.6 %collective-permute-done.46.d = bf16[64,1152]{1,0:T(8,128)(2,1)S(1)} collective-permute-done((bf16[64,1152]{1,0:T(8,128)(2,1)S(1)}, bf16[64,1152]{1,0:T(8,128)(2,1)S(1)}, u32[]{:S(2)}, u32[]{:S(2)}) %collective-permute-start.46) | collective-permute-done | bytes 147488 | tf_op jit(solution)/shard_map/ppermute | solution.py:24
  197.0 2.6 %collective-permute-done.51.b = f32[6,1152]{1,0:T(8,128)S(1)} collective-permute-done((f32[6,1152]{1,0:T(8,128)}, f32[6,1152]{1,0:T(8,128)S(1)}, u32[]{:S(2)}, u32[]{:S(2)}) %collective-permute-start.51) | collective-permute-done | bytes 27680 | tf_op jit(solution)/shard_map/ppermute | solution.py:24
  201.2 3.1 %collective-permute-start.52 = (f32[12,432]{1,0:T(8,128)S(1)}, f32[12,432]{1,0:T(8,128)S(1)}, u32[]{:S(2)}, u32[]{:S(2)}) collective-permute-start(f32[12,432]{1,0:T(8,128)S(1)} %get-tuple-element.181), channel_id=1, source_target_pairs={{0,8},{8,0},{16,24},{24,16},{1,9},{9,1},{17,25},{25,17},{2,10},{10... | collective-permute-start | bytes 62216 | tf_op jit(solution)/shard_map/ppermute | solution.py:24
  232.6 2.5 %fusion.1 = f32[1152,432]{0,1:T(8,128)} fusion(bf16[16,432]{1,0:T(8,128)(2,1)} %shard_map.267, bf16[16,1512]{1,0:T(8,128)(2,1)S(1)} %copy-done.68), kind=kOutput, calls=%fused_computation.16 | convolution fusion | flops 15925248 | bytes 2041344 | tf_op jit(solution)/shard_map/ld,lc->dc/dot_general | solution.py:19
  (378 shorter events, 122.5 us)
Async XLA Ops:
  7.2 49.8 %all-gather.3.cloned.1.call-start = ((), (), s32[]{:S(2)}) async-start(), calls=%async_computation.2 | async-start | bytes 1843200 | tf_op jit(solution)/shard_map/all_gather | solution.py:630
  18.3 95.1 %all-gather.5.cloned.1.call-start = ((), (), s32[]{:S(2)}) async-start(), calls=%async_computation.3 | async-start | bytes 3317760 | tf_op jit(solution)/shard_map/all_gather | solution.py:659
  18.8 7.1 %collective-permute-start.28 = (bf16[72,1152]{1,0:T(8,128)(2,1)S(1)}, bf16[72,1152]{1,0:T(8,128)(2,1)S(1)}, u32[]{:S(2)}, u32[]{:S(2)}) collective-permute-start(bf16[72,1152]{1,0:T(8,128)(2,1)S(1)} %get-tuple-element.110), channel_id=1, source_target_pairs={{0,4},{4,0},{1,5},{5,1},{2,6},{6,2},{3,7},{7,3},{8,12},{12,8},{9,1... | collective-permute-start | bytes 497672 | tf_op jit(solution)/shard_map/ppermute | solution.py:24
  20.5 8.2 %collective-permute-start.29 = (bf16[72,1152]{1,0:T(8,128)(2,1)S(1)}, bf16[72,1152]{1,0:T(8,128)(2,1)S(1)}, u32[]{:S(2)}, u32[]{:S(2)}) collective-permute-start(bf16[72,1152]{1,0:T(8,128)(2,1)S(1)} %get-tuple-element.111), channel_id=1, source_target_pairs={{0,6},{2,4},{4,2},{6,0},{1,7},{3,5},{5,3},{7,1},{8,14},{10,12},{12... | collective-permute-start | bytes 497672 | tf_op jit(solution)/shard_map/ppermute | solution.py:24
  20.7 33.6 %collective-permute-start = (bf16[128,1152]{1,0:T(8,128)(2,1)S(1)}, bf16[128,1152]{1,0:T(8,128)(2,1)S(1)}, u32[]{:S(2)}, u32[]{:S(2)}) collective-permute-start(bf16[128,1152]{1,0:T(8,128)(2,1)S(1)} %pad_maximum_fusion.2), channel_id=1, source_target_pairs={{0,4},{4,0},{1,5},{5,1},{2,6},{6,2},{3,7},{7,3},{8,12},{12,8},{9,1... | collective-permute-start | bytes 884744 | tf_op jit(solution)/shard_map/ppermute | solution.py:24
  29.6 145.7 %reduce-scatter.3.cloned.1.call-start = ((), (), s32[]{:S(2)}) async-start(), calls=%async_computation.4 | async-start | bytes 3317760 | tf_op jit(solution)/shard_map/reduce_scatter | solution.py:696
  53.7 15.3 %collective-permute-start.21 = (bf16[128,1152]{1,0:T(8,128)(2,1)}, bf16[128,1152]{1,0:T(8,128)(2,1)S(1)}, u32[]{:S(2)}, u32[]{:S(2)}) collective-permute-start(bf16[128,1152]{1,0:T(8,128)(2,1)} %shard_map.236), channel_id=1, source_target_pairs={{0,4},{4,0},{1,5},{5,1},{2,6},{6,2},{3,7},{7,3},{8,12},{12,8},{9,1... | collective-permute-start | bytes 884744 | tf_op jit(solution)/shard_map/ppermute | solution.py:24
  54.4 9.3 %collective-permute-start.1 = (bf16[256,1152]{1,0:T(8,128)(2,1)S(1)}, bf16[256,1152]{1,0:T(8,128)(2,1)S(1)}, u32[]{:S(2)}, u32[]{:S(2)}) collective-permute-start(bf16[256,1152]{1,0:T(8,128)(2,1)S(1)} %pad_maximum_fusion.t_near), channel_id=1, source_target_pairs={{0,2},{2,0},{1,3},{3,1},{4,6},{6,4},{5,7},{7,5},{8,10},{10,8},{9,1... | collective-permute-start | bytes 1769480 | tf_op jit(solution)/shard_map/ppermute | solution.py:24
  69.1 17.2 %collective-permute-start.22 = (bf16[256,1152]{1,0:T(8,128)(2,1)S(1)}, bf16[256,1152]{1,0:T(8,128)(2,1)S(1)}, u32[]{:S(2)}, u32[]{:S(2)}) collective-permute-start(bf16[256,1152]{1,0:T(8,128)(2,1)S(1)} %pad_maximum_fusion.1.c_near), channel_id=1, source_target_pairs={{0,2},{2,0},{1,3},{3,1},{4,6},{6,4},{5,7},{7,5},{8,10},{10,8},{9,1... | collective-permute-start | bytes 1769480 | tf_op jit(solution)/shard_map/ppermute | solution.py:24
  73.3 6.9 %collective-permute-start.19 = (bf16[64,1152]{1,0:T(8,128)(2,1)}, bf16[64,1152]{1,0:T(8,128)(2,1)S(1)}, u32[]{:S(2)}, u32[]{:S(2)}) collective-permute-start(bf16[64,1152]{1,0:T(8,128)(2,1)} %get-tuple-element.102), channel_id=1, source_target_pairs={{0,4},{4,0},{1,5},{5,1},{2,6},{6,2},{3,7},{7,3},{8,12},{12,8},{9,1... | collective-permute-start | bytes 442376 | tf_op jit(solution)/shard_map/ppermute | solution.py:24
  74.2 8.1 %collective-permute-start.20 = (bf16[64,1152]{1,0:T(8,128)(2,1)S(1)}, bf16[64,1152]{1,0:T(8,128)(2,1)S(1)}, u32[]{:S(2)}, u32[]{:S(2)}) collective-permute-start(bf16[64,1152]{1,0:T(8,128)(2,1)S(1)} %get-tuple-element.103), channel_id=1, source_target_pairs={{0,5},{1,4},{4,1},{5,0},{2,7},{3,6},{6,3},{7,2},{8,13},{9,12},{12,... | collective-permute-start | bytes 442376 | tf_op jit(solution)/shard_map/ppermute | solution.py:24
  87.1 7.6 %collective-permute-start.25 = (bf16[64,1152]{1,0:T(8,128)(2,1)}, bf16[64,1152]{1,0:T(8,128)(2,1)S(1)}, u32[]{:S(2)}, u32[]{:S(2)}) collective-permute-start(bf16[64,1152]{1,0:T(8,128)(2,1)} %shard_map.237.refs_0_), channel_id=1, source_target_pairs={{0,5},{1,4},{4,1},{5,0},{2,7},{3,6},{6,3},{7,2},{8,13},{9,12},{12,... | collective-permute-start | bytes 442376 | tf_op jit(solution)/shard_map/ppermute | solution.py:24
  88.9 7.3 %collective-permute-start.24 = (bf16[64,1152]{1,0:T(8,128)(2,1)}, bf16[64,1152]{1,0:T(8,128)(2,1)S(1)}, u32[]{:S(2)}, u32[]{:S(2)}) collective-permute-start(bf16[64,1152]{1,0:T(8,128)(2,1)} %shard_map.237.refs_0_), channel_id=1, source_target_pairs={{0,4},{4,0},{1,5},{5,1},{2,6},{6,2},{3,7},{7,3},{8,12},{12,8},{9,1... | collective-permute-start | bytes 442376 | tf_op jit(solution)/shard_map/ppermute | solution.py:24
  122.8 89.9 %reduce-scatter.5.cloned.1.call-start = ((), (), s32[]{:S(2)}) async-start(), calls=%async_computation.5 | async-start | bytes 1843200 | tf_op jit(solution)/shard_map/reduce_scatter | solution.py:722
  130.6 6.7 %collective-permute-start.32 = (bf16[64,1152]{1,0:T(8,128)(2,1)S(1)}, bf16[64,1152]{1,0:T(8,128)(2,1)S(1)}, u32[]{:S(2)}, u32[]{:S(2)}) collective-permute-start(bf16[64,1152]{1,0:T(8,128)(2,1)S(1)} %get-tuple-element.119), channel_id=1, source_target_pairs={{0,4},{4,0},{1,5},{5,1},{2,6},{6,2},{3,7},{7,3},{8,12},{12,8},{9,1... | collective-permute-start | bytes 442376 | tf_op jit(solution)/shard_map/ppermute | solution.py:24
  132.1 7.3 %collective-permute-start.33 = (bf16[64,1152]{1,0:T(8,128)(2,1)S(1)}, bf16[64,1152]{1,0:T(8,128)(2,1)S(1)}, u32[]{:S(2)}, u32[]{:S(2)}) collective-permute-start(bf16[64,1152]{1,0:T(8,128)(2,1)S(1)} %get-tuple-element.120), channel_id=1, source_target_pairs={{0,5},{1,4},{4,1},{5,0},{2,7},{3,6},{6,3},{7,2},{8,13},{9,12},{12,... | collective-permute-start | bytes 442376 | tf_op jit(solution)/shard_map/ppermute | solution.py:24
  140.4 7.7 %collective-permute-start.41 = (bf16[64,1152]{1,0:T(8,128)(2,1)S(1)}, bf16[64,1152]{1,0:T(8,128)(2,1)S(1)}, u32[]{:S(2)}, u32[]{:S(2)}) collective-permute-start(bf16[64,1152]{1,0:T(8,128)(2,1)S(1)} %get-tuple-element.123.refs_1_.refs_0_), channel_id=1, source_target_pairs={{0,5},{1,4},{4,1},{5,0},{2,7},{3,6},{6,3},{7,2},{8,13},{9,12},{12,... | collective-permute-start | bytes 442376 | tf_op jit(solution)/shard_map/ppermute | solution.py:24
  151.6 16.1 %collective-permute-start.35 = (bf16[64,1152]{1,0:T(8,128)(2,1)}, bf16[64,1152]{1,0:T(8,128)(2,1)S(1)}, u32[]{:S(2)}, u32[]{:S(2)}) collective-permute-start(bf16[64,1152]{1,0:T(8,128)(2,1)} %get-tuple-element.127), channel_id=1, source_target_pairs={{0,1},{1,0},{2,3},{3,2},{4,5},{5,4},{6,7},{7,6},{8,9},{9,8},{10,11... | collective-permute-start | bytes 442376 | tf_op jit(solution)/shard_map/ppermute | solution.py:24
  153.1 14.7 %collective-permute-start.36 = (bf16[64,1152]{1,0:T(8,128)(2,1)}, bf16[64,1152]{1,0:T(8,128)(2,1)}, u32[]{:S(2)}, u32[]{:S(2)}) collective-permute-start(bf16[64,1152]{1,0:T(8,128)(2,1)} %get-tuple-element.128), channel_id=1, source_target_pairs={{0,4},{4,0},{1,5},{5,1},{2,6},{6,2},{3,7},{7,3},{8,12},{12,8},{9,1... | collective-permute-start | bytes 442376 | tf_op jit(solution)/shard_map/ppermute | solution.py:24
  154.6 13.2 %collective-permute-start.37 = (bf16[64,1152]{1,0:T(8,128)(2,1)}, bf16[64,1152]{1,0:T(8,128)(2,1)}, u32[]{:S(2)}, u32[]{:S(2)}) collective-permute-start(bf16[64,1152]{1,0:T(8,128)(2,1)} %get-tuple-element.129), channel_id=1, source_target_pairs={{0,5},{1,4},{4,1},{5,0},{2,7},{3,6},{6,3},{7,2},{8,13},{9,12},{12,... | collective-permute-start | bytes 442376 | tf_op jit(solution)/shard_map/ppermute | solution.py:24
  176.5 7.1 %collective-permute-start.49 = (bf16[72,1152]{1,0:T(8,128)(2,1)S(1)}, bf16[72,1152]{1,0:T(8,128)(2,1)S(1)}, u32[]{:S(2)}, u32[]{:S(2)}) collective-permute-start(bf16[72,1152]{1,0:T(8,128)(2,1)S(1)} %get-tuple-element.152), channel_id=1, source_target_pairs={{0,4},{4,0},{1,5},{5,1},{2,6},{6,2},{3,7},{7,3},{8,12},{12,8},{9,1... | collective-permute-start | bytes 497672 | tf_op jit(solution)/shard_map/ppermute | solution.py:24
  178.1 8.2 %collective-permute-start.50 = (bf16[72,1152]{1,0:T(8,128)(2,1)S(1)}, bf16[72,1152]{1,0:T(8,128)(2,1)S(1)}, u32[]{:S(2)}, u32[]{:S(2)}) collective-permute-start(bf16[72,1152]{1,0:T(8,128)(2,1)S(1)} %get-tuple-element.153), channel_id=1, source_target_pairs={{0,6},{2,4},{4,2},{6,0},{1,7},{3,5},{5,3},{7,1},{8,14},{10,12},{12... | collective-permute-start | bytes 497672 | tf_op jit(solution)/shard_map/ppermute | solution.py:24
  178.5 9.1 %collective-permute-start.44 = (bf16[64,1152]{1,0:T(8,128)(2,1)S(1)}, bf16[64,1152]{1,0:T(8,128)(2,1)S(1)}, u32[]{:S(2)}, u32[]{:S(2)}) collective-permute-start(bf16[64,1152]{1,0:T(8,128)(2,1)S(1)} %get-tuple-element.143), channel_id=1, source_target_pairs={{0,1},{1,0},{2,3},{3,2},{4,5},{5,4},{6,7},{7,6},{8,9},{9,8},{10,11... | collective-permute-start | bytes 442376 | tf_op jit(solution)/shard_map/ppermute | solution.py:24
  180.1 10.3 %collective-permute-start.45 = (bf16[64,1152]{1,0:T(8,128)(2,1)S(1)}, bf16[64,1152]{1,0:T(8,128)(2,1)S(1)}, u32[]{:S(2)}, u32[]{:S(2)}) collective-permute-start(bf16[64,1152]{1,0:T(8,128)(2,1)S(1)} %get-tuple-element.144), channel_id=1, source_target_pairs={{0,4},{4,0},{1,5},{5,1},{2,6},{6,2},{3,7},{7,3},{8,12},{12,8},{9,1... | collective-permute-start | bytes 442376 | tf_op jit(solution)/shard_map/ppermute | solution.py:24
  181.5 12.4 %collective-permute-start.46 = (bf16[64,1152]{1,0:T(8,128)(2,1)S(1)}, bf16[64,1152]{1,0:T(8,128)(2,1)S(1)}, u32[]{:S(2)}, u32[]{:S(2)}) collective-permute-start(bf16[64,1152]{1,0:T(8,128)(2,1)S(1)} %get-tuple-element.145), channel_id=1, source_target_pairs={{0,5},{1,4},{4,1},{5,0},{2,7},{3,6},{6,3},{7,2},{8,13},{9,12},{12,... | collective-permute-start | bytes 442376 | tf_op jit(solution)/shard_map/ppermute | solution.py:24
  195.6 8.7 %collective-permute-start.38 = (bf16[64,1152]{1,0:T(8,128)(2,1)S(1)}, bf16[64,1152]{1,0:T(8,128)(2,1)S(1)}, u32[]{:S(2)}, u32[]{:S(2)}) collective-permute-start(bf16[64,1152]{1,0:T(8,128)(2,1)S(1)} %copy-done.45), channel_id=1, source_target_pairs={{0,1},{1,0},{2,3},{3,2},{4,5},{5,4},{6,7},{7,6},{8,9},{9,8},{10,11... | collective-permute-start | bytes 442376 | tf_op jit(solution)/shard_map/ppermute | solution.py:24
  199.8 6.9 %collective-permute-start.54 = (f32[12,432]{1,0:T(8,128)S(1)}, f32[12,432]{1,0:T(8,128)S(1)}, u32[]{:S(2)}, u32[]{:S(2)}) collective-permute-start(f32[12,432]{1,0:T(8,128)S(1)} %get-tuple-element.179), channel_id=1, source_target_pairs={{0,24},{8,16},{16,8},{24,0},{1,25},{9,17},{17,9},{25,1},{2,26},{10... | collective-permute-start | bytes 62216 | tf_op jit(solution)/shard_map/ppermute | solution.py:24
  200.9 7.5 %collective-permute-start.53 = (f32[12,432]{1,0:T(8,128)S(1)}, f32[12,432]{1,0:T(8,128)S(1)}, u32[]{:S(2)}, u32[]{:S(2)}) collective-permute-start(f32[12,432]{1,0:T(8,128)S(1)} %get-tuple-element.180), channel_id=1, source_target_pairs={{0,16},{8,24},{16,0},{24,8},{1,17},{9,25},{17,1},{25,9},{2,18},{10... | collective-permute-start | bytes 62216 | tf_op jit(solution)/shard_map/ppermute | solution.py:24
  201.2 7.3 %collective-permute-start.52 = (f32[12,432]{1,0:T(8,128)S(1)}, f32[12,432]{1,0:T(8,128)S(1)}, u32[]{:S(2)}, u32[]{:S(2)}) collective-permute-start(f32[12,432]{1,0:T(8,128)S(1)} %get-tuple-element.181), channel_id=1, source_target_pairs={{0,8},{8,0},{16,24},{24,16},{1,9},{9,1},{17,25},{25,17},{2,10},{10... | collective-permute-start | bytes 62216 | tf_op jit(solution)/shard_map/ppermute | solution.py:24
  205.0 6.6 %collective-permute-start.47 = (bf16[64,1152]{1,0:T(8,128)(2,1)S(1)}, bf16[64,1152]{1,0:T(8,128)(2,1)S(1)}, u32[]{:S(2)}, u32[]{:S(2)}) collective-permute-start(bf16[64,1152]{1,0:T(8,128)(2,1)S(1)} %get-tuple-element.148), channel_id=1, source_target_pairs={{0,1},{1,0},{2,3},{3,2},{4,5},{5,4},{6,7},{7,6},{8,9},{9,8},{10,11... | collective-permute-start | bytes 442376 | tf_op jit(solution)/shard_map/ppermute | solution.py:24
  215.9 11.1 %collective-permute-start.61 = (bf16[72,576]{1,0:T(8,128)(2,1)S(1)}, bf16[72,576]{1,0:T(8,128)(2,1)S(1)}, u32[]{:S(2)}, u32[]{:S(2)}) collective-permute-start(bf16[72,576]{1,0:T(8,128)(2,1)S(1)} %get-tuple-element.164), channel_id=1, source_target_pairs={{0,2},{2,0},{1,3},{3,1},{4,6},{6,4},{5,7},{7,5},{8,10},{10,8},{9,1... | collective-permute-start | bytes 248840 | tf_op jit(solution)/shard_map/ppermute | solution.py:24
  216.2 10.8 %collective-permute-start.62 = (bf16[72,576]{1,0:T(8,128)(2,1)S(1)}, bf16[72,576]{1,0:T(8,128)(2,1)S(1)}, u32[]{:S(2)}, u32[]{:S(2)}) collective-permute-start(bf16[72,576]{1,0:T(8,128)(2,1)S(1)} %get-tuple-element.165), channel_id=1, source_target_pairs={{0,4},{4,0},{1,5},{5,1},{2,6},{6,2},{3,7},{7,3},{8,12},{12,8},{9,1... | collective-permute-start | bytes 248840 | tf_op jit(solution)/shard_map/ppermute | solution.py:24
  (122 other events, 734.4 us)
Sparse Core Ops, SparseCore 0:
  18.4 38.5 all-gather.2
  59.1 54.2 all-gather.4
  122.9 51.3 reduce-scatter.2
  177.1 35.5 reduce-scatter.4
